TPU v7x, 32 devices: a whole 2x2x4 slice. The times are simulated.
32 devices in a mesh: ens: 2 (over x), gx: 16 (over z, y, core).
Axes of the slice: x: 2, y: 2, z: 4, core: 2. Of those that a mesh axis runs over, the one named last changes fastest.
Arguments:
- fraction: float32 [128, 128, 256], P(('ens', 'gx')), parts along dimension 0, may hold values from 0 to 1
- first_velocity: float32 [128, 128, 256], P(('ens', 'gx')), parts along dimension 0, may hold values from -12 to 12
- second_velocity: float32 [128, 128, 256], P(('ens', 'gx')), parts along dimension 0, may hold values from -12 to 12
- third_velocity: float32 [128, 128, 256], P(('ens', 'gx')), parts along dimension 0, may hold values from -12 to 12
- wall_class: int32 [64, 128], replicated, may hold values from 0 to 3
- seed_mask: int32 [128, 128, 256], P(('ens', 'gx')), parts along dimension 0, may hold values 0 or 1
Outputs:
- liquid: float32 [128, 128, 256], P(('ens', 'gx')), parts along dimension 0
There are 2 independent parts, one for each index of `ens`. A program takes and returns all parts, laid end to end along the dimension named above; an argument that names none is the same for every part. Nothing has to cross between parts.
All inputs are finite; a program needn't handle non-finite values. Where the computation divides by a largest or mean magnitude, that divisor is 1e-20 or more. No bound on the sum of `seed_mask` on one device may be relied on, other than what follows from the above.
Results may differ from a plain program's by a relative error of at most 0.0003.
Values sent between devices are 32-bit elements; how exact they have to be, the bound alone decides.
No kernel may reach another device: no remote copies, remote signals or barrier semaphores. Data moves between devices by JAX's collectives and lax.ppermute only.
A program may use at most 64 MiB of HBM per device.

v0:
```python
import jax
import jax.numpy as jnp
from jax import lax
from jax.sharding import PartitionSpec as P

STEPS = 2
NEWTON = 4
WALL_CLASSES = 4


CFL_NUMBER = 0.45
NEWTON_DAMPING = 0.5


def padded_2(array, sides, width):
    for axis, dim in sides:
        count, length = (lax.axis_size(axis), array.shape[dim])
        up = [(i, (i + 1) % count) for i in range(count)]
        down = [(j, i) for i, j in up]
        last = lax.slice_in_dim(array, length - width, length, axis=dim)
        first = lax.slice_in_dim(array, 0, width, axis=dim)
        before = lax.ppermute(last, axis, up)
        after = lax.ppermute(first, axis, down)
        array = jnp.concatenate([before, array, after], axis=dim)
    return array


def from_behind(array, axis, by):
    count = lax.axis_size(axis)
    return lax.ppermute(array, axis, [(i, (i + by) % count) for i in range(count)])


def cube_part(values):
    positive = jnp.maximum(values, 0.0)
    return positive * positive * positive


def square_part(values):
    positive = jnp.maximum(values, 0.0)
    return positive * positive


def corner_terms(plane_at, slope_a, slope_b, slope_c, power_map):
    paired = slope_b + slope_c
    summed = (
        power_map(plane_at)
        - power_map(plane_at - slope_b)
        - power_map(plane_at - slope_c)
        + power_map(plane_at - paired)
    )
    shifted = plane_at - slope_a
    summed = (
        summed
        - power_map(shifted)
        + power_map(shifted - slope_b)
        + power_map(shifted - slope_c)
        - power_map(shifted - paired)
    )
    return summed


def plane_level(target, slope_a, slope_b, slope_c, inverse):
    plane_at = jnp.full_like(target, 0.5)
    for newton_turn in range(NEWTON):
        volume = corner_terms(plane_at, slope_a, slope_b, slope_c, cube_part) * inverse
        growth = corner_terms(plane_at, slope_a, slope_b, slope_c, square_part) * (3.0 * inverse)
        plane_at = plane_at - NEWTON_DAMPING * (volume - target) / growth
    return plane_at


def flux_volume(donor, normal_along, normal_other, normal_third, velocity, step_size):
    courant = jnp.abs(velocity) * step_size
    heading = jnp.where(velocity > 0.0, 1.0, -1.0)
    weight_sum = jnp.abs(normal_along) + jnp.abs(normal_other) + jnp.abs(normal_third) + 0.3
    slope_along = (jnp.abs(normal_along) + 0.1) / weight_sum
    slope_other = (jnp.abs(normal_other) + 0.1) / weight_sum
    slope_third = (jnp.abs(normal_third) + 0.1) / weight_sum
    inverse = 1.0 / (6.0 * slope_along * slope_other * slope_third)
    lighter = donor <= 0.5
    target = jnp.clip(jnp.minimum(donor, 1.0 - donor), 0.0, 0.5)
    plane_at = plane_level(target, slope_along, slope_other, slope_third, inverse)

    def box_volume(slab_span):
        return (
            corner_terms(plane_at, slab_span * slope_along, slope_other, slope_third, cube_part)
            * inverse
        )

    high_side = box_volume(1.0) - box_volume(1.0 - courant)
    low_side = box_volume(courant)
    facing = jnp.where(lighter, normal_along, -normal_along)
    weight = jnp.clip(0.5 + 2.0 * facing * heading / weight_sum, 0.0, 1.0)
    phase_part = weight * high_side + (1.0 - weight) * low_side
    phase_moved = jnp.where(lighter, phase_part, courant - phase_part)
    return heading * phase_moved


def normal_field(padded, wall_cosine):
    centre_cells = padded[1:-1]
    normal_x = 0.5 * (padded[:-2] - padded[2:])
    normal_y = 0.5 * (jnp.roll(centre_cells, 1, 1) - jnp.roll(centre_cells, -1, 1))
    from_below = jnp.concatenate([centre_cells[:, :, :1], centre_cells[:, :, :-1]], 2)
    from_above = jnp.concatenate([centre_cells[:, :, 1:], centre_cells[:, :, -1:]], 2)
    normal_z = 0.5 * (from_below - from_above)
    bottom_layer = jnp.arange(centre_cells.shape[2]) == 0
    contact = wall_cosine[:, :, None] * (jnp.abs(normal_x) + jnp.abs(normal_y))
    normal_z = jnp.where(bottom_layer[None, None, :], contact, normal_z)
    return (centre_cells, normal_x, normal_y, normal_z)


def advect_first_axis(padded, face_speed, wall_cosine, step_size):
    centre_cells, normal_x, normal_y, normal_z = normal_field(padded, wall_cosine)
    forward = face_speed > 0.0

    def choose_donor(values):
        return jnp.where(forward, values[:-1], values[1:])

    moved_volume = flux_volume(
        choose_donor(centre_cells),
        choose_donor(normal_x),
        choose_donor(normal_y),
        choose_donor(normal_z),
        face_speed,
        step_size,
    )
    return jnp.clip(centre_cells[1:-1] - moved_volume[1:] + moved_volume[:-1], 0.0, 1.0)


def advect_second_axis(padded, face_speed, wall_cosine, step_size):
    centre_cells, normal_x, normal_y, normal_z = normal_field(padded, wall_cosine)
    forward = face_speed > 0.0

    def choose_donor(values):
        return jnp.where(forward, values, jnp.roll(values, -1, 1))

    moved_volume = flux_volume(
        choose_donor(centre_cells),
        choose_donor(normal_y),
        choose_donor(normal_x),
        choose_donor(normal_z),
        face_speed,
        step_size,
    )
    return jnp.clip(centre_cells - moved_volume + jnp.roll(moved_volume, 1, 1), 0.0, 1.0)


def advect_third_axis(padded, face_speed, wall_cosine, step_size):
    centre_cells, normal_x, normal_y, normal_z = normal_field(padded, wall_cosine)
    top_face = jnp.arange(centre_cells.shape[2]) == centre_cells.shape[2] - 1
    face_speed = jnp.where(top_face[None, None, :], 0.0, face_speed)
    forward = face_speed > 0.0

    def choose_donor(values):
        return jnp.where(forward, values, jnp.concatenate([values[:, :, 1:], values[:, :, -1:]], 2))

    moved_volume = flux_volume(
        choose_donor(centre_cells),
        choose_donor(normal_z),
        choose_donor(normal_x),
        choose_donor(normal_y),
        face_speed,
        step_size,
    )
    inflow = jnp.concatenate([jnp.zeros_like(moved_volume[:, :, :1]), moved_volume[:, :, :-1]], 2)
    return jnp.clip(centre_cells - moved_volume + inflow, 0.0, 1.0)


def plane_margin(liquid):
    return padded_2(liquid, (("gx", 0),), 1)


def shards(fraction, first_velocity, second_velocity, third_velocity, wall_class, seed_mask):
    slab_cells = fraction.shape[0]
    wall_cosines = jnp.cos(jnp.pi * (wall_class.astype(jnp.float32) + 1.0) / (WALL_CLASSES + 1))
    slab_start = lax.axis_index("gx") * slab_cells
    wall_cosine = jnp.roll(wall_cosines, 4 - slab_start, 0)[: slab_cells + 8]
    liquid = jnp.where(seed_mask == 1, jnp.ones_like(fraction), fraction)
    local_peak = jnp.maximum(
        jnp.maximum(jnp.max(jnp.abs(first_velocity)), jnp.max(jnp.abs(second_velocity))),
        jnp.max(jnp.abs(third_velocity)),
    )
    speed_peak = lax.pmax(local_peak, "gx")
    step_size = CFL_NUMBER / (speed_peak + 1e-06)
    lower_face = from_behind(first_velocity[-1:], "gx", 1)
    first_faces = jnp.concatenate([lower_face, first_velocity], 0)
    for step_turn in range(STEPS):
        padded = padded_2(liquid, (("gx", 0),), 2)
        liquid = advect_first_axis(padded, first_faces, wall_cosine[3 : slab_cells + 5], step_size)
        liquid = advect_second_axis(
            plane_margin(liquid), second_velocity, wall_cosine[4 : slab_cells + 4], step_size
        )
        liquid = advect_third_axis(
            plane_margin(liquid), third_velocity, wall_cosine[4 : slab_cells + 4], step_size
        )
    return liquid


def solution(mesh):
    placed = (
        P(("ens", "gx"), None, None),
        P(("ens", "gx"), None, None),
        P(("ens", "gx"), None, None),
        P(("ens", "gx"), None, None),
        P(),
        P(("ens", "gx"), None, None),
    )
    return jax.shard_map(
        shards, mesh=mesh, in_specs=placed, out_specs=P(("ens", "gx"), None, None), check_vma=False
    )
```

profile of v0, /device:TPU:0, one launch (start us, length us, event | category | flops | bytes accessed | tf_op | source)
XLA Modules:
  0.0 134.8 jit_solution(5158879368044307862)
XLA Ops:
  0.0 0.9 slice.432
  0.9 0.5 collective-permute-start
  1.4 1.3 compare_select_fusion
  2.7 0.7 fusion.574
  3.4 2.6 %collective-permute-start.1 = (f32[2,128,256]{2,1,0:T(8,128)}, f32[2,128,256]{2,1,0:T(8,128)S(1)}, u32[]{:S(2)}, u32[]{:S(2)}) collective-permute-start(f32[2,128,256]{2,1,0:T(8,128)} %get-tuple-element.79), channel_id=1, source_target_pairs={{0,1},{1,2},{2,3},{3,4},{4,5},{5,6},{6,7},{7,8},{8,9},{9,10},{10,1... | collective-permute-start | bytes 786440 | tf_op jit(solution)/shard_map/ppermute | solution.py:22
  6.1 2.4 %collective-permute-start.2 = (f32[2,128,256]{2,1,0:T(8,128)S(1)}, f32[2,128,256]{2,1,0:T(8,128)S(1)}, u32[]{:S(2)}, u32[]{:S(2)}) collective-permute-start(f32[2,128,256]{2,1,0:T(8,128)S(1)} %get-tuple-element.80), channel_id=1, source_target_pairs={{1,0},{2,1},{3,2},{4,3},{5,4},{6,5},{7,6},{8,7},{9,8},{10,9},{11,1... | collective-permute-start | bytes 786440 | tf_op jit(solution)/shard_map/ppermute | solution.py:23
  8.5 0.7 abs_reduce_fusion
  9.5 0.7 abs_reduce_fusion.2
  10.2 0.9 constant_dynamic-update-slice_fusion.1
  11.1 0.7 abs_reduce_fusion.1
  13.7 0.7 slice.565
  14.4 30.7 %pmax.7 = f32[]{:T(128)} all-reduce(f32[]{:T(128)S(6)} %max.1171), channel_id=1, replica_groups=mesh['ens'=2,'gx'=16] {'gx'}, use_global_device_ids=true, to_apply=%region_3.4 | all-reduce | flops 1 | bytes 8 | tf_op jit(solution)/shard_map/pmax | solution.py:182
  46.0 0.3 fusion.551
  46.4 0.6 fusion.13
  47.0 7.5 %select_multiply_fusion.2 = f32[5,128,256]{2,1,0:T(8,128)S(1)} fusion(f32[6,128,256]{2,1,0:T(8,128)S(1)} %get-tuple-element.16, f32[6,128,256]{2,1,0:T(8,128)S(1)} %get-tuple-element.17, f32[6,128,256]{2,1,0:T(8,128)S(1)} %get-tuple-element.18, f32[2,128,256]{2,1,0:T(8,128)S(1)} %collective-permute-done.2, f32[4,128,256]{2,1,0:T(8,128)S(1)} %compare_select_fusion, ...), kind=kLoop, calls=%fused_computation.2 | loop fusion | flops 54394880 | bytes 6291460 | tf_op jit(solution)/shard_map/mul | solution.py:95
  54.9 0.2 fusion.572
  55.2 4.4 %collective-permute-start.4 = (f32[1,128,256]{2,1,0:T(8,128)S(1)}, f32[1,128,256]{2,1,0:T(8,128)S(1)}, u32[]{:S(2)}, u32[]{:S(2)}) collective-permute-start(f32[1,128,256]{2,1,0:T(8,128)S(1)} %get-tuple-element.72), channel_id=1, source_target_pairs={{1,0},{2,1},{3,2},{4,3},{5,4},{6,5},{7,6},{8,7},{9,8},{10,9},{11,1... | collective-permute-start | bytes 393224 | tf_op jit(solution)/shard_map/ppermute | solution.py:23
  59.6 2.6 %collective-permute-done.3 = f32[1,128,256]{2,1,0:T(8,128)S(1)} collective-permute-done((f32[1,128,256]{2,1,0:T(8,128)S(1)}, f32[1,128,256]{2,1,0:T(8,128)S(1)}, u32[]{:S(2)}, u32[]{:S(2)}) %collective-permute-start.3) | collective-permute-done | bytes 131104 | tf_op jit(solution)/shard_map/ppermute | solution.py:22
  62.3 0.4 fusion.511
  62.9 6.6 %select_multiply_fusion.10 = f32[4,128,256]{2,1,0:T(8,128)S(1)} fusion(f32[4,128,256]{2,1,0:T(8,128)S(1)} %get-tuple-element.14, f32[4,1,256]{2,1,0:T(1,128)S(1)} %slice.590, f32[4,127,256]{2,1,0:T(8,128)S(1)} %slice.589, f32[4,1,256]{2,1,0:T(1,128)S(1)} %slice.583, f32[4,127,256]{2,1,0:T(8,128)S(1)} %slice.582, f32[4,128,256]{2,1,0:T(8,128)S(1)} %get-tuple-element.15, ...), kind=kLoop, calls=%fused_computation.12 | loop fusion | flops 44302336 | bytes 4980740 | tf_op jit(solution)/shard_map/mul | solution.py:95
  69.8 0.2 fusion.567
  70.1 4.5 %collective-permute-start.6 = (f32[1,128,256]{2,1,0:T(8,128)S(1)}, f32[1,128,256]{2,1,0:T(8,128)S(1)}, u32[]{:S(2)}, u32[]{:S(2)}) collective-permute-start(f32[1,128,256]{2,1,0:T(8,128)S(1)} %get-tuple-element.62), channel_id=1, source_target_pairs={{1,0},{2,1},{3,2},{4,3},{5,4},{6,5},{7,6},{8,7},{9,8},{10,9},{11,1... | collective-permute-start | bytes 393224 | tf_op jit(solution)/shard_map/ppermute | solution.py:23
  74.6 2.6 %collective-permute-done.5 = f32[1,128,256]{2,1,0:T(8,128)S(1)} collective-permute-done((f32[1,128,256]{2,1,0:T(8,128)S(1)}, f32[1,128,256]{2,1,0:T(8,128)S(1)}, u32[]{:S(2)}, u32[]{:S(2)}) %collective-permute-start.5) | collective-permute-done | bytes 131104 | tf_op jit(solution)/shard_map/ppermute | solution.py:22
  77.2 0.4 fusion.516
  77.8 0.2 slice.605
  78.1 0.2 slice.603
  78.4 0.2 slice.607
  78.7 6.5 %select_multiply_fusion.6 = f32[4,128,256]{2,1,0:T(8,128)S(1)} fusion(f32[4,128,256]{2,1,0:T(8,128)S(1)} %get-tuple-element.13, f32[4,128,1]{2,1,0:T(8,128)S(1)} %slice.608, f32[4,128,255]{2,1,0:T(8,128)S(1)} %slice.607, f32[4,128,1]{2,1,0:T(8,128)S(1)} %slice.606, f32[4,128,255]{2,1,0:T(8,128)S(1)} %slice.605, f32[4,128,256]{2,1,0:T(8,128)S(1)} %get-tuple-element.12, ...), kind=kLoop, calls=%fused_computation.8 | loop fusion | flops 44433408 | bytes 4980996 | tf_op jit(solution)/shard_map/mul | solution.py:95
  85.1 0.3 add_clamp_fusion.1
  85.5 4.7 %collective-permute-start.8 = (f32[2,128,256]{2,1,0:T(8,128)S(1)}, f32[2,128,256]{2,1,0:T(8,128)S(1)}, u32[]{:S(2)}, u32[]{:S(2)}) collective-permute-start(f32[2,128,256]{2,1,0:T(8,128)S(1)} %get-tuple-element.56), channel_id=1, source_target_pairs={{1,0},{2,1},{3,2},{4,3},{5,4},{6,5},{7,6},{8,7},{9,8},{10,9},{11,1... | collective-permute-start | bytes 786440 | tf_op jit(solution)/shard_map/ppermute | solution.py:23
  90.3 3.8 %collective-permute-done.7 = f32[2,128,256]{2,1,0:T(8,128)S(1)} collective-permute-done((f32[2,128,256]{2,1,0:T(8,128)S(1)}, f32[2,128,256]{2,1,0:T(8,128)S(1)}, u32[]{:S(2)}, u32[]{:S(2)}) %collective-permute-start.7) | collective-permute-done | bytes 262176 | tf_op jit(solution)/shard_map/ppermute | solution.py:22
  94.4 0.3 fusion.548
  94.8 0.6 fusion.15
  95.5 7.5 %select_multiply_fusion = f32[5,128,256]{2,1,0:T(8,128)S(1)} fusion(f32[6,128,256]{2,1,0:T(8,128)S(1)} %get-tuple-element.9, f32[6,128,256]{2,1,0:T(8,128)S(1)} %get-tuple-element.10, f32[6,128,256]{2,1,0:T(8,128)S(1)} %get-tuple-element.11, f32[2,128,256]{2,1,0:T(8,128)S(1)} %collective-permute-done.8, f32[4,128,256]{2,1,0:T(8,128)S(1)} %add_clamp_fusion.1, ...), kind=kLoop, calls=%fused_computation | loop fusion | flops 54394880 | bytes 6291460 | tf_op jit(solution)/shard_map/mul | solution.py:95
  103.3 0.2 fusion.561
  103.6 4.7 %collective-permute-start.10 = (f32[1,128,256]{2,1,0:T(8,128)S(1)}, f32[1,128,256]{2,1,0:T(8,128)S(1)}, u32[]{:S(2)}, u32[]{:S(2)}) collective-permute-start(f32[1,128,256]{2,1,0:T(8,128)S(1)} %get-tuple-element.50), channel_id=1, source_target_pairs={{1,0},{2,1},{3,2},{4,3},{5,4},{6,5},{7,6},{8,7},{9,8},{10,9},{11,1... | collective-permute-start | bytes 393224 | tf_op jit(solution)/shard_map/ppermute | solution.py:23
  108.2 2.6 %collective-permute-done.9 = f32[1,128,256]{2,1,0:T(8,128)S(1)} collective-permute-done((f32[1,128,256]{2,1,0:T(8,128)S(1)}, f32[1,128,256]{2,1,0:T(8,128)S(1)}, u32[]{:S(2)}, u32[]{:S(2)}) %collective-permute-start.9) | collective-permute-done | bytes 131104 | tf_op jit(solution)/shard_map/ppermute | solution.py:22
  110.8 0.4 fusion.522
  111.4 6.6 %select_multiply_fusion.8 = f32[4,128,256]{2,1,0:T(8,128)S(1)} fusion(f32[4,128,256]{2,1,0:T(8,128)S(1)} %get-tuple-element.7, f32[4,1,256]{2,1,0:T(1,128)S(1)} %slice.645, f32[4,127,256]{2,1,0:T(8,128)S(1)} %slice.644, f32[4,1,256]{2,1,0:T(1,128)S(1)} %slice.639, f32[4,127,256]{2,1,0:T(8,128)S(1)} %slice.638, f32[4,128,256]{2,1,0:T(8,128)S(1)} %get-tuple-element.8, ...), kind=kLoop, calls=%fused_computation.10 | loop fusion | flops 44302336 | bytes 4980740 | tf_op jit(solution)/shard_map/mul | solution.py:95
  118.4 0.2 fusion.556
  118.7 4.6 %collective-permute-start.12 = (f32[1,128,256]{2,1,0:T(8,128)S(1)}, f32[1,128,256]{2,1,0:T(8,128)S(1)}, u32[]{:S(2)}, u32[]{:S(2)}) collective-permute-start(f32[1,128,256]{2,1,0:T(8,128)S(1)} %get-tuple-element.40), channel_id=1, source_target_pairs={{1,0},{2,1},{3,2},{4,3},{5,4},{6,5},{7,6},{8,7},{9,8},{10,9},{11,1... | collective-permute-start | bytes 393224 | tf_op jit(solution)/shard_map/ppermute | solution.py:23
  123.3 2.6 %collective-permute-done.11 = f32[1,128,256]{2,1,0:T(8,128)S(1)} collective-permute-done((f32[1,128,256]{2,1,0:T(8,128)S(1)}, f32[1,128,256]{2,1,0:T(8,128)S(1)}, u32[]{:S(2)}, u32[]{:S(2)}) %collective-permute-start.11) | collective-permute-done | bytes 131104 | tf_op jit(solution)/shard_map/ppermute | solution.py:22
  125.8 0.4 fusion.527
  126.4 0.2 slice.660
  126.7 0.2 slice.658
  127.1 0.2 slice.662
  127.3 6.5 %select_multiply_fusion.4 = f32[4,128,256]{2,1,0:T(8,128)S(1)} fusion(f32[4,128,256]{2,1,0:T(8,128)S(1)} %get-tuple-element.6, f32[4,128,1]{2,1,0:T(8,128)S(1)} %slice.663, f32[4,128,255]{2,1,0:T(8,128)S(1)} %slice.662, f32[4,128,1]{2,1,0:T(8,128)S(1)} %slice.661, f32[4,128,255]{2,1,0:T(8,128)S(1)} %slice.660, f32[4,128,256]{2,1,0:T(8,128)S(1)} %get-tuple-element.5, ...), kind=kLoop, calls=%fused_computation.6 | loop fusion | flops 44433408 | bytes 4980996 | tf_op jit(solution)/shard_map/mul | solution.py:95
  133.8 1.0 add_clamp_fusion
  (75 shorter events, 3.8 us)
Async XLA Ops:
  0.9 9.2 %collective-permute-start = (f32[1,128,256]{2,1,0:T(8,128)S(1)}, f32[1,128,256]{2,1,0:T(8,128)}, u32[]{:S(2)}, u32[]{:S(2)}) collective-permute-start(f32[1,128,256]{2,1,0:T(8,128)S(1)} %slice.432), channel_id=1, source_target_pairs={{0,1},{1,2},{2,3},{3,4},{4,5},{5,6},{6,7},{7,8},{8,9},{9,10},{10,1... | collective-permute-start | bytes 393224 | tf_op jit(solution)/shard_map/ppermute | solution.py:30
  2.7 5.8 %copy-start.1 = (f32[4,128,256]{2,1,0:T(8,128)S(1)}, f32[4,128,256]{2,1,0:T(8,128)}, u32[]{:S(2)}) copy-start(f32[4,128,256]{2,1,0:T(8,128)} %param.9) | copy-start | bytes 1572868
  3.4 6.0 %copy-start = (f32[4,128,256]{2,1,0:T(8,128)S(1)}, f32[4,128,256]{2,1,0:T(8,128)}, u32[]{:S(2)}) copy-start(f32[4,128,256]{2,1,0:T(8,128)} %param.8) | copy-start | bytes 1572868
  3.4 42.3 %collective-permute-start.1 = (f32[2,128,256]{2,1,0:T(8,128)}, f32[2,128,256]{2,1,0:T(8,128)S(1)}, u32[]{:S(2)}, u32[]{:S(2)}) collective-permute-start(f32[2,128,256]{2,1,0:T(8,128)} %get-tuple-element.79), channel_id=1, source_target_pairs={{0,1},{1,2},{2,3},{3,4},{4,5},{5,6},{6,7},{7,8},{8,9},{9,10},{10,1... | collective-permute-start | bytes 786440 | tf_op jit(solution)/shard_map/ppermute | solution.py:22
  6.1 39.6 %collective-permute-start.2 = (f32[2,128,256]{2,1,0:T(8,128)S(1)}, f32[2,128,256]{2,1,0:T(8,128)S(1)}, u32[]{:S(2)}, u32[]{:S(2)}) collective-permute-start(f32[2,128,256]{2,1,0:T(8,128)S(1)} %get-tuple-element.80), channel_id=1, source_target_pairs={{1,0},{2,1},{3,2},{4,3},{5,4},{6,5},{7,6},{8,7},{9,8},{10,9},{11,1... | collective-permute-start | bytes 786440 | tf_op jit(solution)/shard_map/ppermute | solution.py:23
  8.5 0.8 copy-start.4
  9.3 1.8 %copy-start.2 = (f32[4,128,256]{2,1,0:T(8,128)S(1)}, f32[4,128,256]{2,1,0:T(8,128)}, u32[]{:S(2)}) copy-start(f32[4,128,256]{2,1,0:T(8,128)} %param.7) | copy-start | bytes 1572868
  9.4 0.7 copy-start.3
  55.1 7.1 %collective-permute-start.3 = (f32[1,128,256]{2,1,0:T(8,128)S(1)}, f32[1,128,256]{2,1,0:T(8,128)S(1)}, u32[]{:S(2)}, u32[]{:S(2)}) collective-permute-start(f32[1,128,256]{2,1,0:T(8,128)S(1)} %get-tuple-element.71), channel_id=1, source_target_pairs={{0,1},{1,2},{2,3},{3,4},{4,5},{5,6},{6,7},{7,8},{8,9},{9,10},{10,1... | collective-permute-start | bytes 393224 | tf_op jit(solution)/shard_map/ppermute | solution.py:22
  55.2 7.1 %collective-permute-start.4 = (f32[1,128,256]{2,1,0:T(8,128)S(1)}, f32[1,128,256]{2,1,0:T(8,128)S(1)}, u32[]{:S(2)}, u32[]{:S(2)}) collective-permute-start(f32[1,128,256]{2,1,0:T(8,128)S(1)} %get-tuple-element.72), channel_id=1, source_target_pairs={{1,0},{2,1},{3,2},{4,3},{5,4},{6,5},{7,6},{8,7},{9,8},{10,9},{11,1... | collective-permute-start | bytes 393224 | tf_op jit(solution)/shard_map/ppermute | solution.py:23
  70.0 7.1 %collective-permute-start.5 = (f32[1,128,256]{2,1,0:T(8,128)S(1)}, f32[1,128,256]{2,1,0:T(8,128)S(1)}, u32[]{:S(2)}, u32[]{:S(2)}) collective-permute-start(f32[1,128,256]{2,1,0:T(8,128)S(1)} %get-tuple-element.61), channel_id=1, source_target_pairs={{0,1},{1,2},{2,3},{3,4},{4,5},{5,6},{6,7},{7,8},{8,9},{9,10},{10,1... | collective-permute-start | bytes 393224 | tf_op jit(solution)/shard_map/ppermute | solution.py:22
  70.1 7.1 %collective-permute-start.6 = (f32[1,128,256]{2,1,0:T(8,128)S(1)}, f32[1,128,256]{2,1,0:T(8,128)S(1)}, u32[]{:S(2)}, u32[]{:S(2)}) collective-permute-start(f32[1,128,256]{2,1,0:T(8,128)S(1)} %get-tuple-element.62), channel_id=1, source_target_pairs={{1,0},{2,1},{3,2},{4,3},{5,4},{6,5},{7,6},{8,7},{9,8},{10,9},{11,1... | collective-permute-start | bytes 393224 | tf_op jit(solution)/shard_map/ppermute | solution.py:23
  85.5 8.6 %collective-permute-start.7 = (f32[2,128,256]{2,1,0:T(8,128)S(1)}, f32[2,128,256]{2,1,0:T(8,128)S(1)}, u32[]{:S(2)}, u32[]{:S(2)}) collective-permute-start(f32[2,128,256]{2,1,0:T(8,128)S(1)} %get-tuple-element.55), channel_id=1, source_target_pairs={{0,1},{1,2},{2,3},{3,4},{4,5},{5,6},{6,7},{7,8},{8,9},{9,10},{10,1... | collective-permute-start | bytes 786440 | tf_op jit(solution)/shard_map/ppermute | solution.py:22
  85.5 8.6 %collective-permute-start.8 = (f32[2,128,256]{2,1,0:T(8,128)S(1)}, f32[2,128,256]{2,1,0:T(8,128)S(1)}, u32[]{:S(2)}, u32[]{:S(2)}) collective-permute-start(f32[2,128,256]{2,1,0:T(8,128)S(1)} %get-tuple-element.56), channel_id=1, source_target_pairs={{1,0},{2,1},{3,2},{4,3},{5,4},{6,5},{7,6},{8,7},{9,8},{10,9},{11,1... | collective-permute-start | bytes 786440 | tf_op jit(solution)/shard_map/ppermute | solution.py:23
  103.5 7.3 %collective-permute-start.9 = (f32[1,128,256]{2,1,0:T(8,128)S(1)}, f32[1,128,256]{2,1,0:T(8,128)S(1)}, u32[]{:S(2)}, u32[]{:S(2)}) collective-permute-start(f32[1,128,256]{2,1,0:T(8,128)S(1)} %get-tuple-element.49), channel_id=1, source_target_pairs={{0,1},{1,2},{2,3},{3,4},{4,5},{5,6},{6,7},{7,8},{8,9},{9,10},{10,1... | collective-permute-start | bytes 393224 | tf_op jit(solution)/shard_map/ppermute | solution.py:22
  103.6 7.2 %collective-permute-start.10 = (f32[1,128,256]{2,1,0:T(8,128)S(1)}, f32[1,128,256]{2,1,0:T(8,128)S(1)}, u32[]{:S(2)}, u32[]{:S(2)}) collective-permute-start(f32[1,128,256]{2,1,0:T(8,128)S(1)} %get-tuple-element.50), channel_id=1, source_target_pairs={{1,0},{2,1},{3,2},{4,3},{5,4},{6,5},{7,6},{8,7},{9,8},{10,9},{11,1... | collective-permute-start | bytes 393224 | tf_op jit(solution)/shard_map/ppermute | solution.py:23
  118.6 7.2 %collective-permute-start.11 = (f32[1,128,256]{2,1,0:T(8,128)S(1)}, f32[1,128,256]{2,1,0:T(8,128)S(1)}, u32[]{:S(2)}, u32[]{:S(2)}) collective-permute-start(f32[1,128,256]{2,1,0:T(8,128)S(1)} %get-tuple-element.39), channel_id=1, source_target_pairs={{0,1},{1,2},{2,3},{3,4},{4,5},{5,6},{6,7},{7,8},{8,9},{9,10},{10,1... | collective-permute-start | bytes 393224 | tf_op jit(solution)/shard_map/ppermute | solution.py:22
  118.7 7.1 %collective-permute-start.12 = (f32[1,128,256]{2,1,0:T(8,128)S(1)}, f32[1,128,256]{2,1,0:T(8,128)S(1)}, u32[]{:S(2)}, u32[]{:S(2)}) collective-permute-start(f32[1,128,256]{2,1,0:T(8,128)S(1)} %get-tuple-element.40), channel_id=1, source_target_pairs={{1,0},{2,1},{3,2},{4,3},{5,4},{6,5},{7,6},{8,7},{9,8},{10,9},{11,1... | collective-permute-start | bytes 393224 | tf_op jit(solution)/shard_map/ppermute | solution.py:23
where the time goes:
time: 135 us
  other arithmetic  49.4 us (37%)
  blocking collectives  30.7 us (23%)
  starting transfers between devices  28.7 us (21%)
  waiting for transfers between devices  14.3 us (11%)
  local copies, waits for them, and re-layouts  8.61 us (6%)
  between operations  3.17 us (2%)
    mul x6, other arithmetic, flux_volume(): return heading * phase_moved  41.1 us
    pmax x1, blocking collectives, shards(): speed_peak = lax.pmax(local_peak, 'gx')  30.7 us
    ppermute x6, starting transfers between devices, padded_2(): after = lax.ppermute(first, axis, down)  25.2 us
    ppermute x6, waiting for transfers between devices, padded_2(): before = lax.ppermute(last, axis, up)  14.2 us
    select_n x6, other arithmetic, normal_field(): normal_z = jnp.where(bottom_layer[None, None, :], contact, normal_z)  2.99 us
    ppermute x6, starting transfers between devices, padded_2(): before = lax.ppermute(last, axis, up)  2.92 us
  transfers between devices with their start and end apart: 13, of which 6 were waited for; matrix products, arithmetic and copies ran while one was open for 4% of the time, Pallas kernels for 0%

commit v1 on v0

v1 whole, which is shorter than its diff:
```python
import functools

import jax
import jax.numpy as jnp
from jax import lax
from jax.experimental import pallas as pl
from jax.experimental.pallas import tpu as pltpu
from jax.sharding import PartitionSpec as P

STEPS = 2
NEWTON = 4
WALL_CLASSES = 4
CFL_NUMBER = 0.45

LANES = 128
PAD = 8
ROWS = 32
HALVES = (0, 1)
OUTER = 3
INNER = 2
VMEM_LIMIT = 24 * 1024 * 1024


def cube(t):
    t = jnp.maximum(t, 0.0)
    return t * t * t


def square(t):
    t = jnp.maximum(t, 0.0)
    return t * t


def rcp(x):
    return pl.reciprocal(x, approx=True)


def plane(donor, span, soft_a, soft_b):
    low = jnp.minimum(soft_a, soft_b)
    high = jnp.maximum(soft_a, soft_b)
    pair = soft_a + soft_b
    half = 0.5 * (span + pair)
    top = jnp.maximum(span, high)
    mid = jnp.minimum(span, high)
    over = half - top
    last = half - jnp.abs(over)
    sign = jnp.where(over > 0.0, -1.0, 1.0)
    flat = low * mid
    bulk = flat * top
    share = jnp.clip(jnp.minimum(donor, 1.0 - donor), 0.0, 0.5)
    goal = bulk * share
    at = half - (0.25 * bulk - 0.5 * goal) * rcp(flat - square(over))
    low_6 = low * (1.0 / 6.0)
    mid_6 = mid * (1.0 / 6.0)
    last_6 = last * (1.0 / 6.0)
    for _ in range(NEWTON - 1):
        by_low = square(at - low)
        by_mid = square(at - mid)
        by_last = sign * square(at - last)
        growth = at * at - by_low - by_mid + by_last
        shift = goal - low_6 * by_low - mid_6 * by_mid + last_6 * by_last
        at = (5.0 / 6.0) * at + shift * rcp(growth)
    return at, low, high, pair, half, bulk


def face_flux(donor, along, soft_a, soft_b, moved):
    forward = moved > 0.0
    span = jnp.abs(along) + 0.2
    at, low, high, pair, half, bulk = plane(donor, span, soft_a, soft_b)
    light = donor <= 0.5
    slab = jnp.abs(moved) * span
    far = at - span
    near = far + slab
    rest = at - slab
    upper = cube(near) - cube(near - low) - cube(far) + cube(far - low)
    lower = (
        at * at * at
        - cube(at - low)
        - cube(at - high)
        + cube(at - pair)
        - cube(rest)
        + cube(rest - low)
        + cube(rest - high)
        - cube(rest - pair)
    )
    sense = jnp.where(jnp.logical_xor(light, forward), -1.0, 1.0)
    weight = jnp.clip(0.5 + (along * sense) * rcp(half), 0.0, 1.0)
    part = (lower + weight * (upper - lower)) * (sense * rcp(6.0 * bulk))
    return part + jnp.where(light, 0.0, moved)


def lane_of(value):
    return lax.broadcasted_iota(jnp.int32, value.shape, 1)


def from_above(pair):
    turned = [pltpu.roll(v, LANES - 1, 1) for v in pair]
    last = lane_of(pair[0]) == LANES - 1
    return [jnp.where(last, turned[1], turned[0]), jnp.where(last, turned[0], turned[1])]


def from_below(pair):
    turned = [pltpu.roll(v, 1, 1) for v in pair]
    first = lane_of(pair[0]) == 0
    return [jnp.where(first, turned[1], turned[0]), jnp.where(first, turned[0], turned[1])]


class Layer:
    def __init__(self, ref, index, padded=True):
        self.ref, self.index, self.pad = ref, index, PAD if padded else 0

    def read(self, half, row):
        return self.ref[self.index, half, pl.ds(self.pad + row, ROWS), :]

    def write(self, half, row, value):
        self.ref[self.index, half, pl.ds(self.pad + row, ROWS), :] = value

    def wrap(self):
        rows = self.ref.shape[2] - 2 * PAD
        for h in HALVES:
            self.ref[self.index, h, pl.ds(0, PAD), :] = self.ref[self.index, h, pl.ds(rows, PAD), :]
            self.ref[self.index, h, pl.ds(PAD + rows, PAD), :] = self.ref[self.index, h, pl.ds(PAD, PAD), :]


def copy_layer(source, target, rows):
    for r in range(0, rows, ROWS):
        for h in HALVES:
            target.write(h, r, source.read(h, r))


def fill(source, field, start, way, count, padded):
    rows = field.shape[2] - 2 * PAD

    @pl.loop(0, count)
    def _(k):
        target = Layer(field, start + way * k)
        copy_layer(Layer(source, k, padded), target, rows)
        target.wrap()


def normals(before, here, after, wall, row):
    centre = [here.read(h, row) for h in HALVES]
    n_x = [before.read(h, row) - after.read(h, row) for h in HALVES]
    n_y = [here.read(h, row - 1) - here.read(h, row + 1) for h in HALVES]
    above = from_above(centre)
    below = from_below(centre)
    lane = lane_of(centre[0])
    above[1] = jnp.where(lane == LANES - 1, centre[1], above[1])
    n_z = [below[h] - above[h] for h in HALVES]
    contact = wall[pl.ds(row, ROWS), :] * (jnp.abs(n_x[0]) + jnp.abs(n_y[0]))
    n_z[0] = jnp.where(lane == 0, contact, n_z[0])
    return centre, n_x, n_y, n_z


def soft(normal):
    return jnp.abs(normal) + 0.2


def own_index(odd, layer, count):
    return jnp.where(odd, OUTER + count - 1 - layer, layer - OUTER)


def natural(ref, index, half, row):
    return ref[index, pl.ds(row, ROWS), half * LANES : (half + 1) * LANES]


def peak_kernel(a_ref, b_ref, c_ref, out_ref):
    count, rows, width = a_ref.shape
    best = jnp.zeros((8, width), jnp.float32)
    for i in range(count):
        for ref in (a_ref, b_ref, c_ref):
            best = jnp.maximum(best, jnp.max(jnp.abs(ref[i]).reshape(rows // 8, 8, width), axis=0))
    out_ref[...] = jnp.maximum(best[:, :LANES], best[:, LANES:])


def begin_kernel(odd_ref, fraction, mask, first, state, send_outer, send_inner):
    odd = odd_ref[0] == 1
    count, rows, _ = fraction.shape
    for p in range(OUTER, OUTER + count):
        index = own_index(odd, p, count)
        to = [Layer(state, p - OUTER)]
        if p - OUTER < OUTER:
            to.append(Layer(send_outer, p - OUTER, False))
        if OUTER + count - 1 - p < INNER:
            to.append(Layer(send_inner, OUTER + count - 1 - p, False))
        for r in range(0, rows, ROWS):
            for h in HALVES:
                value = jnp.where(natural(mask, index, h, r) == 1, 1.0, natural(fraction, index, h, r))
                for target in to:
                    target.write(h, r, value)
        Layer(state, p - OUTER).wrap()
    near = jnp.where(odd, count - 2, 0)
    for r in range(0, rows, ROWS):
        for h in HALVES:
            Layer(send_outer, OUTER, False).write(h, r, natural(first, near, h, r))
            Layer(send_outer, OUTER + 1, False).write(h, r, natural(first, count - 1, h, r))
            Layer(send_inner, INNER, False).write(h, r, natural(first, count - 1, h, r))


def wall_kernel(where_ref, cosine, out):
    odd = where_ref[0] == 1
    total = cosine.shape[0]
    layers = out.shape[0]
    count = layers - OUTER - INNER
    for p in range(1, layers - 1):
        row = lax.rem(where_ref[1] + own_index(odd, p, count) + total, total)
        out[p] = jnp.transpose(jnp.broadcast_to(cosine[pl.ds(row, 1), :], (LANES, cosine.shape[1])))


def moved_kernel(odd_ref, peak, first, outer, inner, out, step_out):
    odd = odd_ref[0] == 1
    count, rows, _ = first.shape
    largest = jnp.max(peak[...])
    step = CFL_NUMBER / (jnp.full((8, LANES), largest, jnp.float32) + 1e-6)
    step_out[...] = step
    signed = jnp.where(odd, -step, step)[:1, :]
    for face in range(1, OUTER + count):
        for r in range(0, rows, ROWS):
            for h in HALVES:
                if face == 1:
                    value = Layer(outer, OUTER, False).read(h, r)
                elif face == OUTER - 1:
                    value = jnp.where(odd, natural(first, count - 1, h, r), Layer(outer, OUTER + 1, False).read(h, r))
                elif face == OUTER + count - 1:
                    value = jnp.where(odd, Layer(inner, INNER, False).read(h, r), natural(first, count - 1, h, r))
                else:
                    value = natural(first, jnp.where(odd, OUTER + count - 2 - face, face - OUTER), h, r)
                Layer(out, face - 1, False).write(h, r, value * signed)


def first_kernel(*refs, own_parts, layers):
    own, (outer, inner, moved, wall, out, send, field, n_s, n_a, n_b, flux) = refs[:own_parts], refs[own_parts:]
    rows = moved.shape[2]
    start = OUTER
    for ref in own:
        fill(ref, field, start, 1, ref.shape[0], True)
        start += ref.shape[0]
    fill(outer, field, OUTER - 1, -1, OUTER, False)
    fill(inner, field, start, 1, INNER, False)

    def slopes(i, r):
        _, n_x, n_y, n_z = normals(Layer(field, i - 1), Layer(field, i), Layer(field, i + 1), wall.at[i], r)
        for h in HALVES:
            Layer(n_s, i).write(h, r, n_x[h])
            Layer(n_a, i).write(h, r, soft(n_y[h]))
            Layer(n_b, i).write(h, r, soft(n_z[h]))

    @pl.loop(1, layers - 1)
    def _(i):
        for r in range(0, rows, ROWS):
            slopes(i, r)

    @pl.loop(1, layers - INNER)
    def _(i):
        for r in range(0, rows, ROWS):
            for h in HALVES:
                speed = Layer(moved, i - 1, False).read(h, r)
                ahead = speed > 0.0

                def donor(ref):
                    return jnp.where(ahead, Layer(ref, i).read(h, r), Layer(ref, i + 1).read(h, r))

                through = face_flux(donor(field), donor(n_s), donor(n_a), donor(n_b), speed)
                Layer(flux, i).write(h, r, through)

    @pl.loop(2, layers - INNER)
    def _(i):
        for r in range(0, rows, ROWS):
            for h in HALVES:
                through = Layer(flux, i).read(h, r)
                value = jnp.clip(Layer(field, i).read(h, r) - through + Layer(flux, i - 1).read(h, r), 0.0, 1.0)
                Layer(out, i - 1).write(h, r, value)
        Layer(out, i - 1).wrap()

    copy_layer(Layer(out, layers - INNER - 2), Layer(send, 0, False), rows)


def second_sweep(before, here, after, wall, speed, out, scratch):
    n_s, n_a, n_b, flux = scratch
    rows = out.ref.shape[2] - 2 * PAD
    for r in range(0, rows, ROWS):
        _, n_x, n_y, n_z = normals(before, here, after, wall, r)
        for h in HALVES:
            n_s.write(h, r, n_y[h])
            n_a.write(h, r, soft(n_x[h]))
            n_b.write(h, r, soft(n_z[h]))
    for s in (n_s, n_a, n_b):
        s.wrap()
    for r in range(0, rows, ROWS):
        for h in HALVES:
            moved = speed(h, r)
            ahead = moved > 0.0
            donor = [jnp.where(ahead, s.read(h, r), s.read(h, r + 1)) for s in (here, n_s, n_a, n_b)]
            flux.write(h, r, face_flux(*donor, moved))
    flux.wrap()
    for r in range(0, rows, ROWS):
        for h in HALVES:
            out.write(h, r, jnp.clip(here.read(h, r) - flux.read(h, r) + flux.read(h, r - 1), 0.0, 1.0))
    out.wrap()


def third_sweep(before, here, after, wall, speed, outs, rows):
    for r in range(0, rows, ROWS):
        centre, n_x, n_y, n_z = normals(before, here, after, wall, r)
        fields = [centre, n_z, [soft(v) for v in n_x], [soft(v) for v in n_y]]
        above = [from_above(f) for f in fields]
        lane = lane_of(centre[0])
        through = []
        for h in HALVES:
            moved = speed(h, r)
            if h == 1:
                moved = jnp.where(lane == LANES - 1, 0.0, moved)
            ahead = moved > 0.0
            through.append(face_flux(*[jnp.where(ahead, f[h], a[h]) for f, a in zip(fields, above)], moved))
        below = from_below(through)
        for h in HALVES:
            value = jnp.clip(centre[h] - through[h] + below[h], 0.0, 1.0)
            for write in outs:
                write(h, r, value)


def gather_layers(refs, places):
    found = {}
    for ref, (start, padded) in zip(refs, places):
        for k in range(ref.shape[0]):
            found[start + k] = Layer(ref, k, padded)
    return found


def second_kernel(odd_ref, step, speed_ref, wall, *refs, places, work, send_last):
    fields, rest = refs[: len(places)], refs[len(places) :]
    out, rest = rest[0], rest[1:]
    send, rest = (rest[0], rest[1:]) if send_last is not None else (None, rest)
    scratch = [Layer(ref, 0) for ref in rest]
    layers = gather_layers(fields, places)
    odd = odd_ref[0] == 1
    count, rows, _ = speed_ref.shape
    for k, p in enumerate(work):
        index = own_index(odd, p, count)
        second_sweep(
            layers[p - 1],
            layers[p],
            layers[p + 1],
            wall.at[p],
            lambda h, r: natural(speed_ref, index, h, r) * step[:1, :],
            Layer(out, k),
            scratch,
        )
    if send is not None:
        copy_layer(Layer(out, work.index(send_last)), Layer(send, 0, False), rows)


def third_kernel(odd_ref, step, speed_ref, wall, *refs, places, work, final):
    fields, outs = refs[: len(places)], refs[len(places) :]
    layers = gather_layers(fields, places)
    odd = odd_ref[0] == 1
    count, rows, _ = speed_ref.shape
    out = outs[0]
    for k, p in enumerate(work):
        index = own_index(odd, p, count)
        if final:
            def write(h, r, value, index=index):
                out[index, pl.ds(r, ROWS), h * LANES : (h + 1) * LANES] = value
        else:
            write = Layer(out, k).write
        third_sweep(
            layers[p - 1],
            layers[p],
            layers[p + 1],
            wall.at[p],
            lambda h, r: natural(speed_ref, index, h, r) * step[:1, :],
            [write],
            rows,
        )
        if not final:
            Layer(out, k).wrap()


IN_VMEM = pl.BlockSpec(memory_space=pltpu.VMEM)
IN_SMEM = pl.BlockSpec(memory_space=pltpu.SMEM)


def held(shape):
    return pltpu.VMEM(shape, jnp.float32)


def call(kernel, name, outs, scalars, arrays, scratch=(), faces=0.0, in_hbm=()):
    arrays = [pltpu.with_memory_space_constraint(a, pltpu.VMEM) for a in arrays]
    work = int(faces * 32 * 1024 * 220) + 1024
    return pl.pallas_call(
        kernel,
        out_shape=outs,
        in_specs=[IN_SMEM] * len(scalars) + [IN_VMEM] * len(arrays),
        out_specs=[IN_VMEM] * len(outs),
        scratch_shapes=list(scratch),
        compiler_params=pltpu.CompilerParams(vmem_limit_bytes=VMEM_LIMIT),
        cost_estimate=pl.CostEstimate(flops=work, bytes_accessed=1024, transcendentals=0),
        name=name,
    )(*scalars, *arrays)


def swap(array, outer):
    count = lax.axis_size("gx")
    if outer:
        pairs = [(i, (i + 1) % count if i % 2 else (i - 1) % count) for i in range(count)]
    else:
        pairs = [(i, i ^ 1) for i in range(count)]
    return lax.ppermute(array, "gx", pairs)


def largest_over(array):
    count = lax.axis_size("gx")
    reach = 1
    while reach < count:
        if count & (count - 1) == 0:
            pairs = [(i, i ^ reach) for i in range(count)]
        else:
            pairs = [(i, (i + reach) % count) for i in range(count)]
        array = jnp.maximum(array, lax.ppermute(array, "gx", pairs))
        reach *= 2
    return array


def shards(fraction, first, second, third, wall_class, seed_mask):
    count, rows, width = fraction.shape
    layers = OUTER + count + INNER
    own_end = OUTER + count
    device = lax.axis_index("gx")
    odd = (device % 2).astype(jnp.int32).reshape(1)
    place = jnp.stack([device % 2, device * count]).astype(jnp.int32)

    def padded(n):
        return (n, 2, rows + 2 * PAD, LANES)

    def plain(n):
        return (n, 2, rows, LANES)

    first, second, third = (pltpu.with_memory_space_constraint(v, pltpu.VMEM) for v in (first, second, third))
    (peak,) = call(peak_kernel, "peak", [held((8, LANES))], [], [first, second, third])
    peak = largest_over(peak)
    state, send_outer, send_inner = call(
        begin_kernel,
        "begin",
        [held(padded(count)), held(plain(OUTER + 2)), held(plain(INNER + 1))],
        [odd],
        [fraction, seed_mask, first],
    )
    outer = swap(send_outer, True)
    inner = swap(send_inner, False)
    cosine = jnp.cos(jnp.pi * (wall_class.astype(jnp.float32) + 1.0) / (WALL_CLASSES + 1))
    (wall,) = call(wall_kernel, "wall", [held((layers, rows, LANES))], [place], [cosine])
    moved, step = call(
        moved_kernel, "moved", [held(plain(layers - INNER - 1)), held((8, LANES))], [odd], [peak, first, outer, inner]
    )
    own = [state]
    line = [pltpu.VMEM(padded(1), jnp.float32)] * 4
    for turn in range(STEPS):
        final = turn == STEPS - 1
        swept, send = call(
            functools.partial(first_kernel, own_parts=len(own), layers=layers),
            "first",
            [held(padded(layers - INNER - 1)), held(plain(1))],
            [],
            [*own, outer, inner, moved, wall],
            [pltpu.VMEM(padded(layers), jnp.float32)] * 5,
            faces=layers - INNER - 1,
        )
        inner = swap(send, False)

        def second_call(work, fields, places, send_last):
            outs = [held(padded(len(work)))] + ([held(plain(1))] if send_last is not None else [])
            return call(
                functools.partial(second_kernel, places=places, work=work, send_last=send_last),
                "second",
                outs,
                [odd],
                [step, second, wall, *fields],
                line,
                faces=len(work),
            )

        edge, send_outer = second_call((OUTER,), [swept], [(1, True)], OUTER)
        outer = swap(send_outer, True)
        (middle,) = second_call(tuple(range(OUTER + 1, own_end - 1)), [swept], [(1, True)], None)
        last, send_inner = second_call(
            (own_end - 1,), [swept, inner], [(1, True), (own_end, False)], own_end - 1
        )
        inner = swap(send_inner, False)

        def third_call(work, fields, places, out):
            return call(
                functools.partial(third_kernel, places=places, work=work, final=False),
                "third",
                [out],
                [odd],
                [step, third, wall, *fields],
                faces=len(work),
            )[0]

        middle_new = third_call(
            tuple(range(OUTER + 1, own_end - 1)),
            [edge, middle, last],
            [(OUTER, True), (OUTER + 1, True), (own_end - 1, True)],
            held(padded(count - 2)),
        )
        last_new = third_call(
            (own_end - 1,),
            [middle, last, inner],
            [(OUTER + 1, True), (own_end - 1, True), (own_end, False)],
            held(padded(1)),
        )
        edge_new = third_call(
            (OUTER,),
            [outer, edge, middle],
            [(OUTER - 1, False), (OUTER, True), (OUTER + 1, True)],
            held(padded(1)),
        )
        own = [edge_new, middle_new, last_new]
        if not final:
            send_outer, send_inner = call(
                pack_kernel, "pack", [held(plain(OUTER)), held(plain(INNER))], [], own
            )
            outer = swap(send_outer, True)
            inner = swap(send_inner, False)
    (out,) = call(unpack_kernel, "unpack", [jax.ShapeDtypeStruct(fraction.shape, jnp.float32)], [odd], own)
    return out


def pack_kernel(edge, middle, last, send_outer, send_inner):
    rows = send_outer.shape[2]
    own = [Layer(ref, k) for ref in (edge, middle, last) for k in range(ref.shape[0])]
    for k in range(OUTER):
        copy_layer(own[k], Layer(send_outer, k, False), rows)
    for k in range(INNER):
        copy_layer(own[-1 - k], Layer(send_inner, k, False), rows)


def unpack_kernel(odd_ref, edge, middle, last, out):
    odd = odd_ref[0] == 1
    count, rows, _ = out.shape
    own = [Layer(ref, k) for ref in (edge, middle, last) for k in range(ref.shape[0])]
    for k, layer in enumerate(own):
        index = own_index(odd, OUTER + k, count)
        for r in range(0, rows, ROWS):
            for h in HALVES:
                out[index, pl.ds(r, ROWS), h * LANES : (h + 1) * LANES] = layer.read(h, r)


def solution(mesh):
    split = P(("ens", "gx"), None, None)
    return jax.shard_map(
        shards, mesh=mesh, in_specs=(split, split, split, split, P(), split), out_specs=split, check_vma=False
    )
```

time: 135 us -> 81.3 us (0.60)
  other arithmetic: 49.4 us -> 0.21 us
  Pallas kernels: 0 us -> 32.3 us
  blocking collectives: 30.7 us -> 0 us
  waiting for transfers between devices: 14.3 us -> 25.4 us
  starting transfers between devices: 28.7 us -> 19.8 us
  local copies, waits for them, and re-layouts: 8.61 us -> 3.14 us
  between operations: 3.17 us -> 0.17 us
    mul x6 -> x0, other arithmetic: 41.1 us -> none  [flux_volume(): return heading * phase_moved]
    pallas_call x0 -> x20, Pallas kernels: none -> 32.3 us  [call(): pl.pallas_call(kernel, out_shape=outs, in_specs=[IN_SMEM] * len(scalars)...]
    pmax x1 -> x0, blocking collectives: 30.7 us -> none  [shards(): speed_peak = lax.pmax(local_peak, 'gx')]
    ppermute x13 -> x14, waiting for transfers between devices: 14.3 us -> 25.4 us  [the longest x4 15.7 us: largest_over(): array = jnp.maximum(array, lax.ppermute(array, 'gx', pairs))]
    ppermute x13 -> x14, starting transfers between devices: 28.7 us -> 19.8 us  [the longest x10 15.1 us: swap(): return lax.ppermute(array, 'gx', pairs)]
    slice x57 -> x0, local copies, waits for them, and re-layouts: 7.58 us -> none  [the longest x8 1.61 us: choose_donor(): values[:, :, 1:]]
    select_n x7 -> x0, other arithmetic: 4.26 us -> none  [the longest x6 2.99 us: normal_field(): normal_z = jnp.where(bottom_layer[None, None, :], contact, normal_z)]
    unnamed x11 -> x14, local copies, waits for them, and re-layouts: 1.03 us -> 3.14 us
  transfers between devices with their start and end apart: 13 -> 14, of which waited for: 6 -> 8; matrix products, arithmetic and copies ran while one was open for 4% -> 0% of each run, Pallas kernels for 0% -> 19%
where the time goes in v1:
time: 81.3 us; the launch traced here: 81 us
  Pallas kernels  32.3 us (40%)
  waiting for transfers between devices  25.4 us (31%)
  starting transfers between devices  19.8 us (24%)
  local copies, waits for them, and re-layouts  3.14 us (4%)
    pallas_call x20, Pallas kernels, call(): pl.pallas_call(kernel, out_shape=outs, in_specs=[IN_SMEM] * len(scalars)...  32.3 us
    ppermute x4, waiting for transfers between devices, largest_over(): array = jnp.maximum(array, lax.ppermute(array, 'gx', pairs))  15.7 us
    ppermute x10, starting transfers between devices, swap(): return lax.ppermute(array, 'gx', pairs)  15.1 us
    ppermute x10, waiting for transfers between devices, swap(): return lax.ppermute(array, 'gx', pairs)  9.64 us
    ppermute x4, starting transfers between devices, largest_over(): array = jnp.maximum(array, lax.ppermute(array, 'gx', pairs))  4.72 us
    unnamed x14, local copies, waits for them, and re-layouts  3.14 us
  transfers between devices with their start and end apart: 14, of which 8 were waited for; matrix products, arithmetic and copies ran while one was open for 0% of the time, Pallas kernels for 19%

profile of v1, /device:TPU:0, one launch (start us, length us, event | category | flops | bytes accessed | tf_op | source)
XLA Modules:
  0.0 81.0 jit_solution(1112500108149662385)
XLA Ops:
  0.0 1.0 %copy-done.2 = f32[4,128,256]{2,1,0:T(8,128)S(1)} copy-done((f32[4,128,256]{2,1,0:T(8,128)S(1)}, f32[4,128,256]{2,1,0:T(8,128)}, u32[]{:S(2)}) %copy-start.2) | copy-done | bytes 524312
  1.0 1.0 %copy-done.4 = f32[4,128,256]{2,1,0:T(8,128)S(1)} copy-done((f32[4,128,256]{2,1,0:T(8,128)S(1)}, f32[4,128,256]{2,1,0:T(8,128)}, u32[]{:S(2)}) %copy-start.4) | copy-done | bytes 524312
  2.1 1.0 %copy-done.5 = s32[4,128,256]{2,1,0:T(8,128)S(1)} copy-done((s32[4,128,256]{2,1,0:T(8,128)S(1)}, s32[4,128,256]{2,1,0:T(8,128)}, u32[]{:S(2)}) %copy-start.5) | copy-done | bytes 524312
  3.1 1.1 %begin.1 = (f32[4,2,144,128]{3,2,1,0:T(8,128)S(1)}, f32[5,2,128,128]{3,2,1,0:T(8,128)}, f32[3,2,128,128]{3,2,1,0:T(8,128)}) custom-call(s32[1]{0:T(128)} %bitcast.odd_ref, f32[4,128,256]{2,1,0:T(8,128)S(1)} %copy-done.4, s32[4,128,256]{2,1,0:T(8,128)S(1)} %copy-done.5, f32[4,128,256]{2,1,0:T(8,128)S(1)} %copy-done.2), custom_call_target="tpu_custom_call" | custom-call | flops 1024 | bytes 1024 | tf_op jit(solution)/shard_map/begin/pallas_call | solution.py:390
  4.2 5.4 %collective-permute-start.4 = (f32[5,2,128,128]{3,2,1,0:T(8,128)}, f32[5,2,128,128]{3,2,1,0:T(8,128)S(1)}, u32[]{:S(2)}, u32[]{:S(2)}) collective-permute-start(f32[5,2,128,128]{3,2,1,0:T(8,128)} %get-tuple-element.24), channel_id=1, source_target_pairs={{0,15},{1,2},{2,1},{3,4},{4,3},{5,6},{6,5},{7,8},{8,7},{9,10},{10,... | collective-permute-start | bytes 1966088 | tf_op jit(solution)/shard_map/ppermute | solution.py:408
  9.7 0.0 copy-start.6
  9.7 0.1 peak.1
  9.7 0.0 copy-start.3
  9.8 0.6 collective-permute-start
  10.3 1.1 %collective-permute-done = f32[8,128]{1,0:T(8,128)S(1)} collective-permute-done((f32[8,128]{1,0:T(8,128)S(1)}, f32[8,128]{1,0:T(8,128)S(1)}, u32[]{:S(2)}, u32[]{:S(2)}) %collective-permute-start) | collective-permute-done | bytes 4128 | tf_op jit(solution)/shard_map/ppermute | solution.py:419
  11.4 11.7 %collective-permute-done.1 = f32[8,128]{1,0:T(8,128)S(1)} collective-permute-done((f32[8,128]{1,0:T(8,128)S(1)}, f32[8,128]{1,0:T(8,128)S(1)}, u32[]{:S(2)}, u32[]{:S(2)}) %collective-permute-start.1) | collective-permute-done | bytes 4128 | tf_op jit(solution)/shard_map/ppermute | solution.py:419
  23.1 1.6 %collective-permute-start.2 = (f32[8,128]{1,0:T(8,128)S(1)}, f32[8,128]{1,0:T(8,128)S(1)}, u32[]{:S(2)}, u32[]{:S(2)}) collective-permute-start(f32[8,128]{1,0:T(8,128)S(1)} %max.13), channel_id=1, source_target_pairs={{0,4},{1,5},{2,6},{3,7},{4,0},{5,1},{6,2},{7,3},{8,12},{9,13},{10,... | collective-permute-start | bytes 12296 | tf_op jit(solution)/shard_map/ppermute | solution.py:419
  24.6 0.1 multiply_cosine_fusion.cosine
  24.8 1.9 %collective-permute-done.2 = f32[8,128]{1,0:T(8,128)S(1)} collective-permute-done((f32[8,128]{1,0:T(8,128)S(1)}, f32[8,128]{1,0:T(8,128)S(1)}, u32[]{:S(2)}, u32[]{:S(2)}) %collective-permute-start.2) | collective-permute-done | bytes 4128 | tf_op jit(solution)/shard_map/ppermute | solution.py:419
  26.7 2.6 %collective-permute-start.3 = (f32[8,128]{1,0:T(8,128)S(1)}, f32[8,128]{1,0:T(8,128)S(1)}, u32[]{:S(2)}, u32[]{:S(2)}) collective-permute-start(f32[8,128]{1,0:T(8,128)S(1)} %max.14), channel_id=1, source_target_pairs={{0,8},{1,9},{2,10},{3,11},{4,12},{5,13},{6,14},{7,15},{8,0},{9,1},... | collective-permute-start | bytes 12296 | tf_op jit(solution)/shard_map/ppermute | solution.py:419
  29.3 0.1 pad_add_fusion.where_ref
  29.3 0.7 wall.1.refs_4_.refs_6_
  30.1 1.1 %collective-permute-done.3 = f32[8,128]{1,0:T(8,128)S(1)} collective-permute-done((f32[8,128]{1,0:T(8,128)S(1)}, f32[8,128]{1,0:T(8,128)S(1)}, u32[]{:S(2)}, u32[]{:S(2)}) %collective-permute-start.3) | collective-permute-done | bytes 4128 | tf_op jit(solution)/shard_map/ppermute | solution.py:419
  31.2 0.2 moved.1
  31.4 6.3 %first.6 = (f32[6,2,144,128]{3,2,1,0:T(8,128)S(1)}, f32[1,2,128,128]{3,2,1,0:T(8,128)S(1)}) custom-call(f32[4,2,144,128]{3,2,1,0:T(8,128)S(1)} %get-tuple-element.27.refs_0_, f32[5,2,128,128]{3,2,1,0:T(8,128)S(1)} %collective-permute-done.4.outer.refs_1_, f32[3,2,128,128]{3,2,1,0:T(8,128)S(1)} %collective-permute-done.5.inner.refs_2_, ...), custom_call_target="tpu_custom_call" | custom-call | flops 43254784 | bytes 1024 | tf_op jit(solution)/shard_map/first/pallas_call | solution.py:390
  37.7 0.1 collective-permute-start.7
  37.8 1.0 %second.6 = (f32[1,2,144,128]{3,2,1,0:T(8,128)S(1)}, f32[1,2,128,128]{3,2,1,0:T(8,128)S(1)}) custom-call(s32[1]{0:T(128)} %bitcast.odd_ref, f32[8,128]{1,0:T(8,128)S(1)} %get-tuple-element.26.step, f32[4,128,256]{2,1,0:T(8,128)S(1)} %copy-done, f32[9,128,128]{2,1,0:T(8,128)S(1)} %wall.1.refs_4_.refs_6_, f32[6,2,144,128]{3,2,1,0:T(8,128)S(1)} %get-tuple-element.29.refs_0_), custom_call_target="tpu_custom_call" | custom-call | flops 7209984 | bytes 1024 | tf_op jit(solution)/shard_map/second/pallas_call | solution.py:390
  38.8 2.8 %collective-permute-start.6 = (f32[1,2,128,128]{3,2,1,0:T(8,128)S(1)}, f32[1,2,128,128]{3,2,1,0:T(8,128)S(1)}, u32[]{:S(2)}, u32[]{:S(2)}) collective-permute-start(f32[1,2,128,128]{3,2,1,0:T(8,128)S(1)} %get-tuple-element.30), channel_id=1, source_target_pairs={{0,15},{1,2},{2,1},{3,4},{4,3},{5,6},{6,5},{7,8},{8,7},{9,10},{10,... | collective-permute-start | bytes 393224 | tf_op jit(solution)/shard_map/ppermute | solution.py:408
  41.6 1.0 %second.8 = (f32[1,2,144,128]{3,2,1,0:T(8,128)S(1)}, f32[1,2,128,128]{3,2,1,0:T(8,128)S(1)}) custom-call(s32[1]{0:T(128)} %bitcast.odd_ref, f32[8,128]{1,0:T(8,128)S(1)} %get-tuple-element.26.step, f32[4,128,256]{2,1,0:T(8,128)S(1)} %copy-done, f32[9,128,128]{2,1,0:T(8,128)S(1)} %wall.1.refs_4_.refs_6_, f32[6,2,144,128]{3,2,1,0:T(8,128)S(1)} %get-tuple-element.29.refs_0_, ...), custom_call_target="tpu_custom_call" | custom-call | flops 7209984 | bytes 1024 | tf_op jit(solution)/shard_map/second/pallas_call | solution.py:390
  42.6 0.1 collective-permute-start.8
  42.7 1.9 %second.7.refs_2_.refs_1_.refs_0_ = f32[2,2,144,128]{3,2,1,0:T(8,128)S(1)} custom-call(s32[1]{0:T(128)} %bitcast.odd_ref, f32[8,128]{1,0:T(8,128)S(1)} %get-tuple-element.26.step, f32[4,128,256]{2,1,0:T(8,128)S(1)} %copy-done, f32[9,128,128]{2,1,0:T(8,128)S(1)} %wall.1.refs_4_.refs_6_, f32[6,2,144,128]{3,2,1,0:T(8,128)S(1)} %get-tuple-element.29.refs_0_), custom_call_target="tpu_custom_call" | custom-call | flops 14418944 | bytes 1024 | tf_op jit(solution)/shard_map/second/pallas_call | solution.py:390
  44.6 1.3 %collective-permute-done.6.refs_0_ = f32[1,2,128,128]{3,2,1,0:T(8,128)S(1)} collective-permute-done((f32[1,2,128,128]{3,2,1,0:T(8,128)S(1)}, f32[1,2,128,128]{3,2,1,0:T(8,128)S(1)}, u32[]{:S(2)}, u32[]{:S(2)}) %collective-permute-start.6) | collective-permute-done | bytes 131104 | tf_op jit(solution)/shard_map/ppermute | solution.py:408
  45.9 1.1 %third.6.edge.refs_0_ = f32[1,2,144,128]{3,2,1,0:T(8,128)S(1)} custom-call(s32[1]{0:T(128)} %bitcast.odd_ref, f32[8,128]{1,0:T(8,128)S(1)} %get-tuple-element.26.step, f32[4,128,256]{2,1,0:T(8,128)S(1)} %copy-done.1, f32[9,128,128]{2,1,0:T(8,128)S(1)} %wall.1.refs_4_.refs_6_, f32[1,2,128,128]{3,2,1,0:T(8,128)S(1)} %collective-permute-done.6.refs_0_, ...), custom_call_target="tpu_custom_call" | custom-call | flops 7209984 | bytes 1024 | tf_op jit(solution)/shard_map/third/pallas_call | solution.py:390
  47.0 2.2 %third.7.middle.refs_1_ = f32[2,2,144,128]{3,2,1,0:T(8,128)S(1)} custom-call(s32[1]{0:T(128)} %bitcast.odd_ref, f32[8,128]{1,0:T(8,128)S(1)} %get-tuple-element.26.step, f32[4,128,256]{2,1,0:T(8,128)S(1)} %copy-done.1, f32[9,128,128]{2,1,0:T(8,128)S(1)} %wall.1.refs_4_.refs_6_, f32[1,2,144,128]{3,2,1,0:T(8,128)S(1)} %get-tuple-element.31.refs_1_.refs_0_, ...), custom_call_target="tpu_custom_call" | custom-call | flops 14418944 | bytes 1024 | tf_op jit(solution)/shard_map/third/pallas_call | solution.py:390
  49.2 0.0 collective-permute-done.8.refs_2_
  49.2 1.1 %third.8.last.refs_2_ = f32[1,2,144,128]{3,2,1,0:T(8,128)S(1)} custom-call(s32[1]{0:T(128)} %bitcast.odd_ref, f32[8,128]{1,0:T(8,128)S(1)} %get-tuple-element.26.step, f32[4,128,256]{2,1,0:T(8,128)S(1)} %copy-done.1, f32[9,128,128]{2,1,0:T(8,128)S(1)} %wall.1.refs_4_.refs_6_, f32[2,2,144,128]{3,2,1,0:T(8,128)S(1)} %second.7.refs_2_.refs_1_.refs_0_, ...), custom_call_target="tpu_custom_call" | custom-call | flops 7209984 | bytes 1024 | tf_op jit(solution)/shard_map/third/pallas_call | solution.py:390
  50.3 0.1 pack.1
  50.4 2.8 %collective-permute-start.9 = (f32[3,2,128,128]{3,2,1,0:T(8,128)S(1)}, f32[3,2,128,128]{3,2,1,0:T(8,128)S(1)}, u32[]{:S(2)}, u32[]{:S(2)}) collective-permute-start(f32[3,2,128,128]{3,2,1,0:T(8,128)S(1)} %get-tuple-element.35), channel_id=1, source_target_pairs={{0,15},{1,2},{2,1},{3,4},{4,3},{5,6},{6,5},{7,8},{8,7},{9,10},{10,... | collective-permute-start | bytes 1179656 | tf_op jit(solution)/shard_map/ppermute | solution.py:408
  53.2 1.5 %collective-permute-done.10.refs_4_ = f32[2,2,128,128]{3,2,1,0:T(8,128)S(1)} collective-permute-done((f32[2,2,128,128]{3,2,1,0:T(8,128)S(1)}, f32[2,2,128,128]{3,2,1,0:T(8,128)S(1)}, u32[]{:S(2)}, u32[]{:S(2)}) %collective-permute-start.10) | collective-permute-done | bytes 262176 | tf_op jit(solution)/shard_map/ppermute | solution.py:408
  54.8 5.7 %collective-permute-done.9.refs_3_ = f32[3,2,128,128]{3,2,1,0:T(8,128)S(1)} collective-permute-done((f32[3,2,128,128]{3,2,1,0:T(8,128)S(1)}, f32[3,2,128,128]{3,2,1,0:T(8,128)S(1)}, u32[]{:S(2)}, u32[]{:S(2)}) %collective-permute-start.9) | collective-permute-done | bytes 393248 | tf_op jit(solution)/shard_map/ppermute | solution.py:408
  60.5 6.5 %first.7 = (f32[6,2,144,128]{3,2,1,0:T(8,128)S(1)}, f32[1,2,128,128]{3,2,1,0:T(8,128)S(1)}) custom-call(f32[1,2,144,128]{3,2,1,0:T(8,128)S(1)} %third.6.edge.refs_0_, f32[2,2,144,128]{3,2,1,0:T(8,128)S(1)} %third.7.middle.refs_1_, f32[1,2,144,128]{3,2,1,0:T(8,128)S(1)} %third.8.last.refs_2_, f32[3,2,128,128]{3,2,1,0:T(8,128)S(1)} %collective-permute-done.9.refs_3_, ...), custom_call_target="tpu_custom_call" | custom-call | flops 43254784 | bytes 1024 | tf_op jit(solution)/shard_map/first/pallas_call | solution.py:390
  67.0 0.6 collective-permute-start.12
  67.6 1.0 %second.9 = (f32[1,2,144,128]{3,2,1,0:T(8,128)S(1)}, f32[1,2,128,128]{3,2,1,0:T(8,128)S(1)}) custom-call(s32[1]{0:T(128)} %bitcast.odd_ref, f32[8,128]{1,0:T(8,128)S(1)} %get-tuple-element.26.step, f32[4,128,256]{2,1,0:T(8,128)S(1)} %copy-done, f32[9,128,128]{2,1,0:T(8,128)S(1)} %wall.1.refs_4_.refs_6_, f32[6,2,144,128]{3,2,1,0:T(8,128)S(1)} %get-tuple-element.37.refs_0_), custom_call_target="tpu_custom_call" | custom-call | flops 7209984 | bytes 1024 | tf_op jit(solution)/shard_map/second/pallas_call | solution.py:390
  68.6 3.1 %collective-permute-start.11 = (f32[1,2,128,128]{3,2,1,0:T(8,128)S(1)}, f32[1,2,128,128]{3,2,1,0:T(8,128)S(1)}, u32[]{:S(2)}, u32[]{:S(2)}) collective-permute-start(f32[1,2,128,128]{3,2,1,0:T(8,128)S(1)} %get-tuple-element.38), channel_id=1, source_target_pairs={{0,15},{1,2},{2,1},{3,4},{4,3},{5,6},{6,5},{7,8},{8,7},{9,10},{10,... | collective-permute-start | bytes 393224 | tf_op jit(solution)/shard_map/ppermute | solution.py:408
  71.8 1.0 %second.11 = (f32[1,2,144,128]{3,2,1,0:T(8,128)S(1)}, f32[1,2,128,128]{3,2,1,0:T(8,128)S(1)}) custom-call(s32[1]{0:T(128)} %bitcast.odd_ref, f32[8,128]{1,0:T(8,128)S(1)} %get-tuple-element.26.step, f32[4,128,256]{2,1,0:T(8,128)S(1)} %copy-done, f32[9,128,128]{2,1,0:T(8,128)S(1)} %wall.1.refs_4_.refs_6_, f32[6,2,144,128]{3,2,1,0:T(8,128)S(1)} %get-tuple-element.37.refs_0_, ...), custom_call_target="tpu_custom_call" | custom-call | flops 7209984 | bytes 1024 | tf_op jit(solution)/shard_map/second/pallas_call | solution.py:390
  72.8 0.1 collective-permute-start.13
  72.9 1.9 %second.10.refs_2_.refs_1_.refs_0_ = f32[2,2,144,128]{3,2,1,0:T(8,128)S(1)} custom-call(s32[1]{0:T(128)} %bitcast.odd_ref, f32[8,128]{1,0:T(8,128)S(1)} %get-tuple-element.26.step, f32[4,128,256]{2,1,0:T(8,128)S(1)} %copy-done, f32[9,128,128]{2,1,0:T(8,128)S(1)} %wall.1.refs_4_.refs_6_, f32[6,2,144,128]{3,2,1,0:T(8,128)S(1)} %get-tuple-element.37.refs_0_), custom_call_target="tpu_custom_call" | custom-call | flops 14418944 | bytes 1024 | tf_op jit(solution)/shard_map/second/pallas_call | solution.py:390
  74.8 1.0 %collective-permute-done.11.refs_0_ = f32[1,2,128,128]{3,2,1,0:T(8,128)S(1)} collective-permute-done((f32[1,2,128,128]{3,2,1,0:T(8,128)S(1)}, f32[1,2,128,128]{3,2,1,0:T(8,128)S(1)}, u32[]{:S(2)}, u32[]{:S(2)}) %collective-permute-start.11) | collective-permute-done | bytes 131104 | tf_op jit(solution)/shard_map/ppermute | solution.py:408
  75.8 1.1 %third.9.edge = f32[1,2,144,128]{3,2,1,0:T(8,128)S(1)} custom-call(s32[1]{0:T(128)} %bitcast.odd_ref, f32[8,128]{1,0:T(8,128)S(1)} %get-tuple-element.26.step, f32[4,128,256]{2,1,0:T(8,128)S(1)} %copy-done.1, f32[9,128,128]{2,1,0:T(8,128)S(1)} %wall.1.refs_4_.refs_6_, f32[1,2,128,128]{3,2,1,0:T(8,128)S(1)} %collective-permute-done.11.refs_0_, ...), custom_call_target="tpu_custom_call" | custom-call | flops 7209984 | bytes 1024 | tf_op jit(solution)/shard_map/third/pallas_call | solution.py:390
  76.9 2.2 %third.10.middle = f32[2,2,144,128]{3,2,1,0:T(8,128)S(1)} custom-call(s32[1]{0:T(128)} %bitcast.odd_ref, f32[8,128]{1,0:T(8,128)S(1)} %get-tuple-element.26.step, f32[4,128,256]{2,1,0:T(8,128)S(1)} %copy-done.1, f32[9,128,128]{2,1,0:T(8,128)S(1)} %wall.1.refs_4_.refs_6_, f32[1,2,144,128]{3,2,1,0:T(8,128)S(1)} %get-tuple-element.39.refs_1_.refs_0_, ...), custom_call_target="tpu_custom_call" | custom-call | flops 14418944 | bytes 1024 | tf_op jit(solution)/shard_map/third/pallas_call | solution.py:390
  79.0 0.0 collective-permute-done.13.refs_2_
  79.1 1.1 %third.11.last = f32[1,2,144,128]{3,2,1,0:T(8,128)S(1)} custom-call(s32[1]{0:T(128)} %bitcast.odd_ref, f32[8,128]{1,0:T(8,128)S(1)} %get-tuple-element.26.step, f32[4,128,256]{2,1,0:T(8,128)S(1)} %copy-done.1, f32[9,128,128]{2,1,0:T(8,128)S(1)} %wall.1.refs_4_.refs_6_, f32[2,2,144,128]{3,2,1,0:T(8,128)S(1)} %second.10.refs_2_.refs_1_.refs_0_, ...), custom_call_target="tpu_custom_call" | custom-call | flops 7209984 | bytes 1024 | tf_op jit(solution)/shard_map/third/pallas_call | solution.py:390
  80.2 0.8 %unpack.1 = f32[4,128,256]{2,1,0:T(8,128)} custom-call(s32[1]{0:T(128)} %bitcast.odd_ref, f32[1,2,144,128]{3,2,1,0:T(8,128)S(1)} %third.9.edge, f32[2,2,144,128]{3,2,1,0:T(8,128)S(1)} %third.10.middle, f32[1,2,144,128]{3,2,1,0:T(8,128)S(1)} %third.11.last), custom_call_target="tpu_custom_call" | custom-call | flops 1024 | bytes 1024 | tf_op jit(solution)/shard_map/unpack/pallas_call | solution.py:390
  (20 shorter events, 0.0 us)
Async XLA Ops:
  0.0 1.0 %copy-start.2 = (f32[4,128,256]{2,1,0:T(8,128)S(1)}, f32[4,128,256]{2,1,0:T(8,128)}, u32[]{:S(2)}) copy-start(f32[4,128,256]{2,1,0:T(8,128)} %first.5) | copy-start | bytes 1572868
  1.0 1.0 %copy-start.4 = (f32[4,128,256]{2,1,0:T(8,128)S(1)}, f32[4,128,256]{2,1,0:T(8,128)}, u32[]{:S(2)}) copy-start(f32[4,128,256]{2,1,0:T(8,128)} %fraction.1) | copy-start | bytes 1572868
  2.1 1.0 %copy-start.5 = (s32[4,128,256]{2,1,0:T(8,128)S(1)}, s32[4,128,256]{2,1,0:T(8,128)}, u32[]{:S(2)}) copy-start(s32[4,128,256]{2,1,0:T(8,128)} %mask.1) | copy-start | bytes 1572868
  3.1 6.5 %copy-start = (f32[4,128,256]{2,1,0:T(8,128)S(1)}, f32[4,128,256]{2,1,0:T(8,128)}, u32[]{:S(2)}) copy-start(f32[4,128,256]{2,1,0:T(8,128)} %speed_ref.21) | copy-start | bytes 1572868
  3.1 6.5 %copy-start.1 = (f32[4,128,256]{2,1,0:T(8,128)S(1)}, f32[4,128,256]{2,1,0:T(8,128)}, u32[]{:S(2)}) copy-start(f32[4,128,256]{2,1,0:T(8,128)} %speed_ref.23) | copy-start | bytes 1572868
  4.2 27.0 %collective-permute-start.4 = (f32[5,2,128,128]{3,2,1,0:T(8,128)}, f32[5,2,128,128]{3,2,1,0:T(8,128)S(1)}, u32[]{:S(2)}, u32[]{:S(2)}) collective-permute-start(f32[5,2,128,128]{3,2,1,0:T(8,128)} %get-tuple-element.24), channel_id=1, source_target_pairs={{0,15},{1,2},{2,1},{3,4},{4,3},{5,6},{6,5},{7,8},{8,7},{9,10},{10,... | collective-permute-start | bytes 1966088 | tf_op jit(solution)/shard_map/ppermute | solution.py:408
  9.6 21.5 %collective-permute-start.5 = (f32[3,2,128,128]{3,2,1,0:T(8,128)}, f32[3,2,128,128]{3,2,1,0:T(8,128)S(1)}, u32[]{:S(2)}, u32[]{:S(2)}) collective-permute-start(f32[3,2,128,128]{3,2,1,0:T(8,128)} %get-tuple-element.25), channel_id=1, source_target_pairs={{0,1},{1,0},{2,3},{3,2},{4,5},{5,4},{6,7},{7,6},{8,9},{9,8},{10,11... | collective-permute-start | bytes 1179656 | tf_op jit(solution)/shard_map/ppermute | solution.py:408
  9.7 15.0 %copy-start.6 = (s32[64,128]{1,0:T(8,128)S(1)}, s32[64,128]{1,0:T(8,128)}, u32[]{:S(2)}) copy-start(s32[64,128]{1,0:T(8,128)} %param.10) | copy-start | bytes 98308
  9.7 21.4 %copy-start.3 = (f32[4,128,256]{2,1,0:T(8,128)S(1)}, f32[4,128,256]{2,1,0:T(8,128)}, u32[]{:S(2)}) copy-start(f32[4,128,256]{2,1,0:T(8,128)} %first.5) | copy-start | bytes 1572868
  9.8 1.6 %collective-permute-start = (f32[8,128]{1,0:T(8,128)S(1)}, f32[8,128]{1,0:T(8,128)S(1)}, u32[]{:S(2)}, u32[]{:S(2)}) collective-permute-start(f32[8,128]{1,0:T(8,128)S(1)} %peak.1), channel_id=1, source_target_pairs={{0,1},{1,0},{2,3},{3,2},{4,5},{5,4},{6,7},{7,6},{8,9},{9,8},{10,11... | collective-permute-start | bytes 12296 | tf_op jit(solution)/shard_map/ppermute | solution.py:419
  11.4 11.7 %collective-permute-start.1 = (f32[8,128]{1,0:T(8,128)S(1)}, f32[8,128]{1,0:T(8,128)S(1)}, u32[]{:S(2)}, u32[]{:S(2)}) collective-permute-start(f32[8,128]{1,0:T(8,128)S(1)} %max.12), channel_id=1, source_target_pairs={{0,2},{1,3},{2,0},{3,1},{4,6},{5,7},{6,4},{7,5},{8,10},{9,11},{10,... | collective-permute-start | bytes 12296 | tf_op jit(solution)/shard_map/ppermute | solution.py:419
  23.1 3.6 %collective-permute-start.2 = (f32[8,128]{1,0:T(8,128)S(1)}, f32[8,128]{1,0:T(8,128)S(1)}, u32[]{:S(2)}, u32[]{:S(2)}) collective-permute-start(f32[8,128]{1,0:T(8,128)S(1)} %max.13), channel_id=1, source_target_pairs={{0,4},{1,5},{2,6},{3,7},{4,0},{5,1},{6,2},{7,3},{8,12},{9,13},{10,... | collective-permute-start | bytes 12296 | tf_op jit(solution)/shard_map/ppermute | solution.py:419
  26.7 4.5 %collective-permute-start.3 = (f32[8,128]{1,0:T(8,128)S(1)}, f32[8,128]{1,0:T(8,128)S(1)}, u32[]{:S(2)}, u32[]{:S(2)}) collective-permute-start(f32[8,128]{1,0:T(8,128)S(1)} %max.14), channel_id=1, source_target_pairs={{0,8},{1,9},{2,10},{3,11},{4,12},{5,13},{6,14},{7,15},{8,0},{9,1},... | collective-permute-start | bytes 12296 | tf_op jit(solution)/shard_map/ppermute | solution.py:419
  37.7 3.9 %collective-permute-start.7 = (f32[1,2,128,128]{3,2,1,0:T(8,128)S(1)}, f32[1,2,128,128]{3,2,1,0:T(8,128)S(1)}, u32[]{:S(2)}, u32[]{:S(2)}) collective-permute-start(f32[1,2,128,128]{3,2,1,0:T(8,128)S(1)} %get-tuple-element.32), channel_id=1, source_target_pairs={{0,1},{1,0},{2,3},{3,2},{4,5},{5,4},{6,7},{7,6},{8,9},{9,8},{10,11... | collective-permute-start | bytes 393224 | tf_op jit(solution)/shard_map/ppermute | solution.py:408
  38.8 7.2 %collective-permute-start.6 = (f32[1,2,128,128]{3,2,1,0:T(8,128)S(1)}, f32[1,2,128,128]{3,2,1,0:T(8,128)S(1)}, u32[]{:S(2)}, u32[]{:S(2)}) collective-permute-start(f32[1,2,128,128]{3,2,1,0:T(8,128)S(1)} %get-tuple-element.30), channel_id=1, source_target_pairs={{0,15},{1,2},{2,1},{3,4},{4,3},{5,6},{6,5},{7,8},{8,7},{9,10},{10,... | collective-permute-start | bytes 393224 | tf_op jit(solution)/shard_map/ppermute | solution.py:408
  42.6 6.6 %collective-permute-start.8 = (f32[1,2,128,128]{3,2,1,0:T(8,128)S(1)}, f32[1,2,128,128]{3,2,1,0:T(8,128)S(1)}, u32[]{:S(2)}, u32[]{:S(2)}) collective-permute-start(f32[1,2,128,128]{3,2,1,0:T(8,128)S(1)} %get-tuple-element.34), channel_id=1, source_target_pairs={{0,1},{1,0},{2,3},{3,2},{4,5},{5,4},{6,7},{7,6},{8,9},{9,8},{10,11... | collective-permute-start | bytes 393224 | tf_op jit(solution)/shard_map/ppermute | solution.py:408
  50.4 10.1 %collective-permute-start.9 = (f32[3,2,128,128]{3,2,1,0:T(8,128)S(1)}, f32[3,2,128,128]{3,2,1,0:T(8,128)S(1)}, u32[]{:S(2)}, u32[]{:S(2)}) collective-permute-start(f32[3,2,128,128]{3,2,1,0:T(8,128)S(1)} %get-tuple-element.35), channel_id=1, source_target_pairs={{0,15},{1,2},{2,1},{3,4},{4,3},{5,6},{6,5},{7,8},{8,7},{9,10},{10,... | collective-permute-start | bytes 1179656 | tf_op jit(solution)/shard_map/ppermute | solution.py:408
  53.2 1.5 %collective-permute-start.10 = (f32[2,2,128,128]{3,2,1,0:T(8,128)S(1)}, f32[2,2,128,128]{3,2,1,0:T(8,128)S(1)}, u32[]{:S(2)}, u32[]{:S(2)}) collective-permute-start(f32[2,2,128,128]{3,2,1,0:T(8,128)S(1)} %get-tuple-element.36), channel_id=1, source_target_pairs={{0,1},{1,0},{2,3},{3,2},{4,5},{5,4},{6,7},{7,6},{8,9},{9,8},{10,11... | collective-permute-start | bytes 786440 | tf_op jit(solution)/shard_map/ppermute | solution.py:408
  67.0 4.8 %collective-permute-start.12 = (f32[1,2,128,128]{3,2,1,0:T(8,128)S(1)}, f32[1,2,128,128]{3,2,1,0:T(8,128)S(1)}, u32[]{:S(2)}, u32[]{:S(2)}) collective-permute-start(f32[1,2,128,128]{3,2,1,0:T(8,128)S(1)} %get-tuple-element.40), channel_id=1, source_target_pairs={{0,1},{1,0},{2,3},{3,2},{4,5},{5,4},{6,7},{7,6},{8,9},{9,8},{10,11... | collective-permute-start | bytes 393224 | tf_op jit(solution)/shard_map/ppermute | solution.py:408
  68.6 7.2 %collective-permute-start.11 = (f32[1,2,128,128]{3,2,1,0:T(8,128)S(1)}, f32[1,2,128,128]{3,2,1,0:T(8,128)S(1)}, u32[]{:S(2)}, u32[]{:S(2)}) collective-permute-start(f32[1,2,128,128]{3,2,1,0:T(8,128)S(1)} %get-tuple-element.38), channel_id=1, source_target_pairs={{0,15},{1,2},{2,1},{3,4},{4,3},{5,6},{6,5},{7,8},{8,7},{9,10},{10,... | collective-permute-start | bytes 393224 | tf_op jit(solution)/shard_map/ppermute | solution.py:408
  72.8 6.3 %collective-permute-start.13 = (f32[1,2,128,128]{3,2,1,0:T(8,128)S(1)}, f32[1,2,128,128]{3,2,1,0:T(8,128)S(1)}, u32[]{:S(2)}, u32[]{:S(2)}) collective-permute-start(f32[1,2,128,128]{3,2,1,0:T(8,128)S(1)} %get-tuple-element.42), channel_id=1, source_target_pairs={{0,1},{1,0},{2,3},{3,2},{4,5},{5,4},{6,7},{7,6},{8,9},{9,8},{10,11... | collective-permute-start | bytes 393224 | tf_op jit(solution)/shard_map/ppermute | solution.py:408

commit v2 on v1

v2 whole, which is shorter than its diff:
```python
import functools

import jax
import jax.numpy as jnp
from jax import lax
from jax.experimental import pallas as pl
from jax.experimental.pallas import tpu as pltpu
from jax.sharding import PartitionSpec as P

STEPS = 2
NEWTON = 4
WALL_CLASSES = 4
CFL_NUMBER = 0.45

LANES = 128
PAD = 8
ROWS = 32
HALVES = (0, 1)
OUTER = 2
INNER = 2
VMEM_LIMIT = 24 * 1024 * 1024
SEND_ROUND = 2


def cube(t):
    t = jnp.maximum(t, 0.0)
    return t * t * t


def square(t):
    t = jnp.maximum(t, 0.0)
    return t * t


def rcp(x):
    return pl.reciprocal(x, approx=True)


def plane(donor, span, soft_a, soft_b):
    low = jnp.minimum(soft_a, soft_b)
    high = jnp.maximum(soft_a, soft_b)
    pair = soft_a + soft_b
    half = 0.5 * (span + pair)
    top = jnp.maximum(span, high)
    mid = jnp.minimum(span, high)
    over = half - top
    last = half - jnp.abs(over)
    sign = jnp.where(over > 0.0, -1.0, 1.0)
    flat = low * mid
    bulk = flat * top
    share = jnp.clip(jnp.minimum(donor, 1.0 - donor), 0.0, 0.5)
    goal = bulk * share
    at = half - (0.25 * bulk - 0.5 * goal) * rcp(flat - square(over))
    low_6 = low * (1.0 / 6.0)
    mid_6 = mid * (1.0 / 6.0)
    last_6 = last * (1.0 / 6.0)
    for _ in range(NEWTON - 1):
        by_low = square(at - low)
        by_mid = square(at - mid)
        by_last = sign * square(at - last)
        growth = at * at - by_low - by_mid + by_last
        shift = goal - low_6 * by_low - mid_6 * by_mid + last_6 * by_last
        at = (5.0 / 6.0) * at + shift * rcp(growth)
    return at, low, high, pair, half, bulk


def edge_sum(at, low):
    return cube(at) - cube(at - low)


def side_sum(at, low, high, pair):
    return cube(at) - cube(at - low) - cube(at - high) + cube(at - pair)


def prepare(donor, along, soft_a, soft_b, ahead):
    span = jnp.abs(along) + 0.2
    at, low, high, pair, half, bulk = plane(donor, span, soft_a, soft_b)
    light = donor <= 0.5
    sense = jnp.where(jnp.logical_xor(light, ahead), -1.0, 1.0)
    weight = jnp.clip(0.5 + (along * sense) * rcp(half), 0.0, 1.0)
    whole = side_sum(at, low, high, pair)
    whole = whole - weight * (whole + edge_sum(at - span, low))
    scale = sense * rcp(6.0 * bulk)
    heavy = jnp.where(light, 0.0, 1.0)
    return at, span, low, high, weight, scale, whole, heavy


def finish(at, span, low, high, weight, scale, whole, heavy, moved):
    slab = jnp.abs(moved) * span
    rest = side_sum(at - slab, low, high, low + high)
    near = edge_sum(at - span + slab, low)
    return (whole - rest + weight * (rest + near)) * scale + heavy * moved


def face_flux(donor, along, soft_a, soft_b, moved):
    return finish(*prepare(donor, along, soft_a, soft_b, moved > 0.0), moved)


def lane_of(value):
    return lax.broadcasted_iota(jnp.int32, value.shape, 1)


def from_above(pair):
    turned = [pltpu.roll(v, LANES - 1, 1) for v in pair]
    last = lane_of(pair[0]) == LANES - 1
    return [jnp.where(last, turned[1], turned[0]), jnp.where(last, turned[0], turned[1])]


def from_below(pair):
    turned = [pltpu.roll(v, 1, 1) for v in pair]
    first = lane_of(pair[0]) == 0
    return [jnp.where(first, turned[1], turned[0]), jnp.where(first, turned[0], turned[1])]


class Layer:
    def __init__(self, ref, index, padded=True):
        self.ref, self.index, self.pad = ref, index, PAD if padded else 0

    def read(self, half, row):
        return self.ref[self.index, half, pl.ds(self.pad + row, ROWS), :]

    def write(self, half, row, value):
        self.ref[self.index, half, pl.ds(self.pad + row, ROWS), :] = value

    def wrap(self):
        rows = self.ref.shape[2] - 2 * PAD
        for h in HALVES:
            self.ref[self.index, h, pl.ds(0, PAD), :] = self.ref[self.index, h, pl.ds(rows, PAD), :]
            self.ref[self.index, h, pl.ds(PAD + rows, PAD), :] = self.ref[self.index, h, pl.ds(PAD, PAD), :]


def copy_layer(source, target, rows):
    for r in range(0, rows, ROWS):
        for h in HALVES:
            target.write(h, r, source.read(h, r))


def fill(source, field, start, way, begin, end, padded):
    rows = field.shape[2] - 2 * PAD

    @pl.loop(begin, end)
    def _(k):
        target = Layer(field, start + way * k)
        copy_layer(Layer(source, k, padded), target, rows)
        target.wrap()


def normals(before, here, after, wall, row):
    centre = [here.read(h, row) for h in HALVES]
    n_x = [before.read(h, row) - after.read(h, row) for h in HALVES]
    n_y = [here.read(h, row - 1) - here.read(h, row + 1) for h in HALVES]
    above = from_above(centre)
    below = from_below(centre)
    lane = lane_of(centre[0])
    above[1] = jnp.where(lane == LANES - 1, centre[1], above[1])
    n_z = [below[h] - above[h] for h in HALVES]
    contact = wall[pl.ds(row, ROWS), :] * (jnp.abs(n_x[0]) + jnp.abs(n_y[0]))
    n_z[0] = jnp.where(lane == 0, contact, n_z[0])
    return centre, n_x, n_y, n_z


def soft(normal):
    return jnp.abs(normal) + 0.2


def own_index(odd, layer, count):
    return jnp.where(odd, OUTER + count - 1 - layer, layer - OUTER)


def natural(ref, index, half, row):
    return ref[index, pl.ds(row, ROWS), half * LANES : (half + 1) * LANES]


def begin_kernel(odd_ref, fraction_in, mask_in, *refs):
    speeds_in, (*speeds, peak, state, send_outer, send_inner, fraction, mask, sems) = refs[:3], refs[3:]
    odd = odd_ref[0] == 1
    count, rows, width = fraction.shape
    sources = (*speeds_in, fraction_in, mask_in)
    copies = [
        pltpu.make_async_copy(source, target, sems.at[n])
        for n, (source, target) in enumerate(zip(sources, (*speeds, fraction, mask)))
    ]
    for copy in copies:
        copy.start()
    best = jnp.zeros((8, width), jnp.float32)
    for n, ref in enumerate(speeds):
        copies[n].wait()
        for i in range(count):
            best = jnp.maximum(best, jnp.max(jnp.abs(ref[i]).reshape(rows // 8, 8, width), axis=0))
    peak[...] = jnp.maximum(best[:, :LANES], best[:, LANES:])
    copies[3].wait()
    copies[4].wait()
    for p in range(OUTER, OUTER + count):
        index = own_index(odd, p, count)
        to = [Layer(state, p - OUTER)]
        if p - OUTER < OUTER:
            to.append(Layer(send_outer, p - OUTER, False))
        if OUTER + count - 1 - p < INNER:
            to.append(Layer(send_inner, OUTER + count - 1 - p, False))
        for r in range(0, rows, ROWS):
            for h in HALVES:
                value = jnp.where(natural(mask, index, h, r) == 1, 1.0, natural(fraction, index, h, r))
                for target in to:
                    target.write(h, r, value)
        Layer(state, p - OUTER).wrap()
    first = speeds[0]
    for r in range(0, rows, ROWS):
        for h in HALVES:
            Layer(send_outer, OUTER, False).write(h, r, natural(first, count - 1, h, r))
            Layer(send_inner, INNER, False).write(h, r, natural(first, count - 1, h, r))


def wall_kernel(where_ref, cosine, out):
    odd = where_ref[0] == 1
    total = cosine.shape[0]
    layers = out.shape[0]
    count = layers - OUTER - INNER
    for p in range(1, layers - 1):
        row = lax.rem(where_ref[1] + own_index(odd, p, count) + total, total)
        out[p] = jnp.transpose(jnp.broadcast_to(cosine[pl.ds(row, 1), :], (LANES, cosine.shape[1])))


KEPT = 9


def prepare_kernel(odd_ref, *refs, kinds, faces, count):
    given = dict(zip(kinds, refs))
    wall = given["wall"]
    out, field, n_s, n_a, n_b = refs[len(kinds) :]
    rows = out.shape[2]
    odd = odd_ref[0] == 1
    sign = jnp.where(odd, -1.0, 1.0)
    start, stop = faces[0], faces[-1] + 1
    lowest, highest = start - 1, stop + 1
    for kind, first_layer, way, number, is_padded in (
        ("outer", OUTER - 1, -1, OUTER, False),
        ("own", OUTER, 1, count, True),
        ("inner", OUTER + count, 1, INNER, False),
    ):
        if kind not in given:
            continue
        used = [k for k in range(number) if lowest <= first_layer + way * k <= highest]
        if used:
            fill(given[kind], field, first_layer, way, used[0], used[-1] + 1, is_padded)

    @pl.loop(start, stop + 1)
    def _(i):
        for r in range(0, rows, ROWS):
            _, n_x, n_y, n_z = normals(Layer(field, i - 1), Layer(field, i), Layer(field, i + 1), wall.at[i], r)
            for h in HALVES:
                Layer(n_s, i, False).write(h, r, n_x[h])
                Layer(n_a, i, False).write(h, r, soft(n_y[h]))
                Layer(n_b, i, False).write(h, r, soft(n_z[h]))

    speed = KEPT - 1
    for k, face in enumerate(faces):
        for r in range(0, rows, ROWS):
            for h in HALVES:
                if face == OUTER - 1:
                    value = natural(given["first"], count - 1, h, r)
                    value = jnp.where(odd, value, Layer(given["outer"], OUTER, False).read(h, r))
                elif face == OUTER + count - 1:
                    value = natural(given["first"], count - 1, h, r)
                    value = jnp.where(odd, Layer(given["inner"], INNER, False).read(h, r), value)
                else:
                    value = natural(given["first"], jnp.where(odd, OUTER + count - 2 - face, face - OUTER), h, r)
                Layer(out, k * KEPT + speed, False).write(h, r, value * sign)

    @pl.loop(0, len(faces))
    def _(k):
        i = start + k
        for r in range(0, rows, ROWS):
            for h in HALVES:
                ahead = Layer(out, k * KEPT + speed, False).read(h, r) > 0.0

                def donor(ref, padded=False):
                    return jnp.where(ahead, Layer(ref, i, padded).read(h, r), Layer(ref, i + 1, padded).read(h, r))

                kept = prepare(donor(field, True), donor(n_s), donor(n_a), donor(n_b), ahead)
                for n, value in enumerate(kept):
                    Layer(out, k * KEPT + n, False).write(h, r, value)


def finish_faces(kept, step, flux, moved, start):
    rows = kept.shape[2]

    @pl.loop(0, kept.shape[0] // KEPT)
    def _(k):
        for r in range(0, rows, ROWS):
            for h in HALVES:
                values = [Layer(kept, k * KEPT + n, False).read(h, r) for n in range(KEPT)]
                values[-1] = values[-1] * step
                Layer(moved, start + k, False).write(h, r, values[-1])
                Layer(flux, start + k, False).write(h, r, finish(*values))


def update(target, here, inward, outward, rows):
    for r in range(0, rows, ROWS):
        for h in HALVES:
            target.write(h, r, jnp.clip(here.read(h, r) - outward.read(h, r) + inward.read(h, r), 0.0, 1.0))
    target.wrap()


def finish_kernel(peak, *refs, parts):
    kept, (state, out, moved, step_out, send_outer, send_inner, flux) = refs[:parts], refs[parts:]
    rows = moved.shape[2]
    largest = jnp.max(peak[...])
    step = CFL_NUMBER / (jnp.full((8, LANES), largest, jnp.float32) + 1e-6)
    step_out[...] = step
    start = 0
    for ref in kept:
        finish_faces(ref, step[:1, :], flux, moved, start)
        start += ref.shape[0] // KEPT

    @pl.loop(0, state.shape[0])
    def _(k):
        update(Layer(out, k), Layer(state, k), Layer(flux, k, False), Layer(flux, k + 1, False), rows)

    copy_layer(Layer(out, 0), Layer(send_outer, 0, False), rows)
    copy_layer(Layer(out, out.shape[0] - 1), Layer(send_inner, 0, False), rows)


def first_fluxes(field, wall, moved, n_s, n_a, n_b, flux, start, stop):
    rows = flux.shape[2]

    @pl.loop(start, stop + 1)
    def _(i):
        for r in range(0, rows, ROWS):
            _, n_x, n_y, n_z = normals(Layer(field, i - 1), Layer(field, i), Layer(field, i + 1), wall.at[i], r)
            for h in HALVES:
                Layer(n_s, i, False).write(h, r, n_x[h])
                Layer(n_a, i, False).write(h, r, soft(n_y[h]))
                Layer(n_b, i, False).write(h, r, soft(n_z[h]))

    @pl.loop(start, stop)
    def _(i):
        for r in range(0, rows, ROWS):
            for h in HALVES:
                speed = Layer(moved, i - 1, False).read(h, r)
                ahead = speed > 0.0

                def donor(ref, padded=False):
                    return jnp.where(ahead, Layer(ref, i, padded).read(h, r), Layer(ref, i + 1, padded).read(h, r))

                through = face_flux(donor(field, True), donor(n_s), donor(n_a), donor(n_b), speed)
                Layer(flux, i - 1, False).write(h, r, through)


def inside_kernel(edge, middle, last, inner, moved, wall, out, flux_out, send, field, n_s, n_a, n_b, flux):
    rows = moved.shape[2]
    count = middle.shape[0] + 2
    fill(edge, field, OUTER, 1, 0, 1, True)
    fill(middle, field, OUTER + 1, 1, 0, count - 2, True)
    fill(last, field, OUTER + count - 1, 1, 0, 1, True)
    fill(inner, field, OUTER + count, 1, 0, INNER, False)
    first_fluxes(field, wall, moved, n_s, n_a, n_b, flux, OUTER + 1, OUTER + count)
    copy_layer(Layer(flux, OUTER, False), Layer(flux_out, 0, False), rows)

    @pl.loop(OUTER + 2, OUTER + count)
    def _(i):
        update(Layer(out, i - OUTER - 2), Layer(field, i), Layer(flux, i - 2, False), Layer(flux, i - 1, False), rows)

    copy_layer(Layer(out, count - 3), Layer(send, 0, False), rows)


def outside_kernel(edge, middle, last, outer, moved, wall, flux_above, out, send, field, n_s, n_a, n_b, flux):
    rows = moved.shape[2]
    count = middle.shape[0] + 2
    fill(outer, field, OUTER - 1, -1, 0, OUTER, False)
    fill(edge, field, OUTER, 1, 0, 1, True)
    fill(middle, field, OUTER + 1, 1, 0, count - 2, True)
    if count < 4:
        fill(last, field, OUTER + count - 1, 1, 0, 1, True)
    first_fluxes(field, wall, moved, n_s, n_a, n_b, flux, OUTER - 1, OUTER + 1)
    edge_layer, next_layer = Layer(out, 0), Layer(out, 1)
    update(edge_layer, Layer(field, OUTER), Layer(flux, 0, False), Layer(flux, 1, False), rows)
    update(next_layer, Layer(field, OUTER + 1), Layer(flux, 1, False), Layer(flux_above, 0, False), rows)
    copy_layer(edge_layer, Layer(send, 0, False), rows)


def second_sweep(before, here, after, wall, speed, out, scratch):
    n_s, n_a, n_b, flux = scratch
    rows = out.ref.shape[2] - 2 * PAD
    for r in range(0, rows, ROWS):
        _, n_x, n_y, n_z = normals(before, here, after, wall, r)
        for h in HALVES:
            n_s.write(h, r, n_y[h])
            n_a.write(h, r, soft(n_x[h]))
            n_b.write(h, r, soft(n_z[h]))
    for s in (n_s, n_a, n_b):
        s.wrap()
    for r in range(0, rows, ROWS):
        for h in HALVES:
            moved = speed(h, r)
            ahead = moved > 0.0
            donor = [jnp.where(ahead, s.read(h, r), s.read(h, r + 1)) for s in (here, n_s, n_a, n_b)]
            flux.write(h, r, face_flux(*donor, moved))
    flux.wrap()
    for r in range(0, rows, ROWS):
        for h in HALVES:
            out.write(h, r, jnp.clip(here.read(h, r) - flux.read(h, r) + flux.read(h, r - 1), 0.0, 1.0))
    out.wrap()


def third_sweep(before, here, after, wall, speed, write, rows):
    for r in range(0, rows, ROWS):
        centre, n_x, n_y, n_z = normals(before, here, after, wall, r)
        fields = [centre, n_z, [soft(v) for v in n_x], [soft(v) for v in n_y]]
        above = [from_above(f) for f in fields]
        lane = lane_of(centre[0])
        through = []
        for h in HALVES:
            moved = speed(h, r)
            if h == 1:
                moved = jnp.where(lane == LANES - 1, 0.0, moved)
            ahead = moved > 0.0
            through.append(face_flux(*[jnp.where(ahead, f[h], a[h]) for f, a in zip(fields, above)], moved))
        below = from_below(through)
        for h in HALVES:
            value = jnp.clip(centre[h] - through[h] + below[h], 0.0, 1.0)
            write(h, r, value)


def gather_layers(refs, places):
    found = {}
    for ref, (start, padded) in zip(refs, places):
        for k in range(ref.shape[0]):
            found[start + k] = Layer(ref, k, padded)
    return found


def second_kernel(odd_ref, step, speed_ref, wall, *refs, places, work, send_last):
    fields, rest = refs[: len(places)], refs[len(places) :]
    out, rest = rest[0], rest[1:]
    send, rest = (rest[0], rest[1:]) if send_last is not None else (None, rest)
    scratch = [Layer(ref, 0) for ref in rest]
    layers = gather_layers(fields, places)
    odd = odd_ref[0] == 1
    count, rows, _ = speed_ref.shape
    for k, p in enumerate(work):
        index = own_index(odd, p, count)
        second_sweep(
            layers[p - 1],
            layers[p],
            layers[p + 1],
            wall.at[p],
            lambda h, r: natural(speed_ref, index, h, r) * step[:1, :],
            Layer(out, k),
            scratch,
        )
    if send is not None:
        copy_layer(Layer(out, work.index(send_last)), Layer(send, 0, False), rows)


def third_kernel(odd_ref, step, speed_ref, wall, *refs, places, work):
    fields, (out,) = refs[: len(places)], refs[len(places) :]
    layers = gather_layers(fields, places)
    odd = odd_ref[0] == 1
    count, rows, _ = speed_ref.shape
    for k, p in enumerate(work):
        index = own_index(odd, p, count)
        third_sweep(
            layers[p - 1],
            layers[p],
            layers[p + 1],
            wall.at[p],
            lambda h, r: natural(speed_ref, index, h, r) * step[:1, :],
            Layer(out, k).write,
            rows,
        )
        Layer(out, k).wrap()


def last_kernel(odd_ref, step, speed_ref, wall, *refs, places):
    fields, rest = refs[: len(places)], refs[len(places) :]
    done, (out, held_out, sems) = rest[:-3], rest[-3:]
    layers = gather_layers(fields, places)
    odd = odd_ref[0] == 1
    count, rows, _ = speed_ref.shape
    copies = []

    def send(source, layer, h):
        target = out.at[own_index(odd, layer, count), :, h * LANES : (h + 1) * LANES]
        copies.append(pltpu.make_async_copy(source, target, sems.at[len(copies)]))
        copies[-1].start()

    p = OUTER + 1
    for ref in done:
        for k in range(ref.shape[0]):
            for h in HALVES:
                send(ref.at[k, h, pl.ds(PAD, rows), :], p, h)
            p += 1

    def write(h, r, value):
        held_out[h, pl.ds(r, ROWS), :] = value

    index = own_index(odd, OUTER, count)
    third_sweep(
        layers[OUTER - 1],
        layers[OUTER],
        layers[OUTER + 1],
        wall.at[OUTER],
        lambda h, r: natural(speed_ref, index, h, r) * step[:1, :],
        write,
        rows,
    )
    for h in HALVES:
        send(held_out.at[h], OUTER, h)
    for copy in copies:
        copy.wait()


IN_VMEM = pl.BlockSpec(memory_space=pltpu.VMEM)
IN_SMEM = pl.BlockSpec(memory_space=pltpu.SMEM)


def held(shape):
    return pltpu.VMEM(shape, jnp.float32)


def call(kernel, name, outs, scalars, arrays, scratch=(), faces=0.1, resident=True):
    space = pltpu.VMEM if resident else pltpu.HBM
    arrays = [pltpu.with_memory_space_constraint(a, space) for a in arrays]
    work = int(faces * 1.1e9)
    return pl.pallas_call(
        kernel,
        out_shape=outs,
        in_specs=[IN_SMEM] * len(scalars) + [pl.BlockSpec(memory_space=space)] * len(arrays),
        out_specs=[IN_VMEM] * len(outs),
        scratch_shapes=list(scratch),
        compiler_params=pltpu.CompilerParams(vmem_limit_bytes=VMEM_LIMIT),
        cost_estimate=pl.CostEstimate(flops=work, bytes_accessed=1024, transcendentals=0),
        name=name,
    )(*scalars, *arrays)


def swap(array, outer):
    count = lax.axis_size("gx")
    if outer:
        pairs = [(i, (i + 1) % count if i % 2 else (i - 1) % count) for i in range(count)]
    else:
        pairs = [(i, i ^ 1) for i in range(count)]
    return lax.ppermute(array, "gx", pairs)


def largest_round(array, reach, beside):
    count = lax.axis_size("gx")
    if count & (count - 1) == 0:
        pairs = [(i, i ^ reach) for i in range(count)]
    else:
        pairs = [(i, (i + reach) % count) for i in range(count)]
    received = lax.ppermute(array, "gx", pairs)
    if beside:
        received, *_ = lax.optimization_barrier((received, *beside))
    return jnp.maximum(array, received)


def shards(fraction, first, second, third, wall_class, seed_mask):
    count, rows, width = fraction.shape
    layers = OUTER + count + INNER
    own_end = OUTER + count
    device = lax.axis_index("gx")
    odd = (device % 2).astype(jnp.int32).reshape(1)
    place = jnp.stack([device % 2, device * count]).astype(jnp.int32)

    def padded(n):
        return (n, 2, rows + 2 * PAD, LANES)

    def plain(n):
        return (n, 2, rows, LANES)

    natural_shape = (count, rows, width)
    first, second, third, peak, state, send_outer, send_inner = call(
        begin_kernel,
        "begin",
        [held(natural_shape)] * 3
        + [held((8, LANES)), held(padded(count)), held(plain(OUTER + 1)), held(plain(INNER + 1))],
        [odd],
        [fraction, seed_mask, first, second, third],
        [
            pltpu.VMEM(natural_shape, jnp.float32),
            pltpu.VMEM(natural_shape, jnp.int32),
            pltpu.SemaphoreType.DMA((5,)),
        ],
        resident=False,
    )
    inner = swap(send_inner, False)
    cosine = jnp.cos(jnp.pi * (wall_class.astype(jnp.float32) + 1.0) / (WALL_CLASSES + 1))
    (wall,) = call(wall_kernel, "wall", [held((layers, rows, LANES))], [place], [cosine])
    slopes = [pltpu.VMEM(padded(layers), jnp.float32)] + [pltpu.VMEM(plain(layers), jnp.float32)] * 3

    def prepare_call(faces, **given):
        return call(
            functools.partial(prepare_kernel, kinds=tuple(given), faces=faces, count=count),
            "prepare",
            [held(plain(KEPT * len(faces)))],
            [odd],
            list(given.values()),
            slopes,
            faces=len(faces),
        )[0]

    size = lax.axis_size("gx")
    prepare_inside = functools.partial(prepare_call, wall=wall, first=first, own=state, inner=inner)
    peak = largest_round(peak, 1, [])
    kept = [prepare_inside(tuple(range(OUTER + 2, own_end)))]
    if size > 2:
        peak = largest_round(peak, 2, kept)
    peak, send_outer = lax.optimization_barrier((peak, send_outer))
    outer = swap(send_outer, True)
    kept.insert(0, prepare_inside((OUTER + 1,)))
    kept.insert(0, prepare_call((OUTER - 1, OUTER), wall=wall, first=first, own=state, outer=outer))
    reach, beside = 4, [[kept[1]]]
    while reach < size:
        peak = largest_round(peak, reach, beside.pop() if beside else [])
        reach *= 2
    own, moved, step, send_outer, send_inner = call(
        functools.partial(finish_kernel, parts=len(kept)),
        "finish",
        [held(padded(count)), held(plain(count + 1)), held((8, LANES)), held(plain(1)), held(plain(1))],
        [],
        [peak, *kept, state],
        [pltpu.VMEM(plain(count + 1), jnp.float32)],
        faces=1,
    )
    swept, places = [own], [(OUTER, True)]
    line = [pltpu.VMEM(padded(1), jnp.float32)] * 4
    for turn in range(STEPS):
        final = turn == STEPS - 1
        if turn > 0:
            flux = pltpu.VMEM(plain(count + 1), jnp.float32)
            inside, flux_low, send_inner = call(
                inside_kernel,
                "inside",
                [held(padded(count - 2)), held(plain(1)), held(plain(1))],
                [],
                [*own, inner, moved, wall],
                [*slopes, flux],
                faces=count - 1,
            )
            outside, send_outer = call(
                outside_kernel,
                "outside",
                [held(padded(2)), held(plain(1))],
                [],
                [*own, outer, moved, wall, flux_low],
                [*slopes, flux],
                faces=2,
            )
            swept, places = [outside, inside], [(OUTER, True), (OUTER + 2, True)]
        inner = swap(send_inner, False)
        outer = swap(send_outer, True)

        def second_call(work, fields, places, send):
            return call(
                functools.partial(second_kernel, places=places, work=work, send_last=work[0] if send else None),
                "second",
                [held(padded(len(work)))] + ([held(plain(1))] if send else []),
                [odd],
                [step, second, wall, *fields],
                line,
                faces=len(work),
            )

        last, send_inner = second_call((own_end - 1,), [swept[-1], inner], [places[-1], (own_end, False)], True)
        inner = swap(send_inner, False)
        (middle,) = second_call(tuple(range(OUTER + 1, own_end - 1)), swept, places, False)
        edge, send_outer = second_call((OUTER,), [outer, swept[0]], [(OUTER - 1, False), places[0]], True)
        outer = swap(send_outer, True)

        fields = [edge, middle, last, inner]
        starts = [(OUTER, True), (OUTER + 1, True), (own_end - 1, True), (own_end, False)]
        inside_work = tuple(range(OUTER + 1, own_end))
        edge_fields, edge_starts = [outer, edge, middle], [(OUTER - 1, False), (OUTER, True), (OUTER + 1, True)]
        def third_call(work, fields, places):
            return call(
                functools.partial(third_kernel, places=places, work=work),
                "third",
                [held(padded(len(work)))],
                [odd],
                [step, third, wall, *fields],
                faces=len(work),
            )[0]

        middle_new = third_call(inside_work[:-1], fields[:-1], starts[:-1])
        last_new = third_call(inside_work[-1:], fields[1:], starts[1:])
        if final:
            return last_call(odd, step, third, wall, edge_fields, edge_starts, [middle_new, last_new], natural_shape)
        edge_new = third_call((OUTER,), edge_fields, edge_starts)
        own = [edge_new, middle_new, last_new]
        send_outer, send_inner = call(pack_kernel, "pack", [held(plain(OUTER)), held(plain(INNER))], [], own)
        outer = swap(send_outer, True)
        inner = swap(send_inner, False)


def last_call(odd, step, speed, wall, fields, places, done, shape):
    arrays = [pltpu.with_memory_space_constraint(a, pltpu.VMEM) for a in (step, speed, wall, *fields, *done)]
    return pl.pallas_call(
        functools.partial(last_kernel, places=places),
        out_shape=jax.ShapeDtypeStruct(shape, jnp.float32),
        in_specs=[IN_SMEM] + [IN_VMEM] * len(arrays),
        out_specs=pl.BlockSpec(memory_space=pltpu.HBM),
        scratch_shapes=[pltpu.VMEM((2, *shape[1:2], LANES), jnp.float32), pltpu.SemaphoreType.DMA((2 * shape[0],))],
        compiler_params=pltpu.CompilerParams(vmem_limit_bytes=VMEM_LIMIT),
        cost_estimate=pl.CostEstimate(flops=int(1.1e9), bytes_accessed=1024, transcendentals=0),
        name="last",
    )(odd, *arrays)


def pack_kernel(edge, middle, last, send_outer, send_inner):
    rows = send_outer.shape[2]
    own = [Layer(ref, k) for ref in (edge, middle, last) for k in range(ref.shape[0])]
    for k in range(OUTER):
        copy_layer(own[k], Layer(send_outer, k, False), rows)
    for k in range(INNER):
        copy_layer(own[-1 - k], Layer(send_inner, k, False), rows)


def solution(mesh):
    split = P(("ens", "gx"), None, None)
    return jax.shard_map(
        shards, mesh=mesh, in_specs=(split, split, split, split, P(), split), out_specs=split, check_vma=False
    )
```

time: 81.3 us -> 70.2 us (0.86)
  waiting for transfers between devices: 25.4 us -> 18.6 us
  local copies, waits for them, and re-layouts: 3.14 us -> 0.01 us
  starting transfers between devices: 19.8 us -> 18.9 us
    ppermute x4, waiting for transfers between devices: 15.7 us -> 7.65 us  [largest_round(): received = lax.ppermute(array, 'gx', pairs)]
    unnamed x14 -> x2, local copies, waits for them, and re-layouts: 3.14 us -> 0.01 us
    pallas_call x20, Pallas kernels: 32.3 us -> 30.2 us  [call(): pl.pallas_call(kernel, out_shape=outs, in_specs=[IN_SMEM] * len(scalars)...]
    pallas_call x0 -> x1, Pallas kernels: none -> 1.88 us  [last_call(): pl.pallas_call(functools.partial(last_kernel, places=places), out_shape=j...]
    ppermute x10 -> x12, waiting for transfers between devices: 9.64 us -> 10.9 us  [swap(): return lax.ppermute(array, 'gx', pairs)]
    ppermute x10 -> x12, starting transfers between devices: 15.1 us -> 14.3 us  [swap(): return lax.ppermute(array, 'gx', pairs)]
  transfers between devices with their start and end apart: 14 -> 16, of which waited for: 8 -> 8; matrix products, arithmetic and copies ran while one was open for 0% -> 0% of each run, Pallas kernels for 19% -> 31%
where the time goes in v2:
time: 70.2 us; the launch traced here: 70.1 us
  Pallas kernels  32.1 us (46%)
  starting transfers between devices  18.9 us (27%)
  waiting for transfers between devices  18.6 us (26%)
    pallas_call x20, Pallas kernels, call(): pl.pallas_call(kernel, out_shape=outs, in_specs=[IN_SMEM] * len(scalars)...  30.2 us
    ppermute x12, starting transfers between devices, swap(): return lax.ppermute(array, 'gx', pairs)  14.3 us
    ppermute x12, waiting for transfers between devices, swap(): return lax.ppermute(array, 'gx', pairs)  10.9 us
    ppermute x4, waiting for transfers between devices, largest_round(): received = lax.ppermute(array, 'gx', pairs)  7.65 us
    ppermute x4, starting transfers between devices, largest_round(): received = lax.ppermute(array, 'gx', pairs)  4.53 us
    pallas_call x1, Pallas kernels, last_call(): pl.pallas_call(functools.partial(last_kernel, places=places), out_shape=j...  1.88 us
  transfers between devices with their start and end apart: 16, of which 8 were waited for; matrix products, arithmetic and copies ran while one was open for 0% of the time, Pallas kernels for 31%

profile of v2, /device:TPU:0, one launch (start us, length us, event | category | flops | bytes accessed | tf_op | source)
XLA Modules:
  0.0 70.1 jit_solution(4896121650481583442)
XLA Ops:
  0.0 1.8 %begin.1 = (f32[4,128,256]{2,1,0:T(8,128)S(1)}, f32[4,128,256]{2,1,0:T(8,128)S(1)}, f32[4,128,256]{2,1,0:T(8,128)S(1)}, f32[8,128]{1,0:T(8,128)S(1)}, f32[4,2,14...) custom-call(s32[1]{0:T(128)} %bitcast.odd_ref, f32[4,128,256]{2,1,0:T(8,128)} %fraction_in.1, ...), custom_call_target="tpu_custom_call" | custom-call | flops 110000000 | bytes 1024 | tf_op jit(solution)/shard_map/begin/pallas_call | solution.py:525
  1.8 0.5 collective-permute-start.2
  2.3 0.1 collective-permute-start
  2.4 0.1 pad_add_fusion.where_ref
  2.5 0.1 multiply_cosine_fusion.cosine
  2.6 0.7 %wall.1.refs_0_ = f32[8,128,128]{2,1,0:T(8,128)S(1)} custom-call(s32[2]{0:T(128)S(1)} %pad_add_fusion.where_ref, f32[64,128]{1,0:T(8,128)S(1)} %multiply_cosine_fusion.cosine), custom_call_target="tpu_custom_call" | custom-call | flops 110000000 | bytes 1024 | tf_op jit(solution)/shard_map/wall/pallas_call | solution.py:525
  3.3 0.4 collective-permute-done
  3.7 2.9 %collective-permute-start.1 = (f32[8,128]{1,0:T(8,128)S(1)}, f32[8,128]{1,0:T(8,128)S(1)}, u32[]{:S(2)}, u32[]{:S(2)}) collective-permute-start(f32[8,128]{1,0:T(8,128)S(1)} %max.12), channel_id=1, source_target_pairs={{0,2},{1,3},{2,0},{3,1},{4,6},{5,7},{6,4},{7,5},{8,10},{9,11},{10,... | collective-permute-start | bytes 12296 | tf_op jit(solution)/shard_map/ppermute | solution.py:552
  6.6 1.9 %prepare.3.refs_2_ = f32[18,2,128,128]{3,2,1,0:T(8,128)S(1)} custom-call(s32[1]{0:T(128)} %bitcast.odd_ref, f32[8,128,128]{2,1,0:T(8,128)S(1)} %wall.1.refs_0_, f32[4,128,256]{2,1,0:T(8,128)S(1)} %get-tuple-element.37.refs_1_, f32[4,2,144,128]{3,2,1,0:T(8,128)S(1)} %get-tuple-element.38.refs_2_.refs_3_, f32[3,2,128,128]{3,2,1,0:T(8,128)S(1)} %collective-permute-done.2.refs_3_), custom_call_target="tpu_custom_call" | custom-call | flops 2200000000 | bytes 1024 | tf_op jit(solution)/shard_map/prepare/pallas_call | solution.py:525
  8.5 0.0 collective-permute-done.1
  8.5 3.3 %collective-permute-start.5 = (f32[3,2,128,128]{3,2,1,0:T(8,128)S(1)}, f32[3,2,128,128]{3,2,1,0:T(8,128)S(1)}, u32[]{:S(2)}, u32[]{:S(2)}) collective-permute-start(f32[3,2,128,128]{3,2,1,0:T(8,128)S(1)} %get-tuple-element.44), channel_id=1, source_target_pairs={{0,15},{1,2},{2,1},{3,4},{4,3},{5,6},{6,5},{7,8},{8,7},{9,10},{10,... | collective-permute-start | bytes 1179656 | tf_op jit(solution)/shard_map/ppermute | solution.py:543
  11.8 0.0 collective-permute-start.3
  11.8 1.0 %prepare.4.refs_1_ = f32[9,2,128,128]{3,2,1,0:T(8,128)S(1)} custom-call(s32[1]{0:T(128)} %bitcast.odd_ref, f32[8,128,128]{2,1,0:T(8,128)S(1)} %wall.1.refs_0_, f32[4,128,256]{2,1,0:T(8,128)S(1)} %get-tuple-element.37.refs_1_, f32[4,2,144,128]{3,2,1,0:T(8,128)S(1)} %get-tuple-element.38.refs_2_.refs_3_, f32[3,2,128,128]{3,2,1,0:T(8,128)S(1)} %collective-permute-done.2.refs_3_), custom_call_target="tpu_custom_call" | custom-call | flops 1100000000 | bytes 1024 | tf_op jit(solution)/shard_map/prepare/pallas_call | solution.py:525
  12.9 4.3 %collective-permute-done.3 = f32[8,128]{1,0:T(8,128)S(1)} collective-permute-done((f32[8,128]{1,0:T(8,128)S(1)}, f32[8,128]{1,0:T(8,128)S(1)}, u32[]{:S(2)}, u32[]{:S(2)}) %collective-permute-start.3) | collective-permute-done | bytes 4128 | tf_op jit(solution)/shard_map/ppermute | solution.py:552
  17.2 1.6 %collective-permute-start.4 = (f32[8,128]{1,0:T(8,128)S(1)}, f32[8,128]{1,0:T(8,128)S(1)}, u32[]{:S(2)}, u32[]{:S(2)}) collective-permute-start(f32[8,128]{1,0:T(8,128)S(1)} %max.14), channel_id=1, source_target_pairs={{0,8},{1,9},{2,10},{3,11},{4,12},{5,13},{6,14},{7,15},{8,0},{9,1},... | collective-permute-start | bytes 12296 | tf_op jit(solution)/shard_map/ppermute | solution.py:552
  18.8 2.9 %collective-permute-done.4 = f32[8,128]{1,0:T(8,128)S(1)} collective-permute-done((f32[8,128]{1,0:T(8,128)S(1)}, f32[8,128]{1,0:T(8,128)S(1)}, u32[]{:S(2)}, u32[]{:S(2)}) %collective-permute-start.4) | collective-permute-done | bytes 4128 | tf_op jit(solution)/shard_map/ppermute | solution.py:552
  21.7 1.9 %prepare.5.refs_0_ = f32[18,2,128,128]{3,2,1,0:T(8,128)S(1)} custom-call(s32[1]{0:T(128)} %bitcast.odd_ref, f32[8,128,128]{2,1,0:T(8,128)S(1)} %wall.1.refs_0_, f32[4,128,256]{2,1,0:T(8,128)S(1)} %get-tuple-element.37.refs_1_, f32[4,2,144,128]{3,2,1,0:T(8,128)S(1)} %get-tuple-element.38.refs_2_.refs_3_, f32[3,2,128,128]{3,2,1,0:T(8,128)S(1)} %collective-permute-done.5.refs_3_), custom_call_target="tpu_custom_call" | custom-call | flops 2200000000 | bytes 1024 | tf_op jit(solution)/shard_map/prepare/pallas_call | solution.py:525
  23.6 1.3 %finish.1 = (f32[4,2,144,128]{3,2,1,0:T(8,128)S(1)}, f32[5,2,128,128]{3,2,1,0:T(8,128)S(1)}, f32[8,128]{1,0:T(8,128)S(1)}, f32[1,2,128,128]{3,2,1,0:T(8,128)S(1)}, f32[1,2,128,128]{3,2,1,0:T(8,128)S(1)}) custom-call(f32[8,128]{1,0:T(8,128)S(1)} %max.15.peak, f32[18,2,128,128]{3,2,1,0:T(8,128)S(1)} %prepare.5.refs_0_, f32[9,2,128,128]{3,2,1,0:T(8,128)S(1)} %prepare.4.refs_1_, ...), custom_call_target="tpu_custom_call" | custom-call | flops 1100000000 | bytes 1024 | tf_op jit(solution)/shard_map/finish/pallas_call | solution.py:525
  24.9 1.9 %collective-permute-start.6 = (f32[1,2,128,128]{3,2,1,0:T(8,128)S(1)}, f32[1,2,128,128]{3,2,1,0:T(8,128)S(1)}, u32[]{:S(2)}, u32[]{:S(2)}) collective-permute-start(f32[1,2,128,128]{3,2,1,0:T(8,128)S(1)} %get-tuple-element.48), channel_id=1, source_target_pairs={{0,15},{1,2},{2,1},{3,4},{4,3},{5,6},{6,5},{7,8},{8,7},{9,10},{10,... | collective-permute-start | bytes 393224 | tf_op jit(solution)/shard_map/ppermute | solution.py:543
  26.8 0.0 collective-permute-start.8
  26.8 2.0 %second.7.refs_2_.refs_1_.refs_0_ = f32[2,2,144,128]{3,2,1,0:T(8,128)S(1)} custom-call(s32[1]{0:T(128)} %bitcast.odd_ref, f32[8,128]{1,0:T(8,128)S(1)} %get-tuple-element.45.step, f32[4,128,256]{2,1,0:T(8,128)S(1)} %get-tuple-element.47.speed_ref, f32[8,128,128]{2,1,0:T(8,128)S(1)} %wall.1.refs_0_, f32[4,2,144,128]{3,2,1,0:T(8,128)S(1)} %get-tuple-element.49.refs_1_.refs_0_), custom_call_target="tpu_custom_call" | custom-call | flops 2200000000 | bytes 1024 | tf_op jit(solution)/shard_map/second/pallas_call | solution.py:525
  28.8 1.0 %second.8 = (f32[1,2,144,128]{3,2,1,0:T(8,128)S(1)}, f32[1,2,128,128]{3,2,1,0:T(8,128)S(1)}) custom-call(s32[1]{0:T(128)} %bitcast.odd_ref, f32[8,128]{1,0:T(8,128)S(1)} %get-tuple-element.45.step, f32[4,128,256]{2,1,0:T(8,128)S(1)} %get-tuple-element.47.speed_ref, f32[8,128,128]{2,1,0:T(8,128)S(1)} %wall.1.refs_0_, ...), custom_call_target="tpu_custom_call" | custom-call | flops 1100000000 | bytes 1024 | tf_op jit(solution)/shard_map/second/pallas_call | solution.py:525
  29.8 0.6 collective-permute-start.9
  30.4 1.7 %collective-permute-done.6.refs_0_ = f32[1,2,128,128]{3,2,1,0:T(8,128)S(1)} collective-permute-done((f32[1,2,128,128]{3,2,1,0:T(8,128)S(1)}, f32[1,2,128,128]{3,2,1,0:T(8,128)S(1)}, u32[]{:S(2)}, u32[]{:S(2)}) %collective-permute-start.6) | collective-permute-done | bytes 131104 | tf_op jit(solution)/shard_map/ppermute | solution.py:543
  32.1 1.0 %second.6 = (f32[1,2,144,128]{3,2,1,0:T(8,128)S(1)}, f32[1,2,128,128]{3,2,1,0:T(8,128)S(1)}) custom-call(s32[1]{0:T(128)} %bitcast.odd_ref, f32[8,128]{1,0:T(8,128)S(1)} %get-tuple-element.45.step, f32[4,128,256]{2,1,0:T(8,128)S(1)} %get-tuple-element.47.speed_ref, f32[8,128,128]{2,1,0:T(8,128)S(1)} %wall.1.refs_0_, ...), custom_call_target="tpu_custom_call" | custom-call | flops 1100000000 | bytes 1024 | tf_op jit(solution)/shard_map/second/pallas_call | solution.py:525
  33.1 1.9 %collective-permute-start.7 = (f32[1,2,128,128]{3,2,1,0:T(8,128)S(1)}, f32[1,2,128,128]{3,2,1,0:T(8,128)S(1)}, u32[]{:S(2)}, u32[]{:S(2)}) collective-permute-start(f32[1,2,128,128]{3,2,1,0:T(8,128)S(1)} %get-tuple-element.50), channel_id=1, source_target_pairs={{0,15},{1,2},{2,1},{3,4},{4,3},{5,6},{6,5},{7,8},{8,7},{9,10},{10,... | collective-permute-start | bytes 393224 | tf_op jit(solution)/shard_map/ppermute | solution.py:543
  35.0 2.2 %third.6.middle = f32[2,2,144,128]{3,2,1,0:T(8,128)S(1)} custom-call(s32[1]{0:T(128)} %bitcast.odd_ref, f32[8,128]{1,0:T(8,128)S(1)} %get-tuple-element.45.step, f32[4,128,256]{2,1,0:T(8,128)S(1)} %get-tuple-element.46.speed_ref, f32[8,128,128]{2,1,0:T(8,128)S(1)} %wall.1.refs_0_, f32[1,2,144,128]{3,2,1,0:T(8,128)S(1)} %get-tuple-element.51.refs_1_.refs_0_, ...), custom_call_target="tpu_custom_call" | custom-call | flops 2200000000 | bytes 1024 | tf_op jit(solution)/shard_map/third/pallas_call | solution.py:525
  37.2 0.0 collective-permute-done.9.refs_2_
  37.2 1.1 %third.7.last = f32[1,2,144,128]{3,2,1,0:T(8,128)S(1)} custom-call(s32[1]{0:T(128)} %bitcast.odd_ref, f32[8,128]{1,0:T(8,128)S(1)} %get-tuple-element.45.step, f32[4,128,256]{2,1,0:T(8,128)S(1)} %get-tuple-element.46.speed_ref, f32[8,128,128]{2,1,0:T(8,128)S(1)} %wall.1.refs_0_, f32[2,2,144,128]{3,2,1,0:T(8,128)S(1)} %second.7.refs_2_.refs_1_.refs_0_, ...), custom_call_target="tpu_custom_call" | custom-call | flops 1100000000 | bytes 1024 | tf_op jit(solution)/shard_map/third/pallas_call | solution.py:525
  38.3 1.9 %collective-permute-done.7.refs_0_ = f32[1,2,128,128]{3,2,1,0:T(8,128)S(1)} collective-permute-done((f32[1,2,128,128]{3,2,1,0:T(8,128)S(1)}, f32[1,2,128,128]{3,2,1,0:T(8,128)S(1)}, u32[]{:S(2)}, u32[]{:S(2)}) %collective-permute-start.7) | collective-permute-done | bytes 131104 | tf_op jit(solution)/shard_map/ppermute | solution.py:543
  40.3 1.1 %third.5.edge = f32[1,2,144,128]{3,2,1,0:T(8,128)S(1)} custom-call(s32[1]{0:T(128)} %bitcast.odd_ref, f32[8,128]{1,0:T(8,128)S(1)} %get-tuple-element.45.step, f32[4,128,256]{2,1,0:T(8,128)S(1)} %get-tuple-element.46.speed_ref, f32[8,128,128]{2,1,0:T(8,128)S(1)} %wall.1.refs_0_, f32[1,2,128,128]{3,2,1,0:T(8,128)S(1)} %collective-permute-done.7.refs_0_, ...), custom_call_target="tpu_custom_call" | custom-call | flops 1100000000 | bytes 1024 | tf_op jit(solution)/shard_map/third/pallas_call | solution.py:525
  41.4 0.1 collective-permute-start.11
  41.5 1.9 %collective-permute-start.10 = (f32[2,2,128,128]{3,2,1,0:T(8,128)S(1)}, f32[2,2,128,128]{3,2,1,0:T(8,128)S(1)}, u32[]{:S(2)}, u32[]{:S(2)}) collective-permute-start(f32[2,2,128,128]{3,2,1,0:T(8,128)S(1)} %get-tuple-element.55), channel_id=1, source_target_pairs={{0,15},{1,2},{2,1},{3,4},{4,3},{5,6},{6,5},{7,8},{8,7},{9,10},{10,... | collective-permute-start | bytes 786440 | tf_op jit(solution)/shard_map/ppermute | solution.py:543
  43.4 3.3 %inside.1 = (f32[2,2,144,128]{3,2,1,0:T(8,128)S(1)}, f32[1,2,128,128]{3,2,1,0:T(8,128)S(1)}, f32[1,2,128,128]{3,2,1,0:T(8,128)S(1)}) custom-call(f32[1,2,144,128]{3,2,1,0:T(8,128)S(1)} %third.5.edge, f32[2,2,144,128]{3,2,1,0:T(8,128)S(1)} %third.6.middle, f32[1,2,144,128]{3,2,1,0:T(8,128)S(1)} %third.7.last, ...), custom_call_target="tpu_custom_call" | custom-call | flops 3300000000 | bytes 1024 | tf_op jit(solution)/shard_map/inside/pallas_call | solution.py:525
  46.7 3.5 %collective-permute-done.10.outer = f32[2,2,128,128]{3,2,1,0:T(8,128)S(1)} collective-permute-done((f32[2,2,128,128]{3,2,1,0:T(8,128)S(1)}, f32[2,2,128,128]{3,2,1,0:T(8,128)S(1)}, u32[]{:S(2)}, u32[]{:S(2)}) %collective-permute-start.10) | collective-permute-done | bytes 262176 | tf_op jit(solution)/shard_map/ppermute | solution.py:543
  50.2 2.5 %outside.1 = (f32[2,2,144,128]{3,2,1,0:T(8,128)S(1)}, f32[1,2,128,128]{3,2,1,0:T(8,128)S(1)}) custom-call(f32[1,2,144,128]{3,2,1,0:T(8,128)S(1)} %third.5.edge, f32[2,2,144,128]{3,2,1,0:T(8,128)S(1)} %third.6.middle, f32[1,2,144,128]{3,2,1,0:T(8,128)S(1)} %third.7.last, f32[2,2,128,128]{3,2,1,0:T(8,128)S(1)} %collective-permute-done.10.outer, ...), custom_call_target="tpu_custom_call" | custom-call | flops 2200000000 | bytes 1024 | tf_op jit(solution)/shard_map/outside/pallas_call | solution.py:525
  52.6 1.8 %collective-permute-start.12 = (f32[1,2,128,128]{3,2,1,0:T(8,128)S(1)}, f32[1,2,128,128]{3,2,1,0:T(8,128)S(1)}, u32[]{:S(2)}, u32[]{:S(2)}) collective-permute-start(f32[1,2,128,128]{3,2,1,0:T(8,128)S(1)} %get-tuple-element.59), channel_id=1, source_target_pairs={{0,15},{1,2},{2,1},{3,4},{4,3},{5,6},{6,5},{7,8},{8,7},{9,10},{10,... | collective-permute-start | bytes 393224 | tf_op jit(solution)/shard_map/ppermute | solution.py:543
  54.4 2.0 %second.10.refs_1_.refs_0_.refs_2_ = f32[2,2,144,128]{3,2,1,0:T(8,128)S(1)} custom-call(s32[1]{0:T(128)} %bitcast.odd_ref, f32[8,128]{1,0:T(8,128)S(1)} %get-tuple-element.45.step, f32[4,128,256]{2,1,0:T(8,128)S(1)} %get-tuple-element.47.speed_ref, f32[8,128,128]{2,1,0:T(8,128)S(1)} %wall.1.refs_0_, ...), custom_call_target="tpu_custom_call" | custom-call | flops 2200000000 | bytes 1024 | tf_op jit(solution)/shard_map/second/pallas_call | solution.py:525
  56.4 1.0 %second.11 = (f32[1,2,144,128]{3,2,1,0:T(8,128)S(1)}, f32[1,2,128,128]{3,2,1,0:T(8,128)S(1)}) custom-call(s32[1]{0:T(128)} %bitcast.odd_ref, f32[8,128]{1,0:T(8,128)S(1)} %get-tuple-element.45.step, f32[4,128,256]{2,1,0:T(8,128)S(1)} %get-tuple-element.47.speed_ref, f32[8,128,128]{2,1,0:T(8,128)S(1)} %wall.1.refs_0_, ...), custom_call_target="tpu_custom_call" | custom-call | flops 1100000000 | bytes 1024 | tf_op jit(solution)/shard_map/second/pallas_call | solution.py:525
  57.4 0.6 collective-permute-start.15
  58.0 1.8 %collective-permute-done.12.refs_0_ = f32[1,2,128,128]{3,2,1,0:T(8,128)S(1)} collective-permute-done((f32[1,2,128,128]{3,2,1,0:T(8,128)S(1)}, f32[1,2,128,128]{3,2,1,0:T(8,128)S(1)}, u32[]{:S(2)}, u32[]{:S(2)}) %collective-permute-start.12) | collective-permute-done | bytes 131104 | tf_op jit(solution)/shard_map/ppermute | solution.py:543
  59.8 1.0 %second.9 = (f32[1,2,144,128]{3,2,1,0:T(8,128)S(1)}, f32[1,2,128,128]{3,2,1,0:T(8,128)S(1)}) custom-call(s32[1]{0:T(128)} %bitcast.odd_ref, f32[8,128]{1,0:T(8,128)S(1)} %get-tuple-element.45.step, f32[4,128,256]{2,1,0:T(8,128)S(1)} %get-tuple-element.47.speed_ref, f32[8,128,128]{2,1,0:T(8,128)S(1)} %wall.1.refs_0_, ...), custom_call_target="tpu_custom_call" | custom-call | flops 1100000000 | bytes 1024 | tf_op jit(solution)/shard_map/second/pallas_call | solution.py:525
  60.8 1.8 %collective-permute-start.13 = (f32[1,2,128,128]{3,2,1,0:T(8,128)S(1)}, f32[1,2,128,128]{3,2,1,0:T(8,128)S(1)}, u32[]{:S(2)}, u32[]{:S(2)}) collective-permute-start(f32[1,2,128,128]{3,2,1,0:T(8,128)S(1)} %get-tuple-element.61), channel_id=1, source_target_pairs={{0,15},{1,2},{2,1},{3,4},{4,3},{5,6},{6,5},{7,8},{8,7},{9,10},{10,... | collective-permute-start | bytes 393224 | tf_op jit(solution)/shard_map/ppermute | solution.py:543
  62.6 2.2 %third.8.refs_3_ = f32[2,2,144,128]{3,2,1,0:T(8,128)S(1)} custom-call(s32[1]{0:T(128)} %bitcast.odd_ref, f32[8,128]{1,0:T(8,128)S(1)} %get-tuple-element.45.step, f32[4,128,256]{2,1,0:T(8,128)S(1)} %get-tuple-element.46.speed_ref, f32[8,128,128]{2,1,0:T(8,128)S(1)} %wall.1.refs_0_, f32[1,2,144,128]{3,2,1,0:T(8,128)S(1)} %get-tuple-element.62.refs_0_.refs_1_, ...), custom_call_target="tpu_custom_call" | custom-call | flops 2200000000 | bytes 1024 | tf_op jit(solution)/shard_map/third/pallas_call | solution.py:525
  64.8 0.0 collective-permute-done.15.refs_2_
  64.9 1.1 %third.9.refs_4_ = f32[1,2,144,128]{3,2,1,0:T(8,128)S(1)} custom-call(s32[1]{0:T(128)} %bitcast.odd_ref, f32[8,128]{1,0:T(8,128)S(1)} %get-tuple-element.45.step, f32[4,128,256]{2,1,0:T(8,128)S(1)} %get-tuple-element.46.speed_ref, f32[8,128,128]{2,1,0:T(8,128)S(1)} %wall.1.refs_0_, f32[2,2,144,128]{3,2,1,0:T(8,128)S(1)} %second.10.refs_1_.refs_0_.refs_2_, ...), custom_call_target="tpu_custom_call" | custom-call | flops 1100000000 | bytes 1024 | tf_op jit(solution)/shard_map/third/pallas_call | solution.py:525
  66.0 2.0 %collective-permute-done.13.refs_0_ = f32[1,2,128,128]{3,2,1,0:T(8,128)S(1)} collective-permute-done((f32[1,2,128,128]{3,2,1,0:T(8,128)S(1)}, f32[1,2,128,128]{3,2,1,0:T(8,128)S(1)}, u32[]{:S(2)}, u32[]{:S(2)}) %collective-permute-start.13) | collective-permute-done | bytes 131104 | tf_op jit(solution)/shard_map/ppermute | solution.py:543
  68.0 1.9 %last.1 = f32[4,128,256]{2,1,0:T(8,128)} custom-call(s32[1]{0:T(128)} %bitcast.odd_ref, f32[8,128]{1,0:T(8,128)S(1)} %get-tuple-element.45.step, f32[4,128,256]{2,1,0:T(8,128)S(1)} %get-tuple-element.46.speed_ref, f32[8,128,128]{2,1,0:T(8,128)S(1)} %wall.1.refs_0_, f32[1,2,128,128]{3,2,1,0:T(8,128)S(1)} %collective-permute-done.13.refs_0_, ...), custom_call_target="tpu_custom_call" | custom-call | flops 1100000000 | bytes 1024 | tf_op jit(solution)/shard_map/last/pallas_call | solution.py:698
  (13 shorter events, 0.1 us)
Async XLA Ops:
  0.0 2.5 %copy-start = (s32[64,128]{1,0:T(8,128)S(1)}, s32[64,128]{1,0:T(8,128)}, u32[]{:S(2)}) copy-start(s32[64,128]{1,0:T(8,128)} %param.10) | copy-start | bytes 98308
  1.8 4.8 %collective-permute-start.2 = (f32[3,2,128,128]{3,2,1,0:T(8,128)S(1)}, f32[3,2,128,128]{3,2,1,0:T(8,128)S(1)}, u32[]{:S(2)}, u32[]{:S(2)}) collective-permute-start(f32[3,2,128,128]{3,2,1,0:T(8,128)S(1)} %get-tuple-element.39), channel_id=1, source_target_pairs={{0,1},{1,0},{2,3},{3,2},{4,5},{5,4},{6,7},{7,6},{8,9},{9,8},{10,11... | collective-permute-start | bytes 1179656 | tf_op jit(solution)/shard_map/ppermute | solution.py:543
  2.3 1.4 %collective-permute-start = (f32[8,128]{1,0:T(8,128)S(1)}, f32[8,128]{1,0:T(8,128)S(1)}, u32[]{:S(2)}, u32[]{:S(2)}) collective-permute-start(f32[8,128]{1,0:T(8,128)S(1)} %get-tuple-element.36), channel_id=1, source_target_pairs={{0,1},{1,0},{2,3},{3,2},{4,5},{5,4},{6,7},{7,6},{8,9},{9,8},{10,11... | collective-permute-start | bytes 12296 | tf_op jit(solution)/shard_map/ppermute | solution.py:552
  3.7 4.8 %collective-permute-start.1 = (f32[8,128]{1,0:T(8,128)S(1)}, f32[8,128]{1,0:T(8,128)S(1)}, u32[]{:S(2)}, u32[]{:S(2)}) collective-permute-start(f32[8,128]{1,0:T(8,128)S(1)} %max.12), channel_id=1, source_target_pairs={{0,2},{1,3},{2,0},{3,1},{4,6},{5,7},{6,4},{7,5},{8,10},{9,11},{10,... | collective-permute-start | bytes 12296 | tf_op jit(solution)/shard_map/ppermute | solution.py:552
  8.5 13.2 %collective-permute-start.5 = (f32[3,2,128,128]{3,2,1,0:T(8,128)S(1)}, f32[3,2,128,128]{3,2,1,0:T(8,128)S(1)}, u32[]{:S(2)}, u32[]{:S(2)}) collective-permute-start(f32[3,2,128,128]{3,2,1,0:T(8,128)S(1)} %get-tuple-element.44), channel_id=1, source_target_pairs={{0,15},{1,2},{2,1},{3,4},{4,3},{5,6},{6,5},{7,8},{8,7},{9,10},{10,... | collective-permute-start | bytes 1179656 | tf_op jit(solution)/shard_map/ppermute | solution.py:543
  11.8 5.4 %collective-permute-start.3 = (f32[8,128]{1,0:T(8,128)S(1)}, f32[8,128]{1,0:T(8,128)S(1)}, u32[]{:S(2)}, u32[]{:S(2)}) collective-permute-start(f32[8,128]{1,0:T(8,128)S(1)} %max.13), channel_id=1, source_target_pairs={{0,4},{1,5},{2,6},{3,7},{4,0},{5,1},{6,2},{7,3},{8,12},{9,13},{10,... | collective-permute-start | bytes 12296 | tf_op jit(solution)/shard_map/ppermute | solution.py:552
  17.2 4.5 %collective-permute-start.4 = (f32[8,128]{1,0:T(8,128)S(1)}, f32[8,128]{1,0:T(8,128)S(1)}, u32[]{:S(2)}, u32[]{:S(2)}) collective-permute-start(f32[8,128]{1,0:T(8,128)S(1)} %max.14), channel_id=1, source_target_pairs={{0,8},{1,9},{2,10},{3,11},{4,12},{5,13},{6,14},{7,15},{8,0},{9,1},... | collective-permute-start | bytes 12296 | tf_op jit(solution)/shard_map/ppermute | solution.py:552
  24.9 7.2 %collective-permute-start.6 = (f32[1,2,128,128]{3,2,1,0:T(8,128)S(1)}, f32[1,2,128,128]{3,2,1,0:T(8,128)S(1)}, u32[]{:S(2)}, u32[]{:S(2)}) collective-permute-start(f32[1,2,128,128]{3,2,1,0:T(8,128)S(1)} %get-tuple-element.48), channel_id=1, source_target_pairs={{0,15},{1,2},{2,1},{3,4},{4,3},{5,6},{6,5},{7,8},{8,7},{9,10},{10,... | collective-permute-start | bytes 393224 | tf_op jit(solution)/shard_map/ppermute | solution.py:543
  26.8 2.0 %collective-permute-start.8 = (f32[1,2,128,128]{3,2,1,0:T(8,128)S(1)}, f32[1,2,128,128]{3,2,1,0:T(8,128)S(1)}, u32[]{:S(2)}, u32[]{:S(2)}) collective-permute-start(f32[1,2,128,128]{3,2,1,0:T(8,128)S(1)} %get-tuple-element.52), channel_id=1, source_target_pairs={{0,1},{1,0},{2,3},{3,2},{4,5},{5,4},{6,7},{7,6},{8,9},{9,8},{10,11... | collective-permute-start | bytes 393224 | tf_op jit(solution)/shard_map/ppermute | solution.py:543
  29.8 7.4 %collective-permute-start.9 = (f32[1,2,128,128]{3,2,1,0:T(8,128)S(1)}, f32[1,2,128,128]{3,2,1,0:T(8,128)S(1)}, u32[]{:S(2)}, u32[]{:S(2)}) collective-permute-start(f32[1,2,128,128]{3,2,1,0:T(8,128)S(1)} %get-tuple-element.54), channel_id=1, source_target_pairs={{0,1},{1,0},{2,3},{3,2},{4,5},{5,4},{6,7},{7,6},{8,9},{9,8},{10,11... | collective-permute-start | bytes 393224 | tf_op jit(solution)/shard_map/ppermute | solution.py:543
  33.1 7.2 %collective-permute-start.7 = (f32[1,2,128,128]{3,2,1,0:T(8,128)S(1)}, f32[1,2,128,128]{3,2,1,0:T(8,128)S(1)}, u32[]{:S(2)}, u32[]{:S(2)}) collective-permute-start(f32[1,2,128,128]{3,2,1,0:T(8,128)S(1)} %get-tuple-element.50), channel_id=1, source_target_pairs={{0,15},{1,2},{2,1},{3,4},{4,3},{5,6},{6,5},{7,8},{8,7},{9,10},{10,... | collective-permute-start | bytes 393224 | tf_op jit(solution)/shard_map/ppermute | solution.py:543
  41.4 2.0 %collective-permute-start.11 = (f32[2,2,128,128]{3,2,1,0:T(8,128)S(1)}, f32[2,2,128,128]{3,2,1,0:T(8,128)S(1)}, u32[]{:S(2)}, u32[]{:S(2)}) collective-permute-start(f32[2,2,128,128]{3,2,1,0:T(8,128)S(1)} %get-tuple-element.57), channel_id=1, source_target_pairs={{0,1},{1,0},{2,3},{3,2},{4,5},{5,4},{6,7},{7,6},{8,9},{9,8},{10,11... | collective-permute-start | bytes 786440 | tf_op jit(solution)/shard_map/ppermute | solution.py:543
  41.5 8.7 %collective-permute-start.10 = (f32[2,2,128,128]{3,2,1,0:T(8,128)S(1)}, f32[2,2,128,128]{3,2,1,0:T(8,128)S(1)}, u32[]{:S(2)}, u32[]{:S(2)}) collective-permute-start(f32[2,2,128,128]{3,2,1,0:T(8,128)S(1)} %get-tuple-element.55), channel_id=1, source_target_pairs={{0,15},{1,2},{2,1},{3,4},{4,3},{5,6},{6,5},{7,8},{8,7},{9,10},{10,... | collective-permute-start | bytes 786440 | tf_op jit(solution)/shard_map/ppermute | solution.py:543
  52.6 7.2 %collective-permute-start.12 = (f32[1,2,128,128]{3,2,1,0:T(8,128)S(1)}, f32[1,2,128,128]{3,2,1,0:T(8,128)S(1)}, u32[]{:S(2)}, u32[]{:S(2)}) collective-permute-start(f32[1,2,128,128]{3,2,1,0:T(8,128)S(1)} %get-tuple-element.59), channel_id=1, source_target_pairs={{0,15},{1,2},{2,1},{3,4},{4,3},{5,6},{6,5},{7,8},{8,7},{9,10},{10,... | collective-permute-start | bytes 393224 | tf_op jit(solution)/shard_map/ppermute | solution.py:543
  54.4 2.0 %collective-permute-start.14 = (f32[1,2,128,128]{3,2,1,0:T(8,128)S(1)}, f32[1,2,128,128]{3,2,1,0:T(8,128)S(1)}, u32[]{:S(2)}, u32[]{:S(2)}) collective-permute-start(f32[1,2,128,128]{3,2,1,0:T(8,128)S(1)} %get-tuple-element.64), channel_id=1, source_target_pairs={{0,1},{1,0},{2,3},{3,2},{4,5},{5,4},{6,7},{7,6},{8,9},{9,8},{10,11... | collective-permute-start | bytes 393224 | tf_op jit(solution)/shard_map/ppermute | solution.py:543
  57.4 7.4 %collective-permute-start.15 = (f32[1,2,128,128]{3,2,1,0:T(8,128)S(1)}, f32[1,2,128,128]{3,2,1,0:T(8,128)S(1)}, u32[]{:S(2)}, u32[]{:S(2)}) collective-permute-start(f32[1,2,128,128]{3,2,1,0:T(8,128)S(1)} %get-tuple-element.66), channel_id=1, source_target_pairs={{0,1},{1,0},{2,3},{3,2},{4,5},{5,4},{6,7},{7,6},{8,9},{9,8},{10,11... | collective-permute-start | bytes 393224 | tf_op jit(solution)/shard_map/ppermute | solution.py:543
  60.8 7.2 %collective-permute-start.13 = (f32[1,2,128,128]{3,2,1,0:T(8,128)S(1)}, f32[1,2,128,128]{3,2,1,0:T(8,128)S(1)}, u32[]{:S(2)}, u32[]{:S(2)}) collective-permute-start(f32[1,2,128,128]{3,2,1,0:T(8,128)S(1)} %get-tuple-element.61), channel_id=1, source_target_pairs={{0,15},{1,2},{2,1},{3,4},{4,3},{5,6},{6,5},{7,8},{8,7},{9,10},{10,... | collective-permute-start | bytes 393224 | tf_op jit(solution)/shard_map/ppermute | solution.py:543

commit v3 on v2

--- a/solution.py
+++ b/solution.py
@@ -16,7 +16,7 @@
 PAD = 8
 ROWS = 32
 HALVES = (0, 1)
-OUTER = 2
+OUTER = 3
 INNER = 2
 VMEM_LIMIT = 24 * 1024 * 1024
 SEND_ROUND = 2
@@ -172,7 +172,7 @@
 
 
 def begin_kernel(odd_ref, fraction_in, mask_in, *refs):
-    speeds_in, (*speeds, peak, state, send_outer, send_inner, fraction, mask, sems) = refs[:3], refs[3:]
+    speeds_in, (*speeds, peak, state, fraction, mask, sems) = refs[:3], refs[3:]
     odd = odd_ref[0] == 1
     count, rows, width = fraction.shape
     sources = (*speeds_in, fraction_in, mask_in)
@@ -190,34 +190,42 @@
     peak[...] = jnp.maximum(best[:, :LANES], best[:, LANES:])
     copies[3].wait()
     copies[4].wait()
-    for p in range(OUTER, OUTER + count):
-        index = own_index(odd, p, count)
-        to = [Layer(state, p - OUTER)]
-        if p - OUTER < OUTER:
-            to.append(Layer(send_outer, p - OUTER, False))
-        if OUTER + count - 1 - p < INNER:
-            to.append(Layer(send_inner, OUTER + count - 1 - p, False))
+    for k in range(count):
+        index = own_index(odd, OUTER + k, count)
         for r in range(0, rows, ROWS):
             for h in HALVES:
                 value = jnp.where(natural(mask, index, h, r) == 1, 1.0, natural(fraction, index, h, r))
-                for target in to:
-                    target.write(h, r, value)
-        Layer(state, p - OUTER).wrap()
-    first = speeds[0]
+                Layer(state, k).write(h, r, value)
+        Layer(state, k).wrap()
+
+
+def first_send_kernel(odd_ref, first, state, send_outer, send_inner):
+    odd = odd_ref[0] == 1
+    count, rows, _ = first.shape
+    for k in range(OUTER):
+        copy_layer(Layer(state, k), Layer(send_outer, k, False), rows)
+    for k in range(INNER):
+        copy_layer(Layer(state, count - 1 - k), Layer(send_inner, k, False), rows)
+    near = jnp.where(odd, count - 2, 0)
     for r in range(0, rows, ROWS):
         for h in HALVES:
-            Layer(send_outer, OUTER, False).write(h, r, natural(first, count - 1, h, r))
+            Layer(send_outer, OUTER, False).write(h, r, natural(first, near, h, r))
+            Layer(send_outer, OUTER + 1, False).write(h, r, natural(first, count - 1, h, r))
             Layer(send_inner, INNER, False).write(h, r, natural(first, count - 1, h, r))
 
 
-def wall_kernel(where_ref, cosine, out):
+def wall_kernel(where_ref, cosine, out, turned):
     odd = where_ref[0] == 1
     total = cosine.shape[0]
     layers = out.shape[0]
     count = layers - OUTER - INNER
+    turned[...] = jnp.zeros(turned.shape, jnp.float32)
     for p in range(1, layers - 1):
         row = lax.rem(where_ref[1] + own_index(odd, p, count) + total, total)
-        out[p] = jnp.transpose(jnp.broadcast_to(cosine[pl.ds(row, 1), :], (LANES, cosine.shape[1])))
+        turned[pl.ds(p, 1), :] = cosine[pl.ds(row, 1), :]
+    columns = jnp.transpose(turned[...])
+    for p in range(1, layers - 1):
+        out[p] = pltpu.roll(columns, LANES - p, 1)
 
 
 KEPT = 9
@@ -256,9 +264,11 @@
     for k, face in enumerate(faces):
         for r in range(0, rows, ROWS):
             for h in HALVES:
-                if face == OUTER - 1:
+                if face == OUTER - 2:
+                    value = Layer(given["outer"], OUTER, False).read(h, r)
+                elif face == OUTER - 1:
                     value = natural(given["first"], count - 1, h, r)
-                    value = jnp.where(odd, value, Layer(given["outer"], OUTER, False).read(h, r))
+                    value = jnp.where(odd, value, Layer(given["outer"], OUTER + 1, False).read(h, r))
                 elif face == OUTER + count - 1:
                     value = natural(given["first"], count - 1, h, r)
                     value = jnp.where(odd, Layer(given["inner"], INNER, False).read(h, r), value)
@@ -298,11 +308,10 @@
     for r in range(0, rows, ROWS):
         for h in HALVES:
             target.write(h, r, jnp.clip(here.read(h, r) - outward.read(h, r) + inward.read(h, r), 0.0, 1.0))
-    target.wrap()
 
 
 def finish_kernel(peak, *refs, parts):
-    kept, (state, out, moved, step_out, send_outer, send_inner, flux) = refs[:parts], refs[parts:]
+    kept, (state, outer, out, above, moved, step_out, send, flux) = refs[:parts], refs[parts:]
     rows = moved.shape[2]
     largest = jnp.max(peak[...])
     step = CFL_NUMBER / (jnp.full((8, LANES), largest, jnp.float32) + 1e-6)
@@ -314,10 +323,11 @@
 
     @pl.loop(0, state.shape[0])
     def _(k):
-        update(Layer(out, k), Layer(state, k), Layer(flux, k, False), Layer(flux, k + 1, False), rows)
-
-    copy_layer(Layer(out, 0), Layer(send_outer, 0, False), rows)
-    copy_layer(Layer(out, out.shape[0] - 1), Layer(send_inner, 0, False), rows)
+        update(Layer(out, k), Layer(state, k), Layer(flux, k + 1, False), Layer(flux, k + 2, False), rows)
+        Layer(out, k).wrap()
+
+    update(Layer(above, 0, False), Layer(outer, 0, False), Layer(flux, 0, False), Layer(flux, 1, False), rows)
+    copy_layer(Layer(out, out.shape[0] - 1), Layer(send, 0, False), rows)
 
 
 def first_fluxes(field, wall, moved, n_s, n_a, n_b, flux, start, stop):
@@ -359,11 +369,12 @@
     @pl.loop(OUTER + 2, OUTER + count)
     def _(i):
         update(Layer(out, i - OUTER - 2), Layer(field, i), Layer(flux, i - 2, False), Layer(flux, i - 1, False), rows)
+        Layer(out, i - OUTER - 2).wrap()
 
     copy_layer(Layer(out, count - 3), Layer(send, 0, False), rows)
 
 
-def outside_kernel(edge, middle, last, outer, moved, wall, flux_above, out, send, field, n_s, n_a, n_b, flux):
+def outside_kernel(edge, middle, last, outer, moved, wall, flux_above, above, out, field, n_s, n_a, n_b, flux):
     rows = moved.shape[2]
     count = middle.shape[0] + 2
     fill(outer, field, OUTER - 1, -1, 0, OUTER, False)
@@ -371,11 +382,12 @@
     fill(middle, field, OUTER + 1, 1, 0, count - 2, True)
     if count < 4:
         fill(last, field, OUTER + count - 1, 1, 0, 1, True)
-    first_fluxes(field, wall, moved, n_s, n_a, n_b, flux, OUTER - 1, OUTER + 1)
-    edge_layer, next_layer = Layer(out, 0), Layer(out, 1)
-    update(edge_layer, Layer(field, OUTER), Layer(flux, 0, False), Layer(flux, 1, False), rows)
-    update(next_layer, Layer(field, OUTER + 1), Layer(flux, 1, False), Layer(flux_above, 0, False), rows)
-    copy_layer(edge_layer, Layer(send, 0, False), rows)
+    first_fluxes(field, wall, moved, n_s, n_a, n_b, flux, OUTER - 2, OUTER + 1)
+    fluxes = [Layer(flux, k, False) for k in range(OUTER)] + [Layer(flux_above, 0, False)]
+    for k, target in enumerate((Layer(above, 0, False), Layer(out, 0), Layer(out, 1))):
+        update(target, Layer(field, OUTER - 1 + k), fluxes[k], fluxes[k + 1], rows)
+        if k > 0:
+            target.wrap()
 
 
 def second_sweep(before, here, after, wall, speed, out, scratch):
@@ -570,11 +582,11 @@
         return (n, 2, rows, LANES)
 
     natural_shape = (count, rows, width)
-    first, second, third, peak, state, send_outer, send_inner = call(
+    first, second, third, peak, state = call(
         begin_kernel,
         "begin",
         [held(natural_shape)] * 3
-        + [held((8, LANES)), held(padded(count)), held(plain(OUTER + 1)), held(plain(INNER + 1))],
+        + [held((8, LANES)), held(padded(count))],
         [odd],
         [fraction, seed_mask, first, second, third],
         [
@@ -584,9 +596,12 @@
         ],
         resident=False,
     )
+    send_outer, send_inner = call(
+        first_send_kernel, "first_send", [held(plain(OUTER + 2)), held(plain(INNER + 1))], [odd], [first, state]
+    )
     inner = swap(send_inner, False)
     cosine = jnp.cos(jnp.pi * (wall_class.astype(jnp.float32) + 1.0) / (WALL_CLASSES + 1))
-    (wall,) = call(wall_kernel, "wall", [held((layers, rows, LANES))], [place], [cosine])
+    (wall,) = call(wall_kernel, "wall", [held((layers, rows, LANES))], [place], [cosine], [pltpu.VMEM((LANES, rows), jnp.float32)])
     slopes = [pltpu.VMEM(padded(layers), jnp.float32)] + [pltpu.VMEM(plain(layers), jnp.float32)] * 3
 
     def prepare_call(faces, **given):
@@ -602,33 +617,29 @@
 
     size = lax.axis_size("gx")
     prepare_inside = functools.partial(prepare_call, wall=wall, first=first, own=state, inner=inner)
+    outer = swap(send_outer, True)
     peak = largest_round(peak, 1, [])
     kept = [prepare_inside(tuple(range(OUTER + 2, own_end)))]
-    if size > 2:
-        peak = largest_round(peak, 2, kept)
-    peak, send_outer = lax.optimization_barrier((peak, send_outer))
-    outer = swap(send_outer, True)
+    peak = largest_round(peak, 8, kept)
     kept.insert(0, prepare_inside((OUTER + 1,)))
-    kept.insert(0, prepare_call((OUTER - 1, OUTER), wall=wall, first=first, own=state, outer=outer))
-    reach, beside = 4, [[kept[1]]]
-    while reach < size:
-        peak = largest_round(peak, reach, beside.pop() if beside else [])
-        reach *= 2
-    own, moved, step, send_outer, send_inner = call(
+    kept.insert(0, prepare_call((OUTER - 2, OUTER - 1, OUTER), wall=wall, first=first, own=state, outer=outer))
+    peak = largest_round(peak, 4, [kept[1]])
+    peak = largest_round(peak, 2, [kept[0]])
+    own, above, moved, step, send_inner = call(
         functools.partial(finish_kernel, parts=len(kept)),
         "finish",
-        [held(padded(count)), held(plain(count + 1)), held((8, LANES)), held(plain(1)), held(plain(1))],
+        [held(padded(count)), held(plain(1)), held(plain(count + 2)), held((8, LANES)), held(plain(1))],
         [],
-        [peak, *kept, state],
-        [pltpu.VMEM(plain(count + 1), jnp.float32)],
+        [peak, *kept, state, outer],
+        [pltpu.VMEM(plain(count + 2), jnp.float32)],
         faces=1,
     )
-    swept, places = [own], [(OUTER, True)]
+    swept, places = [above, own], [(OUTER - 1, False), (OUTER, True)]
     line = [pltpu.VMEM(padded(1), jnp.float32)] * 4
     for turn in range(STEPS):
         final = turn == STEPS - 1
         if turn > 0:
-            flux = pltpu.VMEM(plain(count + 1), jnp.float32)
+            flux = pltpu.VMEM(plain(count + 2), jnp.float32)
             inside, flux_low, send_inner = call(
                 inside_kernel,
                 "inside",
@@ -638,18 +649,18 @@
                 [*slopes, flux],
                 faces=count - 1,
             )
-            outside, send_outer = call(
+            above, outside = call(
                 outside_kernel,
                 "outside",
-                [held(padded(2)), held(plain(1))],
+                [held(plain(1)), held(padded(2))],
                 [],
                 [*own, outer, moved, wall, flux_low],
                 [*slopes, flux],
-                faces=2,
+                faces=3,
             )
-            swept, places = [outside, inside], [(OUTER, True), (OUTER + 2, True)]
+            swept = [above, outside, inside]
+            places = [(OUTER - 1, False), (OUTER, True), (OUTER + 2, True)]
         inner = swap(send_inner, False)
-        outer = swap(send_outer, True)
 
         def second_call(work, fields, places, send):
             return call(
@@ -664,8 +675,9 @@
 
         last, send_inner = second_call((own_end - 1,), [swept[-1], inner], [places[-1], (own_end, False)], True)
         inner = swap(send_inner, False)
-        (middle,) = second_call(tuple(range(OUTER + 1, own_end - 1)), swept, places, False)
-        edge, send_outer = second_call((OUTER,), [outer, swept[0]], [(OUTER - 1, False), places[0]], True)
+        edge, send_outer = second_call((OUTER,), swept[:2], places[:2], True)
+        after = lax.optimization_barrier((edge, *swept[1:]))[1:]
+        (middle,) = second_call(tuple(range(OUTER + 1, own_end - 1)), after, places[1:], False)
         outer = swap(send_outer, True)
 
         fields = [edge, middle, last, inner]

time: 70.2 us -> 64 us (0.912)
  waiting for transfers between devices: 18.6 us -> 9.62 us
  Pallas kernels: 32.1 us -> 37.1 us
  starting transfers between devices: 18.9 us -> 16.5 us
    ppermute x12 -> x10, waiting for transfers between devices: 10.9 us -> 4.42 us  [swap(): return lax.ppermute(array, 'gx', pairs)]
    pallas_call x20 -> x21, Pallas kernels: 30.2 us -> 35.2 us  [call(): pl.pallas_call(kernel, out_shape=outs, in_specs=[IN_SMEM] * len(scalars)...]
    ppermute x4, starting transfers between devices: 4.53 us -> 1.61 us  [largest_round(): received = lax.ppermute(array, 'gx', pairs)]
    ppermute x4, waiting for transfers between devices: 7.65 us -> 5.2 us  [largest_round(): received = lax.ppermute(array, 'gx', pairs)]
    ppermute x12 -> x10, starting transfers between devices: 14.3 us -> 14.9 us  [swap(): return lax.ppermute(array, 'gx', pairs)]
  transfers between devices with their start and end apart: 16 -> 14, of which waited for: 8 -> 6; matrix products, arithmetic and copies ran while one was open for 0% -> 0% of each run, Pallas kernels for 31% -> 47%
where the time goes in v3:
time: 64 us; the launch traced here: 63.7 us
  Pallas kernels  37.1 us (58%)
  starting transfers between devices  16.5 us (26%)
  waiting for transfers between devices  9.62 us (15%)
    pallas_call x21, Pallas kernels, call(): pl.pallas_call(kernel, out_shape=outs, in_specs=[IN_SMEM] * len(scalars)...  35.2 us
    ppermute x10, starting transfers between devices, swap(): return lax.ppermute(array, 'gx', pairs)  14.9 us
    ppermute x4, waiting for transfers between devices, largest_round(): received = lax.ppermute(array, 'gx', pairs)  5.2 us
    ppermute x10, waiting for transfers between devices, swap(): return lax.ppermute(array, 'gx', pairs)  4.42 us
    pallas_call x1, Pallas kernels, last_call(): pl.pallas_call(functools.partial(last_kernel, places=places), out_shape=j...  1.88 us
    ppermute x4, starting transfers between devices, largest_round(): received = lax.ppermute(array, 'gx', pairs)  1.61 us
  transfers between devices with their start and end apart: 14, of which 6 were waited for; matrix products, arithmetic and copies ran while one was open for 0% of the time, Pallas kernels for 47%

profile of v3, /device:TPU:0, one launch (start us, length us, event | category | flops | bytes accessed | tf_op | source)
XLA Modules:
  0.0 63.7 jit_solution(2645371463839188404)
XLA Ops:
  0.0 1.8 %begin.1 = (f32[4,128,256]{2,1,0:T(8,128)S(1)}, f32[4,128,256]{2,1,0:T(8,128)S(1)}, f32[4,128,256]{2,1,0:T(8,128)S(1)}, f32[8,128]{1,0:T(8,128)S(1)}, f32[4,2,144,128]{3,2,1,0:T(8,128)S(1)}) custom-call(s32[1]{0:T(128)} %bitcast.odd_ref, f32[4,128,256]{2,1,0:T(8,128)} %fraction_in.1, s32[4,128,256]{2,1,0:T(8,128)} %mask_in.1, f32[4,128,256]{2,1,0:T(8,128)} %refs_0_.1, ...), custom_call_target="tpu_custom_call" | custom-call | flops 110000000 | bytes 1024 | tf_op jit(solution)/shard_map/begin/pallas_call | solution.py:537
  1.8 0.8 %first_send.1 = (f32[5,2,128,128]{3,2,1,0:T(8,128)S(1)}, f32[3,2,128,128]{3,2,1,0:T(8,128)}) custom-call(s32[1]{0:T(128)} %bitcast.odd_ref, f32[4,128,256]{2,1,0:T(8,128)S(1)} %get-tuple-element.39.first.refs_1_, f32[4,2,144,128]{3,2,1,0:T(8,128)S(1)} %get-tuple-element.40.state.refs_2_.refs_3_), custom_call_target="tpu_custom_call" | custom-call | flops 110000000 | bytes 1024 | tf_op jit(solution)/shard_map/first_send/pallas_call | solution.py:537
  2.6 0.5 collective-permute-start.2
  3.1 0.1 collective-permute-start
  3.1 5.6 %collective-permute-start.5 = (f32[5,2,128,128]{3,2,1,0:T(8,128)S(1)}, f32[5,2,128,128]{3,2,1,0:T(8,128)S(1)}, u32[]{:S(2)}, u32[]{:S(2)}) collective-permute-start(f32[5,2,128,128]{3,2,1,0:T(8,128)S(1)} %get-tuple-element.44), channel_id=1, source_target_pairs={{0,15},{1,2},{2,1},{3,4},{4,3},{5,6},{6,5},{7,8},{8,7},{9,10},{10,... | collective-permute-start | bytes 1966088 | tf_op jit(solution)/shard_map/ppermute | solution.py:555
  8.7 0.1 pad_add_fusion.where_ref
  8.8 0.1 multiply_cosine_fusion.cosine
  8.9 0.8 %wall.1.refs_0_ = f32[9,128,128]{2,1,0:T(8,128)S(1)} custom-call(s32[2]{0:T(128)S(1)} %pad_add_fusion.where_ref, f32[64,128]{1,0:T(8,128)S(1)} %multiply_cosine_fusion.cosine), custom_call_target="tpu_custom_call" | custom-call | flops 110000000 | bytes 1024 | tf_op jit(solution)/shard_map/wall/pallas_call | solution.py:537
  9.8 0.1 collective-permute-start.1
  9.9 2.9 %prepare.3.refs_2_ = f32[18,2,128,128]{3,2,1,0:T(8,128)S(1)} custom-call(s32[1]{0:T(128)} %bitcast.odd_ref, f32[9,128,128]{2,1,0:T(8,128)S(1)} %wall.1.refs_0_, f32[4,128,256]{2,1,0:T(8,128)S(1)} %get-tuple-element.39.first.refs_1_, f32[4,2,144,128]{3,2,1,0:T(8,128)S(1)} %get-tuple-element.40.state.refs_2_.refs_3_, ...), custom_call_target="tpu_custom_call" | custom-call | flops 2200000000 | bytes 1024 | tf_op jit(solution)/shard_map/prepare/pallas_call | solution.py:537
  12.8 4.2 %collective-permute-done.1 = f32[8,128]{1,0:T(8,128)S(1)} collective-permute-done((f32[8,128]{1,0:T(8,128)S(1)}, f32[8,128]{1,0:T(8,128)S(1)}, u32[]{:S(2)}, u32[]{:S(2)}) %collective-permute-start.1) | collective-permute-done | bytes 4128 | tf_op jit(solution)/shard_map/ppermute | solution.py:564
  17.0 1.5 %collective-permute-start.3 = (f32[8,128]{1,0:T(8,128)S(1)}, f32[8,128]{1,0:T(8,128)S(1)}, u32[]{:S(2)}, u32[]{:S(2)}) collective-permute-start(f32[8,128]{1,0:T(8,128)S(1)} %max.13), channel_id=1, source_target_pairs={{0,4},{1,5},{2,6},{3,7},{4,0},{5,1},{6,2},{7,3},{8,12},{9,13},{10,... | collective-permute-start | bytes 12296 | tf_op jit(solution)/shard_map/ppermute | solution.py:564
  18.5 2.0 %prepare.4.refs_1_ = f32[9,2,128,128]{3,2,1,0:T(8,128)S(1)} custom-call(s32[1]{0:T(128)} %bitcast.odd_ref, f32[9,128,128]{2,1,0:T(8,128)S(1)} %wall.1.refs_0_, f32[4,128,256]{2,1,0:T(8,128)S(1)} %get-tuple-element.39.first.refs_1_, f32[4,2,144,128]{3,2,1,0:T(8,128)S(1)} %get-tuple-element.40.state.refs_2_.refs_3_, ...), custom_call_target="tpu_custom_call" | custom-call | flops 1100000000 | bytes 1024 | tf_op jit(solution)/shard_map/prepare/pallas_call | solution.py:537
  20.5 0.1 collective-permute-done.3
  20.6 0.0 collective-permute-start.4
  20.6 2.7 %prepare.5.refs_0_ = f32[27,2,128,128]{3,2,1,0:T(8,128)S(1)} custom-call(s32[1]{0:T(128)} %bitcast.odd_ref, f32[9,128,128]{2,1,0:T(8,128)S(1)} %wall.1.refs_0_, f32[4,128,256]{2,1,0:T(8,128)S(1)} %get-tuple-element.39.first.refs_1_, f32[4,2,144,128]{3,2,1,0:T(8,128)S(1)} %get-tuple-element.40.state.refs_2_.refs_3_, ...), custom_call_target="tpu_custom_call" | custom-call | flops 3300000000 | bytes 1024 | tf_op jit(solution)/shard_map/prepare/pallas_call | solution.py:537
  23.4 0.9 %collective-permute-done.4 = f32[8,128]{1,0:T(8,128)S(1)} collective-permute-done((f32[8,128]{1,0:T(8,128)S(1)}, f32[8,128]{1,0:T(8,128)S(1)}, u32[]{:S(2)}, u32[]{:S(2)}) %collective-permute-start.4) | collective-permute-done | bytes 4128 | tf_op jit(solution)/shard_map/ppermute | solution.py:564
  24.2 1.5 %finish.1 = (f32[4,2,144,128]{3,2,1,0:T(8,128)S(1)}, f32[1,2,128,128]{3,2,1,0:T(8,128)S(1)}, f32[6,2,128,128]{3,2,1,0:T(8,128)S(1)}, f32[8,128]{1,0:T(8,128)S(1)}, f32[1,2,128,128]{3,2,1,0:T(8,128)S(1)}) custom-call(f32[8,128]{1,0:T(8,128)S(1)} %max.15.peak, f32[27,2,128,128]{3,2,1,0:T(8,128)S(1)} %prepare.5.refs_0_, f32[9,2,128,128]{3,2,1,0:T(8,128)S(1)} %prepare.4.refs_1_, ...), custom_call_target="tpu_custom_call" | custom-call | flops 1100000000 | bytes 1024 | tf_op jit(solution)/shard_map/finish/pallas_call | solution.py:537
  25.7 0.1 collective-permute-start.7
  25.8 1.0 %second.6 = (f32[1,2,144,128]{3,2,1,0:T(8,128)S(1)}, f32[1,2,128,128]{3,2,1,0:T(8,128)S(1)}) custom-call(s32[1]{0:T(128)} %bitcast.odd_ref, f32[8,128]{1,0:T(8,128)S(1)} %get-tuple-element.46.step, f32[4,128,256]{2,1,0:T(8,128)S(1)} %get-tuple-element.48.speed_ref, f32[9,128,128]{2,1,0:T(8,128)S(1)} %wall.1.refs_0_, ...), custom_call_target="tpu_custom_call" | custom-call | flops 1100000000 | bytes 1024 | tf_op jit(solution)/shard_map/second/pallas_call | solution.py:537
  26.9 4.8 %collective-permute-start.6 = (f32[1,2,128,128]{3,2,1,0:T(8,128)S(1)}, f32[1,2,128,128]{3,2,1,0:T(8,128)S(1)}, u32[]{:S(2)}, u32[]{:S(2)}) collective-permute-start(f32[1,2,128,128]{3,2,1,0:T(8,128)S(1)} %get-tuple-element.51), channel_id=1, source_target_pairs={{0,15},{1,2},{2,1},{3,4},{4,3},{5,6},{6,5},{7,8},{8,7},{9,10},{10,... | collective-permute-start | bytes 393224 | tf_op jit(solution)/shard_map/ppermute | solution.py:555
  31.7 2.0 %second.7.refs_2_.refs_1_.refs_0_ = f32[2,2,144,128]{3,2,1,0:T(8,128)S(1)} custom-call(s32[1]{0:T(128)} %bitcast.odd_ref, f32[8,128]{1,0:T(8,128)S(1)} %get-tuple-element.46.step, f32[4,128,256]{2,1,0:T(8,128)S(1)} %get-tuple-element.48.speed_ref, f32[9,128,128]{2,1,0:T(8,128)S(1)} %wall.1.refs_0_, f32[4,2,144,128]{3,2,1,0:T(8,128)S(1)} %get-tuple-element.53.refs_1_.refs_0_), custom_call_target="tpu_custom_call" | custom-call | flops 2200000000 | bytes 1024 | tf_op jit(solution)/shard_map/second/pallas_call | solution.py:537
  33.7 0.0 collective-permute-done.7.refs_1_
  33.7 1.0 %second.8 = (f32[1,2,144,128]{3,2,1,0:T(8,128)S(1)}, f32[1,2,128,128]{3,2,1,0:T(8,128)S(1)}) custom-call(s32[1]{0:T(128)} %bitcast.odd_ref, f32[8,128]{1,0:T(8,128)S(1)} %get-tuple-element.46.step, f32[4,128,256]{2,1,0:T(8,128)S(1)} %get-tuple-element.48.speed_ref, f32[9,128,128]{2,1,0:T(8,128)S(1)} %wall.1.refs_0_, ...), custom_call_target="tpu_custom_call" | custom-call | flops 1100000000 | bytes 1024 | tf_op jit(solution)/shard_map/second/pallas_call | solution.py:537
  34.7 0.1 collective-permute-start.8
  34.8 2.2 %third.6.middle = f32[2,2,144,128]{3,2,1,0:T(8,128)S(1)} custom-call(s32[1]{0:T(128)} %bitcast.odd_ref, f32[8,128]{1,0:T(8,128)S(1)} %get-tuple-element.46.step, f32[4,128,256]{2,1,0:T(8,128)S(1)} %get-tuple-element.47.speed_ref, f32[9,128,128]{2,1,0:T(8,128)S(1)} %wall.1.refs_0_, f32[1,2,144,128]{3,2,1,0:T(8,128)S(1)} %get-tuple-element.52.refs_1_.refs_0_, ...), custom_call_target="tpu_custom_call" | custom-call | flops 2200000000 | bytes 1024 | tf_op jit(solution)/shard_map/third/pallas_call | solution.py:537
  37.0 0.0 collective-permute-done.6.refs_0_
  37.0 1.1 %third.5.edge = f32[1,2,144,128]{3,2,1,0:T(8,128)S(1)} custom-call(s32[1]{0:T(128)} %bitcast.odd_ref, f32[8,128]{1,0:T(8,128)S(1)} %get-tuple-element.46.step, f32[4,128,256]{2,1,0:T(8,128)S(1)} %get-tuple-element.47.speed_ref, f32[9,128,128]{2,1,0:T(8,128)S(1)} %wall.1.refs_0_, f32[1,2,128,128]{3,2,1,0:T(8,128)S(1)} %collective-permute-done.6.refs_0_, ...), custom_call_target="tpu_custom_call" | custom-call | flops 1100000000 | bytes 1024 | tf_op jit(solution)/shard_map/third/pallas_call | solution.py:537
  38.1 0.0 collective-permute-done.8.refs_2_
  38.1 1.1 %third.7.last = f32[1,2,144,128]{3,2,1,0:T(8,128)S(1)} custom-call(s32[1]{0:T(128)} %bitcast.odd_ref, f32[8,128]{1,0:T(8,128)S(1)} %get-tuple-element.46.step, f32[4,128,256]{2,1,0:T(8,128)S(1)} %get-tuple-element.47.speed_ref, f32[9,128,128]{2,1,0:T(8,128)S(1)} %wall.1.refs_0_, f32[2,2,144,128]{3,2,1,0:T(8,128)S(1)} %second.7.refs_2_.refs_1_.refs_0_, ...), custom_call_target="tpu_custom_call" | custom-call | flops 1100000000 | bytes 1024 | tf_op jit(solution)/shard_map/third/pallas_call | solution.py:537
  39.3 0.1 pack.1
  39.3 0.6 collective-permute-start.10
  39.9 1.3 %collective-permute-start.9 = (f32[3,2,128,128]{3,2,1,0:T(8,128)S(1)}, f32[3,2,128,128]{3,2,1,0:T(8,128)S(1)}, u32[]{:S(2)}, u32[]{:S(2)}) collective-permute-start(f32[3,2,128,128]{3,2,1,0:T(8,128)S(1)} %get-tuple-element.57), channel_id=1, source_target_pairs={{0,15},{1,2},{2,1},{3,4},{4,3},{5,6},{6,5},{7,8},{8,7},{9,10},{10,... | collective-permute-start | bytes 1179656 | tf_op jit(solution)/shard_map/ppermute | solution.py:555
  41.2 3.3 %inside.1 = (f32[2,2,144,128]{3,2,1,0:T(8,128)S(1)}, f32[1,2,128,128]{3,2,1,0:T(8,128)S(1)}, f32[1,2,128,128]{3,2,1,0:T(8,128)S(1)}) custom-call(f32[1,2,144,128]{3,2,1,0:T(8,128)S(1)} %third.5.edge, f32[2,2,144,128]{3,2,1,0:T(8,128)S(1)} %third.6.middle, f32[1,2,144,128]{3,2,1,0:T(8,128)S(1)} %third.7.last, ...), custom_call_target="tpu_custom_call" | custom-call | flops 3300000000 | bytes 1024 | tf_op jit(solution)/shard_map/inside/pallas_call | solution.py:537
  44.5 0.3 collective-permute-start.12
  44.8 1.1 %collective-permute-done.12.refs_1_ = f32[1,2,128,128]{3,2,1,0:T(8,128)S(1)} collective-permute-done((f32[1,2,128,128]{3,2,1,0:T(8,128)S(1)}, f32[1,2,128,128]{3,2,1,0:T(8,128)S(1)}, u32[]{:S(2)}, u32[]{:S(2)}) %collective-permute-start.12) | collective-permute-done | bytes 131104 | tf_op jit(solution)/shard_map/ppermute | solution.py:555
  45.9 1.0 %second.11 = (f32[1,2,144,128]{3,2,1,0:T(8,128)S(1)}, f32[1,2,128,128]{3,2,1,0:T(8,128)S(1)}) custom-call(s32[1]{0:T(128)} %bitcast.odd_ref, f32[8,128]{1,0:T(8,128)S(1)} %get-tuple-element.46.step, f32[4,128,256]{2,1,0:T(8,128)S(1)} %get-tuple-element.48.speed_ref, f32[9,128,128]{2,1,0:T(8,128)S(1)} %wall.1.refs_0_, ...), custom_call_target="tpu_custom_call" | custom-call | flops 1100000000 | bytes 1024 | tf_op jit(solution)/shard_map/second/pallas_call | solution.py:537
  46.9 0.3 collective-permute-start.13
  47.2 2.7 %collective-permute-done.9.outer = f32[3,2,128,128]{3,2,1,0:T(8,128)S(1)} collective-permute-done((f32[3,2,128,128]{3,2,1,0:T(8,128)S(1)}, f32[3,2,128,128]{3,2,1,0:T(8,128)S(1)}, u32[]{:S(2)}, u32[]{:S(2)}) %collective-permute-start.9) | collective-permute-done | bytes 393248 | tf_op jit(solution)/shard_map/ppermute | solution.py:555
  49.9 3.5 %outside.1 = (f32[1,2,128,128]{3,2,1,0:T(8,128)S(1)}, f32[2,2,144,128]{3,2,1,0:T(8,128)S(1)}) custom-call(f32[1,2,144,128]{3,2,1,0:T(8,128)S(1)} %third.5.edge, f32[2,2,144,128]{3,2,1,0:T(8,128)S(1)} %third.6.middle, f32[1,2,144,128]{3,2,1,0:T(8,128)S(1)} %third.7.last, f32[3,2,128,128]{3,2,1,0:T(8,128)S(1)} %collective-permute-done.9.outer, ...), custom_call_target="tpu_custom_call" | custom-call | flops 3300000000 | bytes 1024 | tf_op jit(solution)/shard_map/outside/pallas_call | solution.py:537
  53.4 1.1 %second.9 = (f32[1,2,144,128]{3,2,1,0:T(8,128)S(1)}, f32[1,2,128,128]{3,2,1,0:T(8,128)S(1)}) custom-call(s32[1]{0:T(128)} %bitcast.odd_ref, f32[8,128]{1,0:T(8,128)S(1)} %get-tuple-element.46.step, f32[4,128,256]{2,1,0:T(8,128)S(1)} %get-tuple-element.48.speed_ref, f32[9,128,128]{2,1,0:T(8,128)S(1)} %wall.1.refs_0_, ...), custom_call_target="tpu_custom_call" | custom-call | flops 1100000000 | bytes 1024 | tf_op jit(solution)/shard_map/second/pallas_call | solution.py:537
  54.4 1.4 %collective-permute-start.11 = (f32[1,2,128,128]{3,2,1,0:T(8,128)S(1)}, f32[1,2,128,128]{3,2,1,0:T(8,128)S(1)}, u32[]{:S(2)}, u32[]{:S(2)}) collective-permute-start(f32[1,2,128,128]{3,2,1,0:T(8,128)S(1)} %get-tuple-element.63), channel_id=1, source_target_pairs={{0,15},{1,2},{2,1},{3,4},{4,3},{5,6},{6,5},{7,8},{8,7},{9,10},{10,... | collective-permute-start | bytes 393224 | tf_op jit(solution)/shard_map/ppermute | solution.py:555
  55.8 2.0 %second.10.refs_1_.refs_0_.refs_2_ = f32[2,2,144,128]{3,2,1,0:T(8,128)S(1)} custom-call(s32[1]{0:T(128)} %bitcast.odd_ref, f32[8,128]{1,0:T(8,128)S(1)} %get-tuple-element.46.step, f32[4,128,256]{2,1,0:T(8,128)S(1)} %get-tuple-element.48.speed_ref, f32[9,128,128]{2,1,0:T(8,128)S(1)} %wall.1.refs_0_, ...), custom_call_target="tpu_custom_call" | custom-call | flops 2200000000 | bytes 1024 | tf_op jit(solution)/shard_map/second/pallas_call | solution.py:537
  57.8 2.2 %third.8.refs_3_ = f32[2,2,144,128]{3,2,1,0:T(8,128)S(1)} custom-call(s32[1]{0:T(128)} %bitcast.odd_ref, f32[8,128]{1,0:T(8,128)S(1)} %get-tuple-element.46.step, f32[4,128,256]{2,1,0:T(8,128)S(1)} %get-tuple-element.47.speed_ref, f32[9,128,128]{2,1,0:T(8,128)S(1)} %wall.1.refs_0_, f32[1,2,144,128]{3,2,1,0:T(8,128)S(1)} %get-tuple-element.64.refs_0_.refs_1_, ...), custom_call_target="tpu_custom_call" | custom-call | flops 2200000000 | bytes 1024 | tf_op jit(solution)/shard_map/third/pallas_call | solution.py:537
  60.0 0.0 collective-permute-done.13.refs_2_
  60.0 1.1 %third.9.refs_4_ = f32[1,2,144,128]{3,2,1,0:T(8,128)S(1)} custom-call(s32[1]{0:T(128)} %bitcast.odd_ref, f32[8,128]{1,0:T(8,128)S(1)} %get-tuple-element.46.step, f32[4,128,256]{2,1,0:T(8,128)S(1)} %get-tuple-element.47.speed_ref, f32[9,128,128]{2,1,0:T(8,128)S(1)} %wall.1.refs_0_, f32[2,2,144,128]{3,2,1,0:T(8,128)S(1)} %second.10.refs_1_.refs_0_.refs_2_, ...), custom_call_target="tpu_custom_call" | custom-call | flops 1100000000 | bytes 1024 | tf_op jit(solution)/shard_map/third/pallas_call | solution.py:537
  61.1 0.6 collective-permute-done.11.refs_0_
  61.7 1.9 %last.1 = f32[4,128,256]{2,1,0:T(8,128)} custom-call(s32[1]{0:T(128)} %bitcast.odd_ref, f32[8,128]{1,0:T(8,128)S(1)} %get-tuple-element.46.step, f32[4,128,256]{2,1,0:T(8,128)S(1)} %get-tuple-element.47.speed_ref, f32[9,128,128]{2,1,0:T(8,128)S(1)} %wall.1.refs_0_, f32[1,2,128,128]{3,2,1,0:T(8,128)S(1)} %collective-permute-done.11.refs_0_, ...), custom_call_target="tpu_custom_call" | custom-call | flops 1100000000 | bytes 1024 | tf_op jit(solution)/shard_map/last/pallas_call | solution.py:710
  (10 shorter events, 0.0 us)
Async XLA Ops:
  0.0 8.8 %copy-start = (s32[64,128]{1,0:T(8,128)S(1)}, s32[64,128]{1,0:T(8,128)}, u32[]{:S(2)}) copy-start(s32[64,128]{1,0:T(8,128)} %param.10) | copy-start | bytes 98308
  2.6 7.3 %collective-permute-start.2 = (f32[3,2,128,128]{3,2,1,0:T(8,128)}, f32[3,2,128,128]{3,2,1,0:T(8,128)}, u32[]{:S(2)}, u32[]{:S(2)}) collective-permute-start(f32[3,2,128,128]{3,2,1,0:T(8,128)} %get-tuple-element.41), channel_id=1, source_target_pairs={{0,1},{1,0},{2,3},{3,2},{4,5},{5,4},{6,7},{7,6},{8,9},{9,8},{10,11... | collective-permute-start | bytes 1179656 | tf_op jit(solution)/shard_map/ppermute | solution.py:555
  3.1 6.7 %collective-permute-start = (f32[8,128]{1,0:T(8,128)S(1)}, f32[8,128]{1,0:T(8,128)S(1)}, u32[]{:S(2)}, u32[]{:S(2)}) collective-permute-start(f32[8,128]{1,0:T(8,128)S(1)} %get-tuple-element.38), channel_id=1, source_target_pairs={{0,1},{1,0},{2,3},{3,2},{4,5},{5,4},{6,7},{7,6},{8,9},{9,8},{10,11... | collective-permute-start | bytes 12296 | tf_op jit(solution)/shard_map/ppermute | solution.py:564
  3.1 17.5 %collective-permute-start.5 = (f32[5,2,128,128]{3,2,1,0:T(8,128)S(1)}, f32[5,2,128,128]{3,2,1,0:T(8,128)S(1)}, u32[]{:S(2)}, u32[]{:S(2)}) collective-permute-start(f32[5,2,128,128]{3,2,1,0:T(8,128)S(1)} %get-tuple-element.44), channel_id=1, source_target_pairs={{0,15},{1,2},{2,1},{3,4},{4,3},{5,6},{6,5},{7,8},{8,7},{9,10},{10,... | collective-permute-start | bytes 1966088 | tf_op jit(solution)/shard_map/ppermute | solution.py:555
  9.8 7.2 %collective-permute-start.1 = (f32[8,128]{1,0:T(8,128)S(1)}, f32[8,128]{1,0:T(8,128)S(1)}, u32[]{:S(2)}, u32[]{:S(2)}) collective-permute-start(f32[8,128]{1,0:T(8,128)S(1)} %max.12), channel_id=1, source_target_pairs={{0,8},{1,9},{2,10},{3,11},{4,12},{5,13},{6,14},{7,15},{8,0},{9,1},... | collective-permute-start | bytes 12296 | tf_op jit(solution)/shard_map/ppermute | solution.py:564
  17.0 3.6 %collective-permute-start.3 = (f32[8,128]{1,0:T(8,128)S(1)}, f32[8,128]{1,0:T(8,128)S(1)}, u32[]{:S(2)}, u32[]{:S(2)}) collective-permute-start(f32[8,128]{1,0:T(8,128)S(1)} %max.13), channel_id=1, source_target_pairs={{0,4},{1,5},{2,6},{3,7},{4,0},{5,1},{6,2},{7,3},{8,12},{9,13},{10,... | collective-permute-start | bytes 12296 | tf_op jit(solution)/shard_map/ppermute | solution.py:564
  20.6 3.6 %collective-permute-start.4 = (f32[8,128]{1,0:T(8,128)S(1)}, f32[8,128]{1,0:T(8,128)S(1)}, u32[]{:S(2)}, u32[]{:S(2)}) collective-permute-start(f32[8,128]{1,0:T(8,128)S(1)} %max.14), channel_id=1, source_target_pairs={{0,2},{1,3},{2,0},{3,1},{4,6},{5,7},{6,4},{7,5},{8,10},{9,11},{10,... | collective-permute-start | bytes 12296 | tf_op jit(solution)/shard_map/ppermute | solution.py:564
  25.7 7.9 %collective-permute-start.7 = (f32[1,2,128,128]{3,2,1,0:T(8,128)S(1)}, f32[1,2,128,128]{3,2,1,0:T(8,128)S(1)}, u32[]{:S(2)}, u32[]{:S(2)}) collective-permute-start(f32[1,2,128,128]{3,2,1,0:T(8,128)S(1)} %get-tuple-element.54), channel_id=1, source_target_pairs={{0,1},{1,0},{2,3},{3,2},{4,5},{5,4},{6,7},{7,6},{8,9},{9,8},{10,11... | collective-permute-start | bytes 393224 | tf_op jit(solution)/shard_map/ppermute | solution.py:555
  26.9 10.1 %collective-permute-start.6 = (f32[1,2,128,128]{3,2,1,0:T(8,128)S(1)}, f32[1,2,128,128]{3,2,1,0:T(8,128)S(1)}, u32[]{:S(2)}, u32[]{:S(2)}) collective-permute-start(f32[1,2,128,128]{3,2,1,0:T(8,128)S(1)} %get-tuple-element.51), channel_id=1, source_target_pairs={{0,15},{1,2},{2,1},{3,4},{4,3},{5,6},{6,5},{7,8},{8,7},{9,10},{10,... | collective-permute-start | bytes 393224 | tf_op jit(solution)/shard_map/ppermute | solution.py:555
  34.7 3.4 %collective-permute-start.8 = (f32[1,2,128,128]{3,2,1,0:T(8,128)S(1)}, f32[1,2,128,128]{3,2,1,0:T(8,128)S(1)}, u32[]{:S(2)}, u32[]{:S(2)}) collective-permute-start(f32[1,2,128,128]{3,2,1,0:T(8,128)S(1)} %get-tuple-element.56), channel_id=1, source_target_pairs={{0,1},{1,0},{2,3},{3,2},{4,5},{5,4},{6,7},{7,6},{8,9},{9,8},{10,11... | collective-permute-start | bytes 393224 | tf_op jit(solution)/shard_map/ppermute | solution.py:555
  39.3 1.9 %collective-permute-start.10 = (f32[2,2,128,128]{3,2,1,0:T(8,128)S(1)}, f32[2,2,128,128]{3,2,1,0:T(8,128)S(1)}, u32[]{:S(2)}, u32[]{:S(2)}) collective-permute-start(f32[2,2,128,128]{3,2,1,0:T(8,128)S(1)} %get-tuple-element.59), channel_id=1, source_target_pairs={{0,1},{1,0},{2,3},{3,2},{4,5},{5,4},{6,7},{7,6},{8,9},{9,8},{10,11... | collective-permute-start | bytes 786440 | tf_op jit(solution)/shard_map/ppermute | solution.py:555
  39.9 10.0 %collective-permute-start.9 = (f32[3,2,128,128]{3,2,1,0:T(8,128)S(1)}, f32[3,2,128,128]{3,2,1,0:T(8,128)S(1)}, u32[]{:S(2)}, u32[]{:S(2)}) collective-permute-start(f32[3,2,128,128]{3,2,1,0:T(8,128)S(1)} %get-tuple-element.57), channel_id=1, source_target_pairs={{0,15},{1,2},{2,1},{3,4},{4,3},{5,6},{6,5},{7,8},{8,7},{9,10},{10,... | collective-permute-start | bytes 1179656 | tf_op jit(solution)/shard_map/ppermute | solution.py:555
  44.5 1.4 %collective-permute-start.12 = (f32[1,2,128,128]{3,2,1,0:T(8,128)S(1)}, f32[1,2,128,128]{3,2,1,0:T(8,128)S(1)}, u32[]{:S(2)}, u32[]{:S(2)}) collective-permute-start(f32[1,2,128,128]{3,2,1,0:T(8,128)S(1)} %get-tuple-element.68), channel_id=1, source_target_pairs={{0,1},{1,0},{2,3},{3,2},{4,5},{5,4},{6,7},{7,6},{8,9},{9,8},{10,11... | collective-permute-start | bytes 393224 | tf_op jit(solution)/shard_map/ppermute | solution.py:555
  46.9 13.1 %collective-permute-start.13 = (f32[1,2,128,128]{3,2,1,0:T(8,128)S(1)}, f32[1,2,128,128]{3,2,1,0:T(8,128)S(1)}, u32[]{:S(2)}, u32[]{:S(2)}) collective-permute-start(f32[1,2,128,128]{3,2,1,0:T(8,128)S(1)} %get-tuple-element.70), channel_id=1, source_target_pairs={{0,1},{1,0},{2,3},{3,2},{4,5},{5,4},{6,7},{7,6},{8,9},{9,8},{10,11... | collective-permute-start | bytes 393224 | tf_op jit(solution)/shard_map/ppermute | solution.py:555
  54.4 7.3 %collective-permute-start.11 = (f32[1,2,128,128]{3,2,1,0:T(8,128)S(1)}, f32[1,2,128,128]{3,2,1,0:T(8,128)S(1)}, u32[]{:S(2)}, u32[]{:S(2)}) collective-permute-start(f32[1,2,128,128]{3,2,1,0:T(8,128)S(1)} %get-tuple-element.63), channel_id=1, source_target_pairs={{0,15},{1,2},{2,1},{3,4},{4,3},{5,6},{6,5},{7,8},{8,7},{9,10},{10,... | collective-permute-start | bytes 393224 | tf_op jit(solution)/shard_map/ppermute | solution.py:555

commit v4 on v3

--- a/solution.py
+++ b/solution.py
@@ -102,8 +102,7 @@
 
 def from_above(pair):
     turned = [pltpu.roll(v, LANES - 1, 1) for v in pair]
-    last = lane_of(pair[0]) == LANES - 1
-    return [jnp.where(last, turned[1], turned[0]), jnp.where(last, turned[0], turned[1])]
+    return [jnp.where(lane_of(pair[0]) == LANES - 1, turned[1], turned[0]), turned[1]]
 
 
 def from_below(pair):
@@ -135,27 +134,26 @@
             target.write(h, r, source.read(h, r))
 
 
-def fill(source, field, start, way, begin, end, padded):
-    rows = field.shape[2] - 2 * PAD
-
-    @pl.loop(begin, end)
-    def _(k):
-        target = Layer(field, start + way * k)
-        copy_layer(Layer(source, k, padded), target, rows)
-        target.wrap()
+def padded_halo(source, field, numbers):
+    found = {}
+    for k, p in numbers:
+        found[p] = Layer(field, p)
+        copy_layer(Layer(source, k, False), found[p], field.shape[2] - 2 * PAD)
+        found[p].wrap()
+    return found
 
 
 def normals(before, here, after, wall, row):
     centre = [here.read(h, row) for h in HALVES]
     n_x = [before.read(h, row) - after.read(h, row) for h in HALVES]
     n_y = [here.read(h, row - 1) - here.read(h, row + 1) for h in HALVES]
-    above = from_above(centre)
-    below = from_below(centre)
     lane = lane_of(centre[0])
-    above[1] = jnp.where(lane == LANES - 1, centre[1], above[1])
-    n_z = [below[h] - above[h] for h in HALVES]
+    up = [pltpu.roll(v, LANES - 1, 1) for v in centre]
+    down = [pltpu.roll(v, 1, 1) for v in centre]
+    top, bottom = lane == LANES - 1, lane == 0
+    n_z = [down[0] - jnp.where(top, up[1], up[0]), jnp.where(bottom, down[0], down[1]) - jnp.where(top, centre[1], up[1])]
     contact = wall[pl.ds(row, ROWS), :] * (jnp.abs(n_x[0]) + jnp.abs(n_y[0]))
-    n_z[0] = jnp.where(lane == 0, contact, n_z[0])
+    n_z[0] = jnp.where(bottom, contact, n_z[0])
     return centre, n_x, n_y, n_z
 
 
@@ -171,14 +169,14 @@
     return ref[index, pl.ds(row, ROWS), half * LANES : (half + 1) * LANES]
 
 
-def begin_kernel(odd_ref, fraction_in, mask_in, *refs):
-    speeds_in, (*speeds, peak, state, fraction, mask, sems) = refs[:3], refs[3:]
+def begin_kernel(odd_ref, fraction_in, mask_in, class_in, *refs):
+    speeds_in, (*speeds, peak, state, classes, fraction, mask, sems) = refs[:3], refs[3:]
     odd = odd_ref[0] == 1
     count, rows, width = fraction.shape
-    sources = (*speeds_in, fraction_in, mask_in)
+    sources = (*speeds_in, fraction_in, mask_in, class_in)
     copies = [
         pltpu.make_async_copy(source, target, sems.at[n])
-        for n, (source, target) in enumerate(zip(sources, (*speeds, fraction, mask)))
+        for n, (source, target) in enumerate(zip(sources, (*speeds, fraction, mask, classes)))
     ]
     for copy in copies:
         copy.start()
@@ -197,6 +195,7 @@
                 value = jnp.where(natural(mask, index, h, r) == 1, 1.0, natural(fraction, index, h, r))
                 Layer(state, k).write(h, r, value)
         Layer(state, k).wrap()
+    copies[5].wait()
 
 
 def first_send_kernel(odd_ref, first, state, send_outer, send_inner):
@@ -214,15 +213,18 @@
             Layer(send_inner, INNER, False).write(h, r, natural(first, count - 1, h, r))
 
 
-def wall_kernel(where_ref, cosine, out, turned):
-    odd = where_ref[0] == 1
-    total = cosine.shape[0]
+def wall_kernel(classes, out, turned):
+    device = lax.axis_index("gx")
+    odd = lax.rem(device, 2) == 1
+    total = classes.shape[0]
     layers = out.shape[0]
     count = layers - OUTER - INNER
     turned[...] = jnp.zeros(turned.shape, jnp.float32)
     for p in range(1, layers - 1):
-        row = lax.rem(where_ref[1] + own_index(odd, p, count) + total, total)
-        turned[pl.ds(p, 1), :] = cosine[pl.ds(row, 1), :]
+        row = lax.rem(device * count + own_index(odd, p, count) + total, total)
+        turned[pl.ds(p, 1), :] = classes[pl.ds(row, 1), :].astype(jnp.float32)
+    used = -(-layers // 8) * 8
+    turned[:used, :] = jnp.cos(jnp.pi * (turned[:used, :] + 1.0) / (WALL_CLASSES + 1))
     columns = jnp.transpose(turned[...])
     for p in range(1, layers - 1):
         out[p] = pltpu.roll(columns, LANES - p, 1)
@@ -231,64 +233,61 @@
 KEPT = 9
 
 
-def prepare_kernel(odd_ref, *refs, kinds, faces, count):
-    given = dict(zip(kinds, refs))
-    wall = given["wall"]
-    out, field, n_s, n_a, n_b = refs[len(kinds) :]
-    rows = out.shape[2]
-    odd = odd_ref[0] == 1
-    sign = jnp.where(odd, -1.0, 1.0)
-    start, stop = faces[0], faces[-1] + 1
-    lowest, highest = start - 1, stop + 1
-    for kind, first_layer, way, number, is_padded in (
-        ("outer", OUTER - 1, -1, OUTER, False),
-        ("own", OUTER, 1, count, True),
-        ("inner", OUTER + count, 1, INNER, False),
-    ):
-        if kind not in given:
-            continue
-        used = [k for k in range(number) if lowest <= first_layer + way * k <= highest]
-        if used:
-            fill(given[kind], field, first_layer, way, used[0], used[-1] + 1, is_padded)
-
-    @pl.loop(start, stop + 1)
-    def _(i):
+def face_work(layers, wall, slopes, faces, rows, work):
+    n_s, n_a, n_b = slopes
+
+    def slope(i):
         for r in range(0, rows, ROWS):
-            _, n_x, n_y, n_z = normals(Layer(field, i - 1), Layer(field, i), Layer(field, i + 1), wall.at[i], r)
+            _, n_x, n_y, n_z = normals(layers[i - 1], layers[i], layers[i + 1], wall.at[i], r)
             for h in HALVES:
                 Layer(n_s, i, False).write(h, r, n_x[h])
                 Layer(n_a, i, False).write(h, r, soft(n_y[h]))
                 Layer(n_b, i, False).write(h, r, soft(n_z[h]))
 
-    speed = KEPT - 1
-    for k, face in enumerate(faces):
+    slope(faces[0])
+    for i in faces:
+        slope(i + 1)
+        sides = [(layers[i], layers[i + 1])] + [(Layer(n, i, False), Layer(n, i + 1, False)) for n in slopes]
         for r in range(0, rows, ROWS):
             for h in HALVES:
-                if face == OUTER - 2:
-                    value = Layer(given["outer"], OUTER, False).read(h, r)
-                elif face == OUTER - 1:
-                    value = natural(given["first"], count - 1, h, r)
-                    value = jnp.where(odd, value, Layer(given["outer"], OUTER + 1, False).read(h, r))
-                elif face == OUTER + count - 1:
-                    value = natural(given["first"], count - 1, h, r)
-                    value = jnp.where(odd, Layer(given["inner"], INNER, False).read(h, r), value)
-                else:
-                    value = natural(given["first"], jnp.where(odd, OUTER + count - 2 - face, face - OUTER), h, r)
-                Layer(out, k * KEPT + speed, False).write(h, r, value * sign)
-
-    @pl.loop(0, len(faces))
-    def _(k):
-        i = start + k
-        for r in range(0, rows, ROWS):
-            for h in HALVES:
-                ahead = Layer(out, k * KEPT + speed, False).read(h, r) > 0.0
-
-                def donor(ref, padded=False):
-                    return jnp.where(ahead, Layer(ref, i, padded).read(h, r), Layer(ref, i + 1, padded).read(h, r))
-
-                kept = prepare(donor(field, True), donor(n_s), donor(n_a), donor(n_b), ahead)
-                for n, value in enumerate(kept):
-                    Layer(out, k * KEPT + n, False).write(h, r, value)
+
+                def donor(ahead):
+                    return [jnp.where(ahead, low.read(h, r), high.read(h, r)) for low, high in sides]
+
+                work(i, h, r, donor)
+
+
+def prepare_kernel(odd_ref, *refs, kinds, faces, count):
+    given = dict(zip(kinds, refs))
+    out, field, *slopes = refs[len(kinds) :]
+    rows = out.shape[2]
+    odd = odd_ref[0] == 1
+    sign = jnp.where(odd, -1.0, 1.0)
+    layers = {OUTER + k: Layer(given["own"], k) for k in range(count)}
+    needed = range(faces[0] - 1, faces[-1] + 3)
+    for kind, first_layer, way, number in (("outer", OUTER - 1, -1, OUTER), ("inner", OUTER + count, 1, INNER)):
+        if kind in given:
+            numbers = [(k, first_layer + way * k) for k in range(number) if first_layer + way * k in needed]
+            layers.update(padded_halo(given[kind], field, numbers))
+
+    def work(face, h, r, donor):
+        if face == OUTER - 2:
+            speed = Layer(given["outer"], OUTER, False).read(h, r)
+        elif face == OUTER - 1:
+            speed = natural(given["first"], count - 1, h, r)
+            speed = jnp.where(odd, speed, Layer(given["outer"], OUTER + 1, False).read(h, r))
+        elif face == OUTER + count - 1:
+            speed = natural(given["first"], count - 1, h, r)
+            speed = jnp.where(odd, Layer(given["inner"], INNER, False).read(h, r), speed)
+        else:
+            speed = natural(given["first"], jnp.where(odd, OUTER + count - 2 - face, face - OUTER), h, r)
+        speed = speed * sign
+        ahead = speed > 0.0
+        first_kept = (face - faces[0]) * KEPT
+        for n, value in enumerate((*prepare(*donor(ahead), ahead), speed)):
+            Layer(out, first_kept + n, False).write(h, r, value)
+
+    face_work(layers, given["wall"], slopes, faces, rows, work)
 
 
 def finish_faces(kept, step, flux, moved, start):
@@ -330,62 +329,43 @@
     copy_layer(Layer(out, out.shape[0] - 1), Layer(send, 0, False), rows)
 
 
-def first_fluxes(field, wall, moved, n_s, n_a, n_b, flux, start, stop):
-    rows = flux.shape[2]
-
-    @pl.loop(start, stop + 1)
-    def _(i):
-        for r in range(0, rows, ROWS):
-            _, n_x, n_y, n_z = normals(Layer(field, i - 1), Layer(field, i), Layer(field, i + 1), wall.at[i], r)
-            for h in HALVES:
-                Layer(n_s, i, False).write(h, r, n_x[h])
-                Layer(n_a, i, False).write(h, r, soft(n_y[h]))
-                Layer(n_b, i, False).write(h, r, soft(n_z[h]))
-
-    @pl.loop(start, stop)
-    def _(i):
-        for r in range(0, rows, ROWS):
-            for h in HALVES:
-                speed = Layer(moved, i - 1, False).read(h, r)
-                ahead = speed > 0.0
-
-                def donor(ref, padded=False):
-                    return jnp.where(ahead, Layer(ref, i, padded).read(h, r), Layer(ref, i + 1, padded).read(h, r))
-
-                through = face_flux(donor(field, True), donor(n_s), donor(n_a), donor(n_b), speed)
-                Layer(flux, i - 1, False).write(h, r, through)
-
-
-def inside_kernel(edge, middle, last, inner, moved, wall, out, flux_out, send, field, n_s, n_a, n_b, flux):
+def first_fluxes(layers, wall, moved, slopes, flux, faces):
+    def work(i, h, r, donor):
+        speed = Layer(moved, i - 1, False).read(h, r)
+        Layer(flux, i - 1, False).write(h, r, face_flux(*donor(speed > 0.0), speed))
+
+    face_work(layers, wall, slopes, faces, flux.shape[2], work)
+
+
+def own_layers(*refs):
+    found = [Layer(ref, k) for ref in refs for k in range(ref.shape[0])]
+    return {OUTER + k: layer for k, layer in enumerate(found)}
+
+
+def inside_kernel(edge, middle, last, inner, moved, wall, out, flux_out, send, field, *more):
+    *slopes, flux = more
     rows = moved.shape[2]
-    count = middle.shape[0] + 2
-    fill(edge, field, OUTER, 1, 0, 1, True)
-    fill(middle, field, OUTER + 1, 1, 0, count - 2, True)
-    fill(last, field, OUTER + count - 1, 1, 0, 1, True)
-    fill(inner, field, OUTER + count, 1, 0, INNER, False)
-    first_fluxes(field, wall, moved, n_s, n_a, n_b, flux, OUTER + 1, OUTER + count)
+    layers = own_layers(edge, middle, last)
+    count = len(layers)
+    layers.update(padded_halo(inner, field, [(k, OUTER + count + k) for k in range(INNER)]))
+    first_fluxes(layers, wall, moved, slopes, flux, range(OUTER + 1, OUTER + count))
     copy_layer(Layer(flux, OUTER, False), Layer(flux_out, 0, False), rows)
-
-    @pl.loop(OUTER + 2, OUTER + count)
-    def _(i):
-        update(Layer(out, i - OUTER - 2), Layer(field, i), Layer(flux, i - 2, False), Layer(flux, i - 1, False), rows)
-        Layer(out, i - OUTER - 2).wrap()
-
+    for i in range(OUTER + 2, OUTER + count):
+        target = Layer(out, i - OUTER - 2)
+        update(target, layers[i], Layer(flux, i - 2, False), Layer(flux, i - 1, False), rows)
+        target.wrap()
     copy_layer(Layer(out, count - 3), Layer(send, 0, False), rows)
 
 
-def outside_kernel(edge, middle, last, outer, moved, wall, flux_above, above, out, field, n_s, n_a, n_b, flux):
+def outside_kernel(edge, middle, last, outer, moved, wall, flux_above, above, out, field, *more):
+    *slopes, flux = more
     rows = moved.shape[2]
-    count = middle.shape[0] + 2
-    fill(outer, field, OUTER - 1, -1, 0, OUTER, False)
-    fill(edge, field, OUTER, 1, 0, 1, True)
-    fill(middle, field, OUTER + 1, 1, 0, count - 2, True)
-    if count < 4:
-        fill(last, field, OUTER + count - 1, 1, 0, 1, True)
-    first_fluxes(field, wall, moved, n_s, n_a, n_b, flux, OUTER - 2, OUTER + 1)
+    layers = own_layers(edge, middle, last)
+    layers.update(padded_halo(outer, field, [(k, OUTER - 1 - k) for k in range(OUTER)]))
+    first_fluxes(layers, wall, moved, slopes, flux, range(OUTER - 2, OUTER + 1))
     fluxes = [Layer(flux, k, False) for k in range(OUTER)] + [Layer(flux_above, 0, False)]
     for k, target in enumerate((Layer(above, 0, False), Layer(out, 0), Layer(out, 1))):
-        update(target, Layer(field, OUTER - 1 + k), fluxes[k], fluxes[k + 1], rows)
+        update(target, layers[OUTER - 1 + k], fluxes[k], fluxes[k + 1], rows)
         if k > 0:
             target.wrap()
 
@@ -423,10 +403,9 @@
         through = []
         for h in HALVES:
             moved = speed(h, r)
-            if h == 1:
-                moved = jnp.where(lane == LANES - 1, 0.0, moved)
             ahead = moved > 0.0
             through.append(face_flux(*[jnp.where(ahead, f[h], a[h]) for f, a in zip(fields, above)], moved))
+        through[1] = jnp.where(lane == LANES - 1, 0.0, through[1])
         below = from_below(through)
         for h in HALVES:
             value = jnp.clip(centre[h] - through[h] + below[h], 0.0, 1.0)
@@ -573,7 +552,6 @@
     own_end = OUTER + count
     device = lax.axis_index("gx")
     odd = (device % 2).astype(jnp.int32).reshape(1)
-    place = jnp.stack([device % 2, device * count]).astype(jnp.int32)
 
     def padded(n):
         return (n, 2, rows + 2 * PAD, LANES)
@@ -582,17 +560,17 @@
         return (n, 2, rows, LANES)
 
     natural_shape = (count, rows, width)
-    first, second, third, peak, state = call(
+    first, second, third, peak, state, classes = call(
         begin_kernel,
         "begin",
         [held(natural_shape)] * 3
-        + [held((8, LANES)), held(padded(count))],
+        + [held((8, LANES)), held(padded(count)), pltpu.VMEM(wall_class.shape, jnp.int32)],
         [odd],
-        [fraction, seed_mask, first, second, third],
+        [fraction, seed_mask, wall_class, first, second, third],
         [
             pltpu.VMEM(natural_shape, jnp.float32),
             pltpu.VMEM(natural_shape, jnp.int32),
-            pltpu.SemaphoreType.DMA((5,)),
+            pltpu.SemaphoreType.DMA((6,)),
         ],
         resident=False,
     )
@@ -600,8 +578,9 @@
         first_send_kernel, "first_send", [held(plain(OUTER + 2)), held(plain(INNER + 1))], [odd], [first, state]
     )
     inner = swap(send_inner, False)
-    cosine = jnp.cos(jnp.pi * (wall_class.astype(jnp.float32) + 1.0) / (WALL_CLASSES + 1))
-    (wall,) = call(wall_kernel, "wall", [held((layers, rows, LANES))], [place], [cosine], [pltpu.VMEM((LANES, rows), jnp.float32)])
+    (wall,) = call(
+        wall_kernel, "wall", [held((layers, rows, LANES))], [], [classes], [pltpu.VMEM((LANES, rows), jnp.float32)]
+    )
     slopes = [pltpu.VMEM(padded(layers), jnp.float32)] + [pltpu.VMEM(plain(layers), jnp.float32)] * 3
 
     def prepare_call(faces, **given):
@@ -612,7 +591,7 @@
             [odd],
             list(given.values()),
             slopes,
-            faces=len(faces),
+            faces=0.02,
         )[0]
 
     size = lax.axis_size("gx")
@@ -636,6 +615,22 @@
     )
     swept, places = [above, own], [(OUTER - 1, False), (OUTER, True)]
     line = [pltpu.VMEM(padded(1), jnp.float32)] * 4
+    def second_call(work, fields, places, send):
+        return call(
+            functools.partial(second_kernel, places=places, work=work, send_last=work[0] if send else None),
+            "second",
+            [held(padded(len(work)))] + ([held(plain(1))] if send else []),
+            [odd],
+            [step, second, wall, *fields],
+            line,
+            faces=0.1 if own_end - 1 in work else len(work),
+        )
+
+    def last_second(part, place, send_inner):
+        inner = swap(send_inner, False)
+        last, send_inner = second_call((own_end - 1,), [part, inner], [place, (own_end, False)], True)
+        return last, swap(send_inner, False)
+
     for turn in range(STEPS):
         final = turn == STEPS - 1
         if turn > 0:
@@ -647,8 +642,10 @@
                 [],
                 [*own, inner, moved, wall],
                 [*slopes, flux],
-                faces=count - 1,
+                faces=0.1,
             )
+            last, inner = last_second(inside, (OUTER + 2, True), send_inner)
+            outer, last = lax.optimization_barrier((outer, last))
             above, outside = call(
                 outside_kernel,
                 "outside",
@@ -660,21 +657,8 @@
             )
             swept = [above, outside, inside]
             places = [(OUTER - 1, False), (OUTER, True), (OUTER + 2, True)]
-        inner = swap(send_inner, False)
-
-        def second_call(work, fields, places, send):
-            return call(
-                functools.partial(second_kernel, places=places, work=work, send_last=work[0] if send else None),
-                "second",
-                [held(padded(len(work)))] + ([held(plain(1))] if send else []),
-                [odd],
-                [step, second, wall, *fields],
-                line,
-                faces=len(work),
-            )
-
-        last, send_inner = second_call((own_end - 1,), [swept[-1], inner], [places[-1], (own_end, False)], True)
-        inner = swap(send_inner, False)
+        else:
+            last, inner = last_second(swept[-1], places[-1], send_inner)
         edge, send_outer = second_call((OUTER,), swept[:2], places[:2], True)
         after = lax.optimization_barrier((edge, *swept[1:]))[1:]
         (middle,) = second_call(tuple(range(OUTER + 1, own_end - 1)), after, places[1:], False)
@@ -695,13 +679,16 @@
             )[0]
 
         middle_new = third_call(inside_work[:-1], fields[:-1], starts[:-1])
-        last_new = third_call(inside_work[-1:], fields[1:], starts[1:])
         if final:
+            last_new = third_call(inside_work[-1:], fields[1:], starts[1:])
             return last_call(odd, step, third, wall, edge_fields, edge_starts, [middle_new, last_new], natural_shape)
         edge_new = third_call((OUTER,), edge_fields, edge_starts)
+        (send_outer,) = call(pack_kernel, "pack", [held(plain(OUTER))], [], [edge_new, middle_new])
+        outer = swap(send_outer, True)
+        _, *after = lax.optimization_barrier((send_outer, *fields[1:]))
+        last_new = third_call(inside_work[-1:], after, starts[1:])
         own = [edge_new, middle_new, last_new]
-        send_outer, send_inner = call(pack_kernel, "pack", [held(plain(OUTER)), held(plain(INNER))], [], own)
-        outer = swap(send_outer, True)
+        (send_inner,) = call(pack_kernel, "pack", [held(plain(INNER))], [], [last_new, middle_new])
         inner = swap(send_inner, False)
 
 
@@ -719,13 +706,12 @@
     )(odd, *arrays)
 
 
-def pack_kernel(edge, middle, last, send_outer, send_inner):
-    rows = send_outer.shape[2]
-    own = [Layer(ref, k) for ref in (edge, middle, last) for k in range(ref.shape[0])]
-    for k in range(OUTER):
-        copy_layer(own[k], Layer(send_outer, k, False), rows)
-    for k in range(INNER):
-        copy_layer(own[-1 - k], Layer(send_inner, k, False), rows)
+def pack_kernel(edge, middle, send):
+    rows = send.shape[2]
+    copy_layer(Layer(edge, 0), Layer(send, 0, False), rows)
+    number = send.shape[0] - 1
+    for k in range(number):
+        copy_layer(Layer(middle, k if number == OUTER - 1 else middle.shape[0] - 1 - k), Layer(send, 1 + k, False), rows)
 
 
 def solution(mesh):

time: 64 us -> 61.7 us (0.964)
  Pallas kernels: 37.1 us -> 32.3 us
  waiting for transfers between devices: 9.62 us -> 12.8 us
    pallas_call x21 -> x22, Pallas kernels: 35.2 us -> 30.4 us  [call(): pl.pallas_call(kernel, out_shape=outs, in_specs=[IN_SMEM] * len(scalars)...]
    ppermute x4, waiting for transfers between devices: 5.2 us -> 8.16 us  [largest_round(): received = lax.ppermute(array, 'gx', pairs)]
    ppermute x10, starting transfers between devices: 14.9 us -> 14.1 us  [swap(): return lax.ppermute(array, 'gx', pairs)]
  transfers between devices with their start and end apart: 14 -> 14, of which waited for: 6 -> 7; matrix products, arithmetic and copies ran while one was open for 0% -> 0% of each run, Pallas kernels for 47% -> 42%
where the time goes in v4:
time: 61.7 us; the launch traced here: 61.5 us
  Pallas kernels  32.3 us (52%)
  starting transfers between devices  16.1 us (26%)
  waiting for transfers between devices  12.8 us (21%)
    pallas_call x22, Pallas kernels, call(): pl.pallas_call(kernel, out_shape=outs, in_specs=[IN_SMEM] * len(scalars)...  30.4 us
    ppermute x10, starting transfers between devices, swap(): return lax.ppermute(array, 'gx', pairs)  14.1 us
    ppermute x4, waiting for transfers between devices, largest_round(): received = lax.ppermute(array, 'gx', pairs)  8.16 us
    ppermute x10, waiting for transfers between devices, swap(): return lax.ppermute(array, 'gx', pairs)  4.65 us
    ppermute x4, starting transfers between devices, largest_round(): received = lax.ppermute(array, 'gx', pairs)  2 us
    pallas_call x1, Pallas kernels, last_call(): pl.pallas_call(functools.partial(last_kernel, places=places), out_shape=j...  1.85 us
  transfers between devices with their start and end apart: 14, of which 7 were waited for; matrix products, arithmetic and copies ran while one was open for 0% of the time, Pallas kernels for 42%

profile of v4, /device:TPU:0, one launch (start us, length us, event | category | flops | bytes accessed | tf_op | source)
XLA Modules:
  0.0 61.5 jit_solution(10592021154423103995)
XLA Ops:
  0.0 1.8 %begin.1 = (f32[4,128,256]{2,1,0:T(8,128)S(1)}, f32[4,128,256]{2,1,0:T(8,128)S(1)}, f32[4,128,256]{2,1,0:T(8,128)S(1)}, f32[8,128]{1,0:T(8,128)S(1)}, f32[4,2,14...) custom-call(s32[1]{0:T(128)} %bitcast.odd_ref, f32[4,128,256]{2,1,0:T(8,128)} %fraction_in.1, s32[4,128,256]{2,1,0:T(8,128)} %mask_in.1, ...), custom_call_target="tpu_custom_call" | custom-call | flops 110000000 | bytes 1024 | tf_op jit(solution)/shard_map/begin/pallas_call | solution.py:516
  1.8 0.1 first_send.1
  1.9 5.5 %collective-permute-start.5 = (f32[5,2,128,128]{3,2,1,0:T(8,128)S(1)}, f32[5,2,128,128]{3,2,1,0:T(8,128)S(1)}, u32[]{:S(2)}, u32[]{:S(2)}) collective-permute-start(f32[5,2,128,128]{3,2,1,0:T(8,128)S(1)} %get-tuple-element.49), channel_id=1, source_target_pairs={{0,15},{1,2},{2,1},{3,4},{4,3},{5,6},{6,5},{7,8},{8,7},{9,10},{10,... | collective-permute-start | bytes 1966088 | tf_op jit(solution)/shard_map/ppermute | solution.py:534
  7.4 0.0 collective-permute-start.2
  7.4 0.5 collective-permute-start
  7.9 1.2 %collective-permute-done = f32[8,128]{1,0:T(8,128)S(1)} collective-permute-done((f32[8,128]{1,0:T(8,128)S(1)}, f32[8,128]{1,0:T(8,128)S(1)}, u32[]{:S(2)}, u32[]{:S(2)}) %collective-permute-start) | collective-permute-done | bytes 4128 | tf_op jit(solution)/shard_map/ppermute | solution.py:543
  9.1 0.0 collective-permute-start.1
  9.1 0.4 wall.1.refs_0_
  9.5 0.0 collective-permute-done.2.refs_3_
  9.5 1.6 %prepare.3.refs_2_ = f32[18,2,128,128]{3,2,1,0:T(8,128)S(1)} custom-call(s32[1]{0:T(128)} %bitcast.odd_ref, f32[9,128,128]{2,1,0:T(8,128)S(1)} %wall.1.refs_0_, f32[4,128,256]{2,1,0:T(8,128)S(1)} %get-tuple-element.44.first.refs_1_, f32[4,2,144,128]{3,2,1,0:T(8,128)S(1)} %get-tuple-element.45.state.refs_2_.refs_3_, ...), custom_call_target="tpu_custom_call" | custom-call | flops 22000000 | bytes 1024 | tf_op jit(solution)/shard_map/prepare/pallas_call | solution.py:516
  11.1 4.5 %collective-permute-done.1 = f32[8,128]{1,0:T(8,128)S(1)} collective-permute-done((f32[8,128]{1,0:T(8,128)S(1)}, f32[8,128]{1,0:T(8,128)S(1)}, u32[]{:S(2)}, u32[]{:S(2)}) %collective-permute-start.1) | collective-permute-done | bytes 4128 | tf_op jit(solution)/shard_map/ppermute | solution.py:543
  15.7 1.5 %collective-permute-start.3 = (f32[8,128]{1,0:T(8,128)S(1)}, f32[8,128]{1,0:T(8,128)S(1)}, u32[]{:S(2)}, u32[]{:S(2)}) collective-permute-start(f32[8,128]{1,0:T(8,128)S(1)} %max.13), channel_id=1, source_target_pairs={{0,4},{1,5},{2,6},{3,7},{4,0},{5,1},{6,2},{7,3},{8,12},{9,13},{10,... | collective-permute-start | bytes 12296 | tf_op jit(solution)/shard_map/ppermute | solution.py:543
  17.1 0.9 %prepare.4.refs_1_ = f32[9,2,128,128]{3,2,1,0:T(8,128)S(1)} custom-call(s32[1]{0:T(128)} %bitcast.odd_ref, f32[9,128,128]{2,1,0:T(8,128)S(1)} %wall.1.refs_0_, f32[4,128,256]{2,1,0:T(8,128)S(1)} %get-tuple-element.44.first.refs_1_, f32[4,2,144,128]{3,2,1,0:T(8,128)S(1)} %get-tuple-element.45.state.refs_2_.refs_3_, ...), custom_call_target="tpu_custom_call" | custom-call | flops 22000000 | bytes 1024 | tf_op jit(solution)/shard_map/prepare/pallas_call | solution.py:516
  18.1 1.2 %collective-permute-done.3 = f32[8,128]{1,0:T(8,128)S(1)} collective-permute-done((f32[8,128]{1,0:T(8,128)S(1)}, f32[8,128]{1,0:T(8,128)S(1)}, u32[]{:S(2)}, u32[]{:S(2)}) %collective-permute-start.3) | collective-permute-done | bytes 4128 | tf_op jit(solution)/shard_map/ppermute | solution.py:543
  19.3 0.0 collective-permute-start.4
  19.3 0.0 collective-permute-done.5.refs_3_.refs_4_
  19.3 2.4 %prepare.5.refs_0_ = f32[27,2,128,128]{3,2,1,0:T(8,128)S(1)} custom-call(s32[1]{0:T(128)} %bitcast.odd_ref, f32[9,128,128]{2,1,0:T(8,128)S(1)} %wall.1.refs_0_, f32[4,128,256]{2,1,0:T(8,128)S(1)} %get-tuple-element.44.first.refs_1_, f32[4,2,144,128]{3,2,1,0:T(8,128)S(1)} %get-tuple-element.45.state.refs_2_.refs_3_, ...), custom_call_target="tpu_custom_call" | custom-call | flops 22000000 | bytes 1024 | tf_op jit(solution)/shard_map/prepare/pallas_call | solution.py:516
  21.6 1.2 %collective-permute-done.4 = f32[8,128]{1,0:T(8,128)S(1)} collective-permute-done((f32[8,128]{1,0:T(8,128)S(1)}, f32[8,128]{1,0:T(8,128)S(1)}, u32[]{:S(2)}, u32[]{:S(2)}) %collective-permute-start.4) | collective-permute-done | bytes 4128 | tf_op jit(solution)/shard_map/ppermute | solution.py:543
  22.9 1.5 %finish.1 = (f32[4,2,144,128]{3,2,1,0:T(8,128)S(1)}, f32[1,2,128,128]{3,2,1,0:T(8,128)S(1)}, f32[6,2,128,128]{3,2,1,0:T(8,128)S(1)}, f32[8,128]{1,0:T(8,128)S(1)}, f32[1,2,128,128]{3,2,1,0:T(8,128)S(1)}) custom-call(f32[8,128]{1,0:T(8,128)S(1)} %max.15.peak, f32[27,2,128,128]{3,2,1,0:T(8,128)S(1)} %prepare.5.refs_0_, f32[9,2,128,128]{3,2,1,0:T(8,128)S(1)} %prepare.4.refs_1_, ...), custom_call_target="tpu_custom_call" | custom-call | flops 1100000000 | bytes 1024 | tf_op jit(solution)/shard_map/finish/pallas_call | solution.py:516
  24.4 0.1 collective-permute-start.7
  24.5 1.1 %second.6 = (f32[1,2,144,128]{3,2,1,0:T(8,128)S(1)}, f32[1,2,128,128]{3,2,1,0:T(8,128)S(1)}) custom-call(s32[1]{0:T(128)} %bitcast.odd_ref, f32[8,128]{1,0:T(8,128)S(1)} %get-tuple-element.51.step, f32[4,128,256]{2,1,0:T(8,128)S(1)} %get-tuple-element.53.speed_ref, f32[9,128,128]{2,1,0:T(8,128)S(1)} %wall.1.refs_0_, ...), custom_call_target="tpu_custom_call" | custom-call | flops 1100000000 | bytes 1024 | tf_op jit(solution)/shard_map/second/pallas_call | solution.py:516
  25.5 4.6 %collective-permute-start.6 = (f32[1,2,128,128]{3,2,1,0:T(8,128)S(1)}, f32[1,2,128,128]{3,2,1,0:T(8,128)S(1)}, u32[]{:S(2)}, u32[]{:S(2)}) collective-permute-start(f32[1,2,128,128]{3,2,1,0:T(8,128)S(1)} %get-tuple-element.56), channel_id=1, source_target_pairs={{0,15},{1,2},{2,1},{3,4},{4,3},{5,6},{6,5},{7,8},{8,7},{9,10},{10,... | collective-permute-start | bytes 393224 | tf_op jit(solution)/shard_map/ppermute | solution.py:534
  30.2 2.0 %second.7.refs_2_.refs_1_.refs_0_ = f32[2,2,144,128]{3,2,1,0:T(8,128)S(1)} custom-call(s32[1]{0:T(128)} %bitcast.odd_ref, f32[8,128]{1,0:T(8,128)S(1)} %get-tuple-element.51.step, f32[4,128,256]{2,1,0:T(8,128)S(1)} %get-tuple-element.53.speed_ref, f32[9,128,128]{2,1,0:T(8,128)S(1)} %wall.1.refs_0_, f32[4,2,144,128]{3,2,1,0:T(8,128)S(1)} %get-tuple-element.58.refs_1_.refs_0_), custom_call_target="tpu_custom_call" | custom-call | flops 2200000000 | bytes 1024 | tf_op jit(solution)/shard_map/second/pallas_call | solution.py:516
  32.2 1.1 %second.8 = (f32[1,2,144,128]{3,2,1,0:T(8,128)S(1)}, f32[1,2,128,128]{3,2,1,0:T(8,128)S(1)}) custom-call(s32[1]{0:T(128)} %bitcast.odd_ref, f32[8,128]{1,0:T(8,128)S(1)} %get-tuple-element.51.step, f32[4,128,256]{2,1,0:T(8,128)S(1)} %get-tuple-element.53.speed_ref, f32[9,128,128]{2,1,0:T(8,128)S(1)} %wall.1.refs_0_, ...), custom_call_target="tpu_custom_call" | custom-call | flops 110000000 | bytes 1024 | tf_op jit(solution)/shard_map/second/pallas_call | solution.py:516
  33.2 0.1 collective-permute-start.8
  33.3 2.1 %third.6.middle = f32[2,2,144,128]{3,2,1,0:T(8,128)S(1)} custom-call(s32[1]{0:T(128)} %bitcast.odd_ref, f32[8,128]{1,0:T(8,128)S(1)} %get-tuple-element.51.step, f32[4,128,256]{2,1,0:T(8,128)S(1)} %get-tuple-element.52.speed_ref, f32[9,128,128]{2,1,0:T(8,128)S(1)} %wall.1.refs_0_, f32[1,2,144,128]{3,2,1,0:T(8,128)S(1)} %get-tuple-element.57.refs_1_.refs_0_, ...), custom_call_target="tpu_custom_call" | custom-call | flops 2200000000 | bytes 1024 | tf_op jit(solution)/shard_map/third/pallas_call | solution.py:516
  35.4 0.0 collective-permute-done.6.refs_0_
  35.5 1.1 %third.5.edge = f32[1,2,144,128]{3,2,1,0:T(8,128)S(1)} custom-call(s32[1]{0:T(128)} %bitcast.odd_ref, f32[8,128]{1,0:T(8,128)S(1)} %get-tuple-element.51.step, f32[4,128,256]{2,1,0:T(8,128)S(1)} %get-tuple-element.52.speed_ref, f32[9,128,128]{2,1,0:T(8,128)S(1)} %wall.1.refs_0_, f32[1,2,128,128]{3,2,1,0:T(8,128)S(1)} %collective-permute-done.6.refs_0_, ...), custom_call_target="tpu_custom_call" | custom-call | flops 1100000000 | bytes 1024 | tf_op jit(solution)/shard_map/third/pallas_call | solution.py:516
  36.6 0.0 collective-permute-done.8.refs_2_
  36.6 1.1 %third.7.edge.last = f32[1,2,144,128]{3,2,1,0:T(8,128)S(1)} custom-call(s32[1]{0:T(128)} %bitcast.odd_ref, f32[8,128]{1,0:T(8,128)S(1)} %get-tuple-element.51.step, f32[4,128,256]{2,1,0:T(8,128)S(1)} %get-tuple-element.52.speed_ref, f32[9,128,128]{2,1,0:T(8,128)S(1)} %wall.1.refs_0_, f32[2,2,144,128]{3,2,1,0:T(8,128)S(1)} %second.7.refs_2_.refs_1_.refs_0_, ...), custom_call_target="tpu_custom_call" | custom-call | flops 1100000000 | bytes 1024 | tf_op jit(solution)/shard_map/third/pallas_call | solution.py:516
  37.7 0.6 collective-permute-start.10
  38.3 1.4 %collective-permute-start.9 = (f32[3,2,128,128]{3,2,1,0:T(8,128)S(1)}, f32[3,2,128,128]{3,2,1,0:T(8,128)S(1)}, u32[]{:S(2)}, u32[]{:S(2)}) collective-permute-start(f32[3,2,128,128]{3,2,1,0:T(8,128)S(1)} %pack.2), channel_id=1, source_target_pairs={{0,15},{1,2},{2,1},{3,4},{4,3},{5,6},{6,5},{7,8},{8,7},{9,10},{10,... | collective-permute-start | bytes 1179656 | tf_op jit(solution)/shard_map/ppermute | solution.py:534
  39.7 0.0 collective-permute-done.10.inner
  39.7 2.9 %inside.1 = (f32[2,2,144,128]{3,2,1,0:T(8,128)S(1)}, f32[1,2,128,128]{3,2,1,0:T(8,128)S(1)}, f32[1,2,128,128]{3,2,1,0:T(8,128)S(1)}) custom-call(f32[1,2,144,128]{3,2,1,0:T(8,128)S(1)} %third.5.edge, f32[2,2,144,128]{3,2,1,0:T(8,128)S(1)} %third.6.middle, f32[1,2,144,128]{3,2,1,0:T(8,128)S(1)} %third.7.edge.last, ...), custom_call_target="tpu_custom_call" | custom-call | flops 110000000 | bytes 1024 | tf_op jit(solution)/shard_map/inside/pallas_call | solution.py:516
  42.6 0.2 collective-permute-start.11
  42.8 1.2 %collective-permute-done.11.refs_1_ = f32[1,2,128,128]{3,2,1,0:T(8,128)S(1)} collective-permute-done((f32[1,2,128,128]{3,2,1,0:T(8,128)S(1)}, f32[1,2,128,128]{3,2,1,0:T(8,128)S(1)}, u32[]{:S(2)}, u32[]{:S(2)}) %collective-permute-start.11) | collective-permute-done | bytes 131104 | tf_op jit(solution)/shard_map/ppermute | solution.py:534
  44.0 1.3 %second.9 = (f32[1,2,144,128]{3,2,1,0:T(8,128)S(1)}, f32[1,2,128,128]{3,2,1,0:T(8,128)S(1)}) custom-call(s32[1]{0:T(128)} %bitcast.odd_ref, f32[8,128]{1,0:T(8,128)S(1)} %get-tuple-element.51.step, f32[4,128,256]{2,1,0:T(8,128)S(1)} %get-tuple-element.53.speed_ref, f32[9,128,128]{2,1,0:T(8,128)S(1)} %wall.1.refs_0_, ...), custom_call_target="tpu_custom_call" | custom-call | flops 110000000 | bytes 1024 | tf_op jit(solution)/shard_map/second/pallas_call | solution.py:516
  45.2 0.2 collective-permute-start.13
  45.5 2.8 %collective-permute-done.9.outer = f32[3,2,128,128]{3,2,1,0:T(8,128)S(1)} collective-permute-done((f32[3,2,128,128]{3,2,1,0:T(8,128)S(1)}, f32[3,2,128,128]{3,2,1,0:T(8,128)S(1)}, u32[]{:S(2)}, u32[]{:S(2)}) %collective-permute-start.9) | collective-permute-done | bytes 393248 | tf_op jit(solution)/shard_map/ppermute | solution.py:534
  48.3 2.9 %outside.1 = (f32[1,2,128,128]{3,2,1,0:T(8,128)S(1)}, f32[2,2,144,128]{3,2,1,0:T(8,128)S(1)}) custom-call(f32[1,2,144,128]{3,2,1,0:T(8,128)S(1)} %third.5.edge, f32[2,2,144,128]{3,2,1,0:T(8,128)S(1)} %third.6.middle, f32[1,2,144,128]{3,2,1,0:T(8,128)S(1)} %third.7.edge.last, f32[3,2,128,128]{3,2,1,0:T(8,128)S(1)} %collective-permute-done.9.outer, ...), custom_call_target="tpu_custom_call" | custom-call | flops 3300000000 | bytes 1024 | tf_op jit(solution)/shard_map/outside/pallas_call | solution.py:516
  51.2 1.1 %second.10 = (f32[1,2,144,128]{3,2,1,0:T(8,128)S(1)}, f32[1,2,128,128]{3,2,1,0:T(8,128)S(1)}) custom-call(s32[1]{0:T(128)} %bitcast.odd_ref, f32[8,128]{1,0:T(8,128)S(1)} %get-tuple-element.51.step, f32[4,128,256]{2,1,0:T(8,128)S(1)} %get-tuple-element.53.speed_ref, f32[9,128,128]{2,1,0:T(8,128)S(1)} %wall.1.refs_0_, ...), custom_call_target="tpu_custom_call" | custom-call | flops 1100000000 | bytes 1024 | tf_op jit(solution)/shard_map/second/pallas_call | solution.py:516
  52.3 1.4 %collective-permute-start.12 = (f32[1,2,128,128]{3,2,1,0:T(8,128)S(1)}, f32[1,2,128,128]{3,2,1,0:T(8,128)S(1)}, u32[]{:S(2)}, u32[]{:S(2)}) collective-permute-start(f32[1,2,128,128]{3,2,1,0:T(8,128)S(1)} %get-tuple-element.73), channel_id=1, source_target_pairs={{0,15},{1,2},{2,1},{3,4},{4,3},{5,6},{6,5},{7,8},{8,7},{9,10},{10,... | collective-permute-start | bytes 393224 | tf_op jit(solution)/shard_map/ppermute | solution.py:534
  53.7 2.0 %second.11.refs_1_.refs_0_.refs_2_ = f32[2,2,144,128]{3,2,1,0:T(8,128)S(1)} custom-call(s32[1]{0:T(128)} %bitcast.odd_ref, f32[8,128]{1,0:T(8,128)S(1)} %get-tuple-element.51.step, f32[4,128,256]{2,1,0:T(8,128)S(1)} %get-tuple-element.53.speed_ref, f32[9,128,128]{2,1,0:T(8,128)S(1)} %wall.1.refs_0_, ...), custom_call_target="tpu_custom_call" | custom-call | flops 2200000000 | bytes 1024 | tf_op jit(solution)/shard_map/second/pallas_call | solution.py:516
  55.7 2.2 %third.8.refs_3_ = f32[2,2,144,128]{3,2,1,0:T(8,128)S(1)} custom-call(s32[1]{0:T(128)} %bitcast.odd_ref, f32[8,128]{1,0:T(8,128)S(1)} %get-tuple-element.51.step, f32[4,128,256]{2,1,0:T(8,128)S(1)} %get-tuple-element.52.speed_ref, f32[9,128,128]{2,1,0:T(8,128)S(1)} %wall.1.refs_0_, f32[1,2,144,128]{3,2,1,0:T(8,128)S(1)} %get-tuple-element.74.refs_0_.refs_1_, ...), custom_call_target="tpu_custom_call" | custom-call | flops 2200000000 | bytes 1024 | tf_op jit(solution)/shard_map/third/pallas_call | solution.py:516
  57.8 0.0 collective-permute-done.13.refs_2_
  57.9 1.1 %third.9.refs_4_ = f32[1,2,144,128]{3,2,1,0:T(8,128)S(1)} custom-call(s32[1]{0:T(128)} %bitcast.odd_ref, f32[8,128]{1,0:T(8,128)S(1)} %get-tuple-element.51.step, f32[4,128,256]{2,1,0:T(8,128)S(1)} %get-tuple-element.52.speed_ref, f32[9,128,128]{2,1,0:T(8,128)S(1)} %wall.1.refs_0_, f32[2,2,144,128]{3,2,1,0:T(8,128)S(1)} %second.11.refs_1_.refs_0_.refs_2_, ...), custom_call_target="tpu_custom_call" | custom-call | flops 1100000000 | bytes 1024 | tf_op jit(solution)/shard_map/third/pallas_call | solution.py:516
  58.9 0.6 collective-permute-done.12.refs_0_
  59.5 1.9 %last.1 = f32[4,128,256]{2,1,0:T(8,128)} custom-call(s32[1]{0:T(128)} %bitcast.odd_ref, f32[8,128]{1,0:T(8,128)S(1)} %get-tuple-element.51.step, f32[4,128,256]{2,1,0:T(8,128)S(1)} %get-tuple-element.52.speed_ref, f32[9,128,128]{2,1,0:T(8,128)S(1)} %wall.1.refs_0_, f32[1,2,128,128]{3,2,1,0:T(8,128)S(1)} %collective-permute-done.12.refs_0_, ...), custom_call_target="tpu_custom_call" | custom-call | flops 1100000000 | bytes 1024 | tf_op jit(solution)/shard_map/last/pallas_call | solution.py:697
  (7 shorter events, 0.1 us)
Async XLA Ops:
  1.9 17.4 %collective-permute-start.5 = (f32[5,2,128,128]{3,2,1,0:T(8,128)S(1)}, f32[5,2,128,128]{3,2,1,0:T(8,128)S(1)}, u32[]{:S(2)}, u32[]{:S(2)}) collective-permute-start(f32[5,2,128,128]{3,2,1,0:T(8,128)S(1)} %get-tuple-element.49), channel_id=1, source_target_pairs={{0,15},{1,2},{2,1},{3,4},{4,3},{5,6},{6,5},{7,8},{8,7},{9,10},{10,... | collective-permute-start | bytes 1966088 | tf_op jit(solution)/shard_map/ppermute | solution.py:534
  7.4 2.1 %collective-permute-start.2 = (f32[3,2,128,128]{3,2,1,0:T(8,128)S(1)}, f32[3,2,128,128]{3,2,1,0:T(8,128)S(1)}, u32[]{:S(2)}, u32[]{:S(2)}) collective-permute-start(f32[3,2,128,128]{3,2,1,0:T(8,128)S(1)} %get-tuple-element.46), channel_id=1, source_target_pairs={{0,1},{1,0},{2,3},{3,2},{4,5},{5,4},{6,7},{7,6},{8,9},{9,8},{10,11... | collective-permute-start | bytes 1179656 | tf_op jit(solution)/shard_map/ppermute | solution.py:534
  7.4 1.7 %collective-permute-start = (f32[8,128]{1,0:T(8,128)S(1)}, f32[8,128]{1,0:T(8,128)S(1)}, u32[]{:S(2)}, u32[]{:S(2)}) collective-permute-start(f32[8,128]{1,0:T(8,128)S(1)} %get-tuple-element.42), channel_id=1, source_target_pairs={{0,1},{1,0},{2,3},{3,2},{4,5},{5,4},{6,7},{7,6},{8,9},{9,8},{10,11... | collective-permute-start | bytes 12296 | tf_op jit(solution)/shard_map/ppermute | solution.py:543
  9.1 6.5 %collective-permute-start.1 = (f32[8,128]{1,0:T(8,128)S(1)}, f32[8,128]{1,0:T(8,128)S(1)}, u32[]{:S(2)}, u32[]{:S(2)}) collective-permute-start(f32[8,128]{1,0:T(8,128)S(1)} %max.12), channel_id=1, source_target_pairs={{0,8},{1,9},{2,10},{3,11},{4,12},{5,13},{6,14},{7,15},{8,0},{9,1},... | collective-permute-start | bytes 12296 | tf_op jit(solution)/shard_map/ppermute | solution.py:543
  15.7 3.6 %collective-permute-start.3 = (f32[8,128]{1,0:T(8,128)S(1)}, f32[8,128]{1,0:T(8,128)S(1)}, u32[]{:S(2)}, u32[]{:S(2)}) collective-permute-start(f32[8,128]{1,0:T(8,128)S(1)} %max.13), channel_id=1, source_target_pairs={{0,4},{1,5},{2,6},{3,7},{4,0},{5,1},{6,2},{7,3},{8,12},{9,13},{10,... | collective-permute-start | bytes 12296 | tf_op jit(solution)/shard_map/ppermute | solution.py:543
  19.3 3.6 %collective-permute-start.4 = (f32[8,128]{1,0:T(8,128)S(1)}, f32[8,128]{1,0:T(8,128)S(1)}, u32[]{:S(2)}, u32[]{:S(2)}) collective-permute-start(f32[8,128]{1,0:T(8,128)S(1)} %max.14), channel_id=1, source_target_pairs={{0,2},{1,3},{2,0},{3,1},{4,6},{5,7},{6,4},{7,5},{8,10},{9,11},{10,... | collective-permute-start | bytes 12296 | tf_op jit(solution)/shard_map/ppermute | solution.py:543
  24.4 7.8 %collective-permute-start.7 = (f32[1,2,128,128]{3,2,1,0:T(8,128)S(1)}, f32[1,2,128,128]{3,2,1,0:T(8,128)S(1)}, u32[]{:S(2)}, u32[]{:S(2)}) collective-permute-start(f32[1,2,128,128]{3,2,1,0:T(8,128)S(1)} %get-tuple-element.59), channel_id=1, source_target_pairs={{0,1},{1,0},{2,3},{3,2},{4,5},{5,4},{6,7},{7,6},{8,9},{9,8},{10,11... | collective-permute-start | bytes 393224 | tf_op jit(solution)/shard_map/ppermute | solution.py:534
  25.5 9.9 %collective-permute-start.6 = (f32[1,2,128,128]{3,2,1,0:T(8,128)S(1)}, f32[1,2,128,128]{3,2,1,0:T(8,128)S(1)}, u32[]{:S(2)}, u32[]{:S(2)}) collective-permute-start(f32[1,2,128,128]{3,2,1,0:T(8,128)S(1)} %get-tuple-element.56), channel_id=1, source_target_pairs={{0,15},{1,2},{2,1},{3,4},{4,3},{5,6},{6,5},{7,8},{8,7},{9,10},{10,... | collective-permute-start | bytes 393224 | tf_op jit(solution)/shard_map/ppermute | solution.py:534
  33.2 3.4 %collective-permute-start.8 = (f32[1,2,128,128]{3,2,1,0:T(8,128)S(1)}, f32[1,2,128,128]{3,2,1,0:T(8,128)S(1)}, u32[]{:S(2)}, u32[]{:S(2)}) collective-permute-start(f32[1,2,128,128]{3,2,1,0:T(8,128)S(1)} %get-tuple-element.61), channel_id=1, source_target_pairs={{0,1},{1,0},{2,3},{3,2},{4,5},{5,4},{6,7},{7,6},{8,9},{9,8},{10,11... | collective-permute-start | bytes 393224 | tf_op jit(solution)/shard_map/ppermute | solution.py:534
  37.7 1.9 %collective-permute-start.10 = (f32[2,2,128,128]{3,2,1,0:T(8,128)S(1)}, f32[2,2,128,128]{3,2,1,0:T(8,128)S(1)}, u32[]{:S(2)}, u32[]{:S(2)}) collective-permute-start(f32[2,2,128,128]{3,2,1,0:T(8,128)S(1)} %pack.3), channel_id=1, source_target_pairs={{0,1},{1,0},{2,3},{3,2},{4,5},{5,4},{6,7},{7,6},{8,9},{9,8},{10,11... | collective-permute-start | bytes 786440 | tf_op jit(solution)/shard_map/ppermute | solution.py:534
  38.3 10.0 %collective-permute-start.9 = (f32[3,2,128,128]{3,2,1,0:T(8,128)S(1)}, f32[3,2,128,128]{3,2,1,0:T(8,128)S(1)}, u32[]{:S(2)}, u32[]{:S(2)}) collective-permute-start(f32[3,2,128,128]{3,2,1,0:T(8,128)S(1)} %pack.2), channel_id=1, source_target_pairs={{0,15},{1,2},{2,1},{3,4},{4,3},{5,6},{6,5},{7,8},{8,7},{9,10},{10,... | collective-permute-start | bytes 1179656 | tf_op jit(solution)/shard_map/ppermute | solution.py:534
  42.6 1.4 %collective-permute-start.11 = (f32[1,2,128,128]{3,2,1,0:T(8,128)S(1)}, f32[1,2,128,128]{3,2,1,0:T(8,128)S(1)}, u32[]{:S(2)}, u32[]{:S(2)}) collective-permute-start(f32[1,2,128,128]{3,2,1,0:T(8,128)S(1)} %get-tuple-element.67), channel_id=1, source_target_pairs={{0,1},{1,0},{2,3},{3,2},{4,5},{5,4},{6,7},{7,6},{8,9},{9,8},{10,11... | collective-permute-start | bytes 393224 | tf_op jit(solution)/shard_map/ppermute | solution.py:534
  45.2 12.6 %collective-permute-start.13 = (f32[1,2,128,128]{3,2,1,0:T(8,128)S(1)}, f32[1,2,128,128]{3,2,1,0:T(8,128)S(1)}, u32[]{:S(2)}, u32[]{:S(2)}) collective-permute-start(f32[1,2,128,128]{3,2,1,0:T(8,128)S(1)} %get-tuple-element.78), channel_id=1, source_target_pairs={{0,1},{1,0},{2,3},{3,2},{4,5},{5,4},{6,7},{7,6},{8,9},{9,8},{10,11... | collective-permute-start | bytes 393224 | tf_op jit(solution)/shard_map/ppermute | solution.py:534
  52.3 7.3 %collective-permute-start.12 = (f32[1,2,128,128]{3,2,1,0:T(8,128)S(1)}, f32[1,2,128,128]{3,2,1,0:T(8,128)S(1)}, u32[]{:S(2)}, u32[]{:S(2)}) collective-permute-start(f32[1,2,128,128]{3,2,1,0:T(8,128)S(1)} %get-tuple-element.73), channel_id=1, source_target_pairs={{0,15},{1,2},{2,1},{3,4},{4,3},{5,6},{6,5},{7,8},{8,7},{9,10},{10,... | collective-permute-start | bytes 393224 | tf_op jit(solution)/shard_map/ppermute | solution.py:534

commit v5 on v4

--- a/solution.py
+++ b/solution.py
@@ -342,12 +342,13 @@
     return {OUTER + k: layer for k, layer in enumerate(found)}
 
 
-def inside_kernel(edge, middle, last, inner, moved, wall, out, flux_out, send, field, *more):
+def inside_kernel(edge, middle, last, inner, beyond, moved, wall, out, flux_out, send, field, *more):
     *slopes, flux = more
     rows = moved.shape[2]
     layers = own_layers(edge, middle, last)
     count = len(layers)
-    layers.update(padded_halo(inner, field, [(k, OUTER + count + k) for k in range(INNER)]))
+    layers.update(padded_halo(inner, field, [(0, OUTER + count)]))
+    layers[OUTER + count + 1] = Layer(beyond, 0, False)
     first_fluxes(layers, wall, moved, slopes, flux, range(OUTER + 1, OUTER + count))
     copy_layer(Layer(flux, OUTER, False), Layer(flux_out, 0, False), rows)
     for i in range(OUTER + 2, OUTER + count):
@@ -470,8 +471,9 @@
     count, rows, _ = speed_ref.shape
     copies = []
 
-    def send(source, layer, h):
-        target = out.at[own_index(odd, layer, count), :, h * LANES : (h + 1) * LANES]
+    def send(source, layer, h, first_row=0):
+        rows_here = pl.ds(first_row, source.shape[0])
+        target = out.at[own_index(odd, layer, count), rows_here, h * LANES : (h + 1) * LANES]
         copies.append(pltpu.make_async_copy(source, target, sems.at[len(copies)]))
         copies[-1].start()
 
@@ -482,8 +484,13 @@
                 send(ref.at[k, h, pl.ds(PAD, rows), :], p, h)
             p += 1
 
+    piece = rows // 2
+
     def write(h, r, value):
         held_out[h, pl.ds(r, ROWS), :] = value
+        if (r + ROWS) % piece == 0:
+            start = r + ROWS - piece
+            send(held_out.at[h, pl.ds(start, piece), :], OUTER, h, start)
 
     index = own_index(odd, OUTER, count)
     third_sweep(
@@ -495,8 +502,6 @@
         write,
         rows,
     )
-    for h in HALVES:
-        send(held_out.at[h], OUTER, h)
     for copy in copies:
         copy.wait()
 
@@ -594,16 +599,18 @@
             faces=0.02,
         )[0]
 
-    size = lax.axis_size("gx")
     prepare_inside = functools.partial(prepare_call, wall=wall, first=first, own=state, inner=inner)
     outer = swap(send_outer, True)
+    size = lax.axis_size("gx")
+    reaches = [1 << k for k in range(1, size.bit_length()) if 1 << k < size]
     peak = largest_round(peak, 1, [])
     kept = [prepare_inside(tuple(range(OUTER + 2, own_end)))]
-    peak = largest_round(peak, 8, kept)
     kept.insert(0, prepare_inside((OUTER + 1,)))
     kept.insert(0, prepare_call((OUTER - 2, OUTER - 1, OUTER), wall=wall, first=first, own=state, outer=outer))
-    peak = largest_round(peak, 4, [kept[1]])
-    peak = largest_round(peak, 2, [kept[0]])
+    beside = [[kept[2]], [kept[1]], [kept[0]]]
+    for n, reach in enumerate(reaches[::-1]):
+        left = len(reaches) - n
+        peak = largest_round(peak, reach, beside[-left] if left <= len(beside) else [])
     own, above, moved, step, send_inner = call(
         functools.partial(finish_kernel, parts=len(kept)),
         "finish",
@@ -640,7 +647,7 @@
                 "inside",
                 [held(padded(count - 2)), held(plain(1)), held(plain(1))],
                 [],
-                [*own, inner, moved, wall],
+                [*own, inner, beyond, moved, wall],
                 [*slopes, flux],
                 faces=0.1,
             )
@@ -683,12 +690,15 @@
             last_new = third_call(inside_work[-1:], fields[1:], starts[1:])
             return last_call(odd, step, third, wall, edge_fields, edge_starts, [middle_new, last_new], natural_shape)
         edge_new = third_call((OUTER,), edge_fields, edge_starts)
-        (send_outer,) = call(pack_kernel, "pack", [held(plain(OUTER))], [], [edge_new, middle_new])
+        send_outer, send_beyond = call(
+            pack_kernel, "pack", [held(plain(OUTER)), held(plain(1))], [], [edge_new, middle_new]
+        )
         outer = swap(send_outer, True)
-        _, *after = lax.optimization_barrier((send_outer, *fields[1:]))
+        beyond = swap(send_beyond, False)
+        beyond, *after = lax.optimization_barrier((beyond, *fields[1:]))
         last_new = third_call(inside_work[-1:], after, starts[1:])
         own = [edge_new, middle_new, last_new]
-        (send_inner,) = call(pack_kernel, "pack", [held(plain(INNER))], [], [last_new, middle_new])
+        (send_inner,) = call(strip_kernel, "strip", [held(plain(1))], [], [last_new])
         inner = swap(send_inner, False)
 
 
@@ -699,19 +709,23 @@
         out_shape=jax.ShapeDtypeStruct(shape, jnp.float32),
         in_specs=[IN_SMEM] + [IN_VMEM] * len(arrays),
         out_specs=pl.BlockSpec(memory_space=pltpu.HBM),
-        scratch_shapes=[pltpu.VMEM((2, *shape[1:2], LANES), jnp.float32), pltpu.SemaphoreType.DMA((2 * shape[0],))],
+        scratch_shapes=[pltpu.VMEM((2, *shape[1:2], LANES), jnp.float32), pltpu.SemaphoreType.DMA((2 * shape[0] + 2,))],
         compiler_params=pltpu.CompilerParams(vmem_limit_bytes=VMEM_LIMIT),
         cost_estimate=pl.CostEstimate(flops=int(1.1e9), bytes_accessed=1024, transcendentals=0),
         name="last",
     )(odd, *arrays)
 
 
-def pack_kernel(edge, middle, send):
-    rows = send.shape[2]
-    copy_layer(Layer(edge, 0), Layer(send, 0, False), rows)
-    number = send.shape[0] - 1
-    for k in range(number):
-        copy_layer(Layer(middle, k if number == OUTER - 1 else middle.shape[0] - 1 - k), Layer(send, 1 + k, False), rows)
+def pack_kernel(edge, middle, send_outer, send_beyond):
+    rows = send_outer.shape[2]
+    copy_layer(Layer(edge, 0), Layer(send_outer, 0, False), rows)
+    for k in range(OUTER - 1):
+        copy_layer(Layer(middle, k), Layer(send_outer, 1 + k, False), rows)
+    copy_layer(Layer(middle, middle.shape[0] - 1), Layer(send_beyond, 0, False), rows)
+
+
+def strip_kernel(last, send):
+    copy_layer(Layer(last, 0), Layer(send, 0, False), send.shape[2])
 
 
 def solution(mesh):

time: 61.7 us -> 61.4 us (level)
  waiting for transfers between devices: 12.8 us -> 11 us
  starting transfers between devices: 16.1 us -> 17.5 us
    ppermute x10 -> x11, waiting for transfers between devices: 4.65 us -> 2.89 us  [swap(): return lax.ppermute(array, 'gx', pairs)]
    ppermute x10 -> x11, starting transfers between devices: 14.1 us -> 15.5 us  [swap(): return lax.ppermute(array, 'gx', pairs)]
  transfers between devices with their start and end apart: 14 -> 15, of which waited for: 7 -> 7; matrix products, arithmetic and copies ran while one was open for 0% -> 0% of each run, Pallas kernels for 42% -> 44%
where the time goes in v5:
time: 61.4 us; the launch traced here: 61.2 us
  Pallas kernels  32.3 us (53%)
  starting transfers between devices  17.5 us (29%)
  waiting for transfers between devices  11 us (18%)
    pallas_call x22, Pallas kernels, call(): pl.pallas_call(kernel, out_shape=outs, in_specs=[IN_SMEM] * len(scalars)...  30.5 us
    ppermute x11, starting transfers between devices, swap(): return lax.ppermute(array, 'gx', pairs)  15.5 us
    ppermute x4, waiting for transfers between devices, largest_round(): received = lax.ppermute(array, 'gx', pairs)  8.16 us
    ppermute x11, waiting for transfers between devices, swap(): return lax.ppermute(array, 'gx', pairs)  2.89 us
    ppermute x4, starting transfers between devices, largest_round(): received = lax.ppermute(array, 'gx', pairs)  2 us
    pallas_call x1, Pallas kernels, last_call(): pl.pallas_call(functools.partial(last_kernel, places=places), out_shape=j...  1.83 us
  transfers between devices with their start and end apart: 15, of which 7 were waited for; matrix products, arithmetic and copies ran while one was open for 0% of the time, Pallas kernels for 44%

profile of v5, /device:TPU:0, one launch (start us, length us, event | category | flops | bytes accessed | tf_op | source)
XLA Modules:
  0.0 61.2 jit_solution(14639851062285213845)
XLA Ops:
  0.0 1.8 %begin.1 = (f32[4,128,256]{2,1,0:T(8,128)S(1)}, f32[4,128,256]{2,1,0:T(8,128)S(1)}, f32[4,128,256]{2,1,0:T(8,128)S(1)}, f32[8,128]{1,0:T(8,128)S(1)}, f32[4,2,14...) custom-call(s32[1]{0:T(128)} %bitcast.odd_ref, f32[4,128,256]{2,1,0:T(8,128)} %fraction_in.1, s32[4,128,256]{2,1,0:T(8,128)} %mask_in.1, ...), custom_call_target="tpu_custom_call" | custom-call | flops 110000000 | bytes 1024 | tf_op jit(solution)/shard_map/begin/pallas_call | solution.py:521
  1.8 0.1 first_send.1
  1.9 5.5 %collective-permute-start.5 = (f32[5,2,128,128]{3,2,1,0:T(8,128)S(1)}, f32[5,2,128,128]{3,2,1,0:T(8,128)S(1)}, u32[]{:S(2)}, u32[]{:S(2)}) collective-permute-start(f32[5,2,128,128]{3,2,1,0:T(8,128)S(1)} %get-tuple-element.52), channel_id=1, source_target_pairs={{0,15},{1,2},{2,1},{3,4},{4,3},{5,6},{6,5},{7,8},{8,7},{9,10},{10,... | collective-permute-start | bytes 1966088 | tf_op jit(solution)/shard_map/ppermute | solution.py:539
  7.4 0.0 collective-permute-start.2
  7.4 0.5 collective-permute-start
  7.9 1.2 %collective-permute-done = f32[8,128]{1,0:T(8,128)S(1)} collective-permute-done((f32[8,128]{1,0:T(8,128)S(1)}, f32[8,128]{1,0:T(8,128)S(1)}, u32[]{:S(2)}, u32[]{:S(2)}) %collective-permute-start) | collective-permute-done | bytes 4128 | tf_op jit(solution)/shard_map/ppermute | solution.py:548
  9.1 0.4 wall.1.refs_0_
  9.5 0.0 collective-permute-done.2.refs_3_
  9.5 1.6 %prepare.3.refs_2_ = f32[18,2,128,128]{3,2,1,0:T(8,128)S(1)} custom-call(s32[1]{0:T(128)} %bitcast.odd_ref, f32[9,128,128]{2,1,0:T(8,128)S(1)} %wall.1.refs_0_, f32[4,128,256]{2,1,0:T(8,128)S(1)} %get-tuple-element.47.first.refs_1_, f32[4,2,144,128]{3,2,1,0:T(8,128)S(1)} %get-tuple-element.48.state.refs_2_.refs_3_, ...), custom_call_target="tpu_custom_call" | custom-call | flops 22000000 | bytes 1024 | tf_op jit(solution)/shard_map/prepare/pallas_call | solution.py:521
  11.1 4.5 %collective-permute-done.1 = f32[8,128]{1,0:T(8,128)S(1)} collective-permute-done((f32[8,128]{1,0:T(8,128)S(1)}, f32[8,128]{1,0:T(8,128)S(1)}, u32[]{:S(2)}, u32[]{:S(2)}) %collective-permute-start.1) | collective-permute-done | bytes 4128 | tf_op jit(solution)/shard_map/ppermute | solution.py:548
  15.7 1.5 %collective-permute-start.3 = (f32[8,128]{1,0:T(8,128)S(1)}, f32[8,128]{1,0:T(8,128)S(1)}, u32[]{:S(2)}, u32[]{:S(2)}) collective-permute-start(f32[8,128]{1,0:T(8,128)S(1)} %max.13), channel_id=1, source_target_pairs={{0,4},{1,5},{2,6},{3,7},{4,0},{5,1},{6,2},{7,3},{8,12},{9,13},{10,... | collective-permute-start | bytes 12296 | tf_op jit(solution)/shard_map/ppermute | solution.py:548
  17.1 0.9 %prepare.4.refs_1_ = f32[9,2,128,128]{3,2,1,0:T(8,128)S(1)} custom-call(s32[1]{0:T(128)} %bitcast.odd_ref, f32[9,128,128]{2,1,0:T(8,128)S(1)} %wall.1.refs_0_, f32[4,128,256]{2,1,0:T(8,128)S(1)} %get-tuple-element.47.first.refs_1_, f32[4,2,144,128]{3,2,1,0:T(8,128)S(1)} %get-tuple-element.48.state.refs_2_.refs_3_, ...), custom_call_target="tpu_custom_call" | custom-call | flops 22000000 | bytes 1024 | tf_op jit(solution)/shard_map/prepare/pallas_call | solution.py:521
  18.1 1.2 %collective-permute-done.3 = f32[8,128]{1,0:T(8,128)S(1)} collective-permute-done((f32[8,128]{1,0:T(8,128)S(1)}, f32[8,128]{1,0:T(8,128)S(1)}, u32[]{:S(2)}, u32[]{:S(2)}) %collective-permute-start.3) | collective-permute-done | bytes 4128 | tf_op jit(solution)/shard_map/ppermute | solution.py:548
  19.3 0.0 collective-permute-start.4
  19.3 0.0 collective-permute-done.5.refs_3_.refs_4_
  19.3 2.4 %prepare.5.refs_0_ = f32[27,2,128,128]{3,2,1,0:T(8,128)S(1)} custom-call(s32[1]{0:T(128)} %bitcast.odd_ref, f32[9,128,128]{2,1,0:T(8,128)S(1)} %wall.1.refs_0_, f32[4,128,256]{2,1,0:T(8,128)S(1)} %get-tuple-element.47.first.refs_1_, f32[4,2,144,128]{3,2,1,0:T(8,128)S(1)} %get-tuple-element.48.state.refs_2_.refs_3_, ...), custom_call_target="tpu_custom_call" | custom-call | flops 22000000 | bytes 1024 | tf_op jit(solution)/shard_map/prepare/pallas_call | solution.py:521
  21.6 1.2 %collective-permute-done.4 = f32[8,128]{1,0:T(8,128)S(1)} collective-permute-done((f32[8,128]{1,0:T(8,128)S(1)}, f32[8,128]{1,0:T(8,128)S(1)}, u32[]{:S(2)}, u32[]{:S(2)}) %collective-permute-start.4) | collective-permute-done | bytes 4128 | tf_op jit(solution)/shard_map/ppermute | solution.py:548
  22.9 1.5 %finish.1 = (f32[4,2,144,128]{3,2,1,0:T(8,128)S(1)}, f32[1,2,128,128]{3,2,1,0:T(8,128)S(1)}, f32[6,2,128,128]{3,2,1,0:T(8,128)S(1)}, f32[8,128]{1,0:T(8,128)S(1)}, f32[1,2,128,128]{3,2,1,0:T(8,128)S(1)}) custom-call(f32[8,128]{1,0:T(8,128)S(1)} %max.15.peak, f32[27,2,128,128]{3,2,1,0:T(8,128)S(1)} %prepare.5.refs_0_, f32[9,2,128,128]{3,2,1,0:T(8,128)S(1)} %prepare.4.refs_1_, ...), custom_call_target="tpu_custom_call" | custom-call | flops 1100000000 | bytes 1024 | tf_op jit(solution)/shard_map/finish/pallas_call | solution.py:521
  24.4 0.1 collective-permute-start.7
  24.5 1.1 %second.6 = (f32[1,2,144,128]{3,2,1,0:T(8,128)S(1)}, f32[1,2,128,128]{3,2,1,0:T(8,128)S(1)}) custom-call(s32[1]{0:T(128)} %bitcast.odd_ref, f32[8,128]{1,0:T(8,128)S(1)} %get-tuple-element.54.step, f32[4,128,256]{2,1,0:T(8,128)S(1)} %get-tuple-element.56.speed_ref, f32[9,128,128]{2,1,0:T(8,128)S(1)} %wall.1.refs_0_, ...), custom_call_target="tpu_custom_call" | custom-call | flops 1100000000 | bytes 1024 | tf_op jit(solution)/shard_map/second/pallas_call | solution.py:521
  25.5 4.6 %collective-permute-start.6 = (f32[1,2,128,128]{3,2,1,0:T(8,128)S(1)}, f32[1,2,128,128]{3,2,1,0:T(8,128)S(1)}, u32[]{:S(2)}, u32[]{:S(2)}) collective-permute-start(f32[1,2,128,128]{3,2,1,0:T(8,128)S(1)} %get-tuple-element.59), channel_id=1, source_target_pairs={{0,15},{1,2},{2,1},{3,4},{4,3},{5,6},{6,5},{7,8},{8,7},{9,10},{10,... | collective-permute-start | bytes 393224 | tf_op jit(solution)/shard_map/ppermute | solution.py:539
  30.2 2.0 %second.7.refs_2_.refs_1_.refs_0_ = f32[2,2,144,128]{3,2,1,0:T(8,128)S(1)} custom-call(s32[1]{0:T(128)} %bitcast.odd_ref, f32[8,128]{1,0:T(8,128)S(1)} %get-tuple-element.54.step, f32[4,128,256]{2,1,0:T(8,128)S(1)} %get-tuple-element.56.speed_ref, f32[9,128,128]{2,1,0:T(8,128)S(1)} %wall.1.refs_0_, f32[4,2,144,128]{3,2,1,0:T(8,128)S(1)} %get-tuple-element.61.refs_1_.refs_0_), custom_call_target="tpu_custom_call" | custom-call | flops 2200000000 | bytes 1024 | tf_op jit(solution)/shard_map/second/pallas_call | solution.py:521
  32.1 0.0 collective-permute-done.7.refs_1_
  32.2 1.1 %second.8 = (f32[1,2,144,128]{3,2,1,0:T(8,128)S(1)}, f32[1,2,128,128]{3,2,1,0:T(8,128)S(1)}) custom-call(s32[1]{0:T(128)} %bitcast.odd_ref, f32[8,128]{1,0:T(8,128)S(1)} %get-tuple-element.54.step, f32[4,128,256]{2,1,0:T(8,128)S(1)} %get-tuple-element.56.speed_ref, f32[9,128,128]{2,1,0:T(8,128)S(1)} %wall.1.refs_0_, ...), custom_call_target="tpu_custom_call" | custom-call | flops 110000000 | bytes 1024 | tf_op jit(solution)/shard_map/second/pallas_call | solution.py:521
  33.2 0.1 collective-permute-start.9
  33.3 2.2 %third.6.middle = f32[2,2,144,128]{3,2,1,0:T(8,128)S(1)} custom-call(s32[1]{0:T(128)} %bitcast.odd_ref, f32[8,128]{1,0:T(8,128)S(1)} %get-tuple-element.54.step, f32[4,128,256]{2,1,0:T(8,128)S(1)} %get-tuple-element.55.speed_ref, f32[9,128,128]{2,1,0:T(8,128)S(1)} %wall.1.refs_0_, f32[1,2,144,128]{3,2,1,0:T(8,128)S(1)} %get-tuple-element.60.refs_1_.refs_0_, ...), custom_call_target="tpu_custom_call" | custom-call | flops 2200000000 | bytes 1024 | tf_op jit(solution)/shard_map/third/pallas_call | solution.py:521
  35.4 0.0 collective-permute-done.6.refs_0_
  35.5 1.1 %third.5.edge = f32[1,2,144,128]{3,2,1,0:T(8,128)S(1)} custom-call(s32[1]{0:T(128)} %bitcast.odd_ref, f32[8,128]{1,0:T(8,128)S(1)} %get-tuple-element.54.step, f32[4,128,256]{2,1,0:T(8,128)S(1)} %get-tuple-element.55.speed_ref, f32[9,128,128]{2,1,0:T(8,128)S(1)} %wall.1.refs_0_, f32[1,2,128,128]{3,2,1,0:T(8,128)S(1)} %collective-permute-done.6.refs_0_, ...), custom_call_target="tpu_custom_call" | custom-call | flops 1100000000 | bytes 1024 | tf_op jit(solution)/shard_map/third/pallas_call | solution.py:521
  36.6 0.6 collective-permute-start.8
  37.2 1.4 %collective-permute-start.10 = (f32[3,2,128,128]{3,2,1,0:T(8,128)S(1)}, f32[3,2,128,128]{3,2,1,0:T(8,128)S(1)}, u32[]{:S(2)}, u32[]{:S(2)}) collective-permute-start(f32[3,2,128,128]{3,2,1,0:T(8,128)S(1)} %get-tuple-element.69), channel_id=1, source_target_pairs={{0,15},{1,2},{2,1},{3,4},{4,3},{5,6},{6,5},{7,8},{8,7},{9,10},{10,... | collective-permute-start | bytes 1179656 | tf_op jit(solution)/shard_map/ppermute | solution.py:539
  38.5 0.0 collective-permute-done.9.refs_2_
  38.5 1.1 %third.7.last = f32[1,2,144,128]{3,2,1,0:T(8,128)S(1)} custom-call(s32[1]{0:T(128)} %bitcast.odd_ref, f32[8,128]{1,0:T(8,128)S(1)} %get-tuple-element.54.step, f32[4,128,256]{2,1,0:T(8,128)S(1)} %get-tuple-element.55.speed_ref, f32[9,128,128]{2,1,0:T(8,128)S(1)} %wall.1.refs_0_, f32[2,2,144,128]{3,2,1,0:T(8,128)S(1)} %second.7.refs_2_.refs_1_.refs_0_, ...), custom_call_target="tpu_custom_call" | custom-call | flops 1100000000 | bytes 1024 | tf_op jit(solution)/shard_map/third/pallas_call | solution.py:521
  39.7 0.1 collective-permute-start.11
  39.7 1.3 %collective-permute-done.11.inner = f32[1,2,128,128]{3,2,1,0:T(8,128)S(1)} collective-permute-done((f32[1,2,128,128]{3,2,1,0:T(8,128)S(1)}, f32[1,2,128,128]{3,2,1,0:T(8,128)S(1)}, u32[]{:S(2)}, u32[]{:S(2)}) %collective-permute-start.11) | collective-permute-done | bytes 131104 | tf_op jit(solution)/shard_map/ppermute | solution.py:539
  41.1 2.9 %inside.1 = (f32[2,2,144,128]{3,2,1,0:T(8,128)S(1)}, f32[1,2,128,128]{3,2,1,0:T(8,128)S(1)}, f32[1,2,128,128]{3,2,1,0:T(8,128)S(1)}) custom-call(f32[1,2,144,128]{3,2,1,0:T(8,128)S(1)} %third.5.edge, f32[2,2,144,128]{3,2,1,0:T(8,128)S(1)} %third.6.middle, f32[1,2,144,128]{3,2,1,0:T(8,128)S(1)} %third.7.last, ...), custom_call_target="tpu_custom_call" | custom-call | flops 110000000 | bytes 1024 | tf_op jit(solution)/shard_map/inside/pallas_call | solution.py:521
  44.0 0.2 collective-permute-start.12
  44.2 1.2 %collective-permute-done.12.refs_1_ = f32[1,2,128,128]{3,2,1,0:T(8,128)S(1)} collective-permute-done((f32[1,2,128,128]{3,2,1,0:T(8,128)S(1)}, f32[1,2,128,128]{3,2,1,0:T(8,128)S(1)}, u32[]{:S(2)}, u32[]{:S(2)}) %collective-permute-start.12) | collective-permute-done | bytes 131104 | tf_op jit(solution)/shard_map/ppermute | solution.py:539
  45.4 1.3 %second.9 = (f32[1,2,144,128]{3,2,1,0:T(8,128)S(1)}, f32[1,2,128,128]{3,2,1,0:T(8,128)S(1)}) custom-call(s32[1]{0:T(128)} %bitcast.odd_ref, f32[8,128]{1,0:T(8,128)S(1)} %get-tuple-element.54.step, f32[4,128,256]{2,1,0:T(8,128)S(1)} %get-tuple-element.56.speed_ref, f32[9,128,128]{2,1,0:T(8,128)S(1)} %wall.1.refs_0_, ...), custom_call_target="tpu_custom_call" | custom-call | flops 110000000 | bytes 1024 | tf_op jit(solution)/shard_map/second/pallas_call | solution.py:521
  46.6 0.2 collective-permute-start.14
  46.9 0.3 collective-permute-done.10.outer
  47.2 2.9 %outside.1 = (f32[1,2,128,128]{3,2,1,0:T(8,128)S(1)}, f32[2,2,144,128]{3,2,1,0:T(8,128)S(1)}) custom-call(f32[1,2,144,128]{3,2,1,0:T(8,128)S(1)} %third.5.edge, f32[2,2,144,128]{3,2,1,0:T(8,128)S(1)} %third.6.middle, f32[1,2,144,128]{3,2,1,0:T(8,128)S(1)} %third.7.last, f32[3,2,128,128]{3,2,1,0:T(8,128)S(1)} %collective-permute-done.10.outer, ...), custom_call_target="tpu_custom_call" | custom-call | flops 3300000000 | bytes 1024 | tf_op jit(solution)/shard_map/outside/pallas_call | solution.py:521
  50.1 1.1 %second.10 = (f32[1,2,144,128]{3,2,1,0:T(8,128)S(1)}, f32[1,2,128,128]{3,2,1,0:T(8,128)S(1)}) custom-call(s32[1]{0:T(128)} %bitcast.odd_ref, f32[8,128]{1,0:T(8,128)S(1)} %get-tuple-element.54.step, f32[4,128,256]{2,1,0:T(8,128)S(1)} %get-tuple-element.56.speed_ref, f32[9,128,128]{2,1,0:T(8,128)S(1)} %wall.1.refs_0_, ...), custom_call_target="tpu_custom_call" | custom-call | flops 1100000000 | bytes 1024 | tf_op jit(solution)/shard_map/second/pallas_call | solution.py:521
  51.1 2.8 %collective-permute-start.13 = (f32[1,2,128,128]{3,2,1,0:T(8,128)S(1)}, f32[1,2,128,128]{3,2,1,0:T(8,128)S(1)}, u32[]{:S(2)}, u32[]{:S(2)}) collective-permute-start(f32[1,2,128,128]{3,2,1,0:T(8,128)S(1)} %get-tuple-element.79), channel_id=1, source_target_pairs={{0,15},{1,2},{2,1},{3,4},{4,3},{5,6},{6,5},{7,8},{8,7},{9,10},{10,... | collective-permute-start | bytes 393224 | tf_op jit(solution)/shard_map/ppermute | solution.py:539
  54.0 2.0 %second.11.refs_1_.refs_0_.refs_2_ = f32[2,2,144,128]{3,2,1,0:T(8,128)S(1)} custom-call(s32[1]{0:T(128)} %bitcast.odd_ref, f32[8,128]{1,0:T(8,128)S(1)} %get-tuple-element.54.step, f32[4,128,256]{2,1,0:T(8,128)S(1)} %get-tuple-element.56.speed_ref, f32[9,128,128]{2,1,0:T(8,128)S(1)} %wall.1.refs_0_, ...), custom_call_target="tpu_custom_call" | custom-call | flops 2200000000 | bytes 1024 | tf_op jit(solution)/shard_map/second/pallas_call | solution.py:521
  55.9 2.2 %third.8.refs_3_ = f32[2,2,144,128]{3,2,1,0:T(8,128)S(1)} custom-call(s32[1]{0:T(128)} %bitcast.odd_ref, f32[8,128]{1,0:T(8,128)S(1)} %get-tuple-element.54.step, f32[4,128,256]{2,1,0:T(8,128)S(1)} %get-tuple-element.55.speed_ref, f32[9,128,128]{2,1,0:T(8,128)S(1)} %wall.1.refs_0_, f32[1,2,144,128]{3,2,1,0:T(8,128)S(1)} %get-tuple-element.80.refs_0_.refs_1_, ...), custom_call_target="tpu_custom_call" | custom-call | flops 2200000000 | bytes 1024 | tf_op jit(solution)/shard_map/third/pallas_call | solution.py:521
  58.1 0.0 collective-permute-done.14.refs_2_
  58.1 1.1 %third.9.refs_4_ = f32[1,2,144,128]{3,2,1,0:T(8,128)S(1)} custom-call(s32[1]{0:T(128)} %bitcast.odd_ref, f32[8,128]{1,0:T(8,128)S(1)} %get-tuple-element.54.step, f32[4,128,256]{2,1,0:T(8,128)S(1)} %get-tuple-element.55.speed_ref, f32[9,128,128]{2,1,0:T(8,128)S(1)} %wall.1.refs_0_, f32[2,2,144,128]{3,2,1,0:T(8,128)S(1)} %second.11.refs_1_.refs_0_.refs_2_, ...), custom_call_target="tpu_custom_call" | custom-call | flops 1100000000 | bytes 1024 | tf_op jit(solution)/shard_map/third/pallas_call | solution.py:521
  59.2 1.8 %last.1 = f32[4,128,256]{2,1,0:T(8,128)} custom-call(s32[1]{0:T(128)} %bitcast.odd_ref, f32[8,128]{1,0:T(8,128)S(1)} %get-tuple-element.54.step, f32[4,128,256]{2,1,0:T(8,128)S(1)} %get-tuple-element.55.speed_ref, f32[9,128,128]{2,1,0:T(8,128)S(1)} %wall.1.refs_0_, f32[1,2,128,128]{3,2,1,0:T(8,128)S(1)} %collective-permute-done.13.refs_0_, ...), custom_call_target="tpu_custom_call" | custom-call | flops 1100000000 | bytes 1024 | tf_op jit(solution)/shard_map/last/pallas_call | solution.py:707
  (9 shorter events, 0.1 us)
Async XLA Ops:
  1.9 17.4 %collective-permute-start.5 = (f32[5,2,128,128]{3,2,1,0:T(8,128)S(1)}, f32[5,2,128,128]{3,2,1,0:T(8,128)S(1)}, u32[]{:S(2)}, u32[]{:S(2)}) collective-permute-start(f32[5,2,128,128]{3,2,1,0:T(8,128)S(1)} %get-tuple-element.52), channel_id=1, source_target_pairs={{0,15},{1,2},{2,1},{3,4},{4,3},{5,6},{6,5},{7,8},{8,7},{9,10},{10,... | collective-permute-start | bytes 1966088 | tf_op jit(solution)/shard_map/ppermute | solution.py:539
  7.4 2.1 %collective-permute-start.2 = (f32[3,2,128,128]{3,2,1,0:T(8,128)S(1)}, f32[3,2,128,128]{3,2,1,0:T(8,128)S(1)}, u32[]{:S(2)}, u32[]{:S(2)}) collective-permute-start(f32[3,2,128,128]{3,2,1,0:T(8,128)S(1)} %get-tuple-element.49), channel_id=1, source_target_pairs={{0,1},{1,0},{2,3},{3,2},{4,5},{5,4},{6,7},{7,6},{8,9},{9,8},{10,11... | collective-permute-start | bytes 1179656 | tf_op jit(solution)/shard_map/ppermute | solution.py:539
  7.4 1.7 %collective-permute-start = (f32[8,128]{1,0:T(8,128)S(1)}, f32[8,128]{1,0:T(8,128)S(1)}, u32[]{:S(2)}, u32[]{:S(2)}) collective-permute-start(f32[8,128]{1,0:T(8,128)S(1)} %get-tuple-element.45), channel_id=1, source_target_pairs={{0,1},{1,0},{2,3},{3,2},{4,5},{5,4},{6,7},{7,6},{8,9},{9,8},{10,11... | collective-permute-start | bytes 12296 | tf_op jit(solution)/shard_map/ppermute | solution.py:548
  9.1 6.5 %collective-permute-start.1 = (f32[8,128]{1,0:T(8,128)S(1)}, f32[8,128]{1,0:T(8,128)S(1)}, u32[]{:S(2)}, u32[]{:S(2)}) collective-permute-start(f32[8,128]{1,0:T(8,128)S(1)} %max.12), channel_id=1, source_target_pairs={{0,8},{1,9},{2,10},{3,11},{4,12},{5,13},{6,14},{7,15},{8,0},{9,1},... | collective-permute-start | bytes 12296 | tf_op jit(solution)/shard_map/ppermute | solution.py:548
  15.7 3.6 %collective-permute-start.3 = (f32[8,128]{1,0:T(8,128)S(1)}, f32[8,128]{1,0:T(8,128)S(1)}, u32[]{:S(2)}, u32[]{:S(2)}) collective-permute-start(f32[8,128]{1,0:T(8,128)S(1)} %max.13), channel_id=1, source_target_pairs={{0,4},{1,5},{2,6},{3,7},{4,0},{5,1},{6,2},{7,3},{8,12},{9,13},{10,... | collective-permute-start | bytes 12296 | tf_op jit(solution)/shard_map/ppermute | solution.py:548
  19.3 3.6 %collective-permute-start.4 = (f32[8,128]{1,0:T(8,128)S(1)}, f32[8,128]{1,0:T(8,128)S(1)}, u32[]{:S(2)}, u32[]{:S(2)}) collective-permute-start(f32[8,128]{1,0:T(8,128)S(1)} %max.14), channel_id=1, source_target_pairs={{0,2},{1,3},{2,0},{3,1},{4,6},{5,7},{6,4},{7,5},{8,10},{9,11},{10,... | collective-permute-start | bytes 12296 | tf_op jit(solution)/shard_map/ppermute | solution.py:548
  24.4 7.8 %collective-permute-start.7 = (f32[1,2,128,128]{3,2,1,0:T(8,128)S(1)}, f32[1,2,128,128]{3,2,1,0:T(8,128)S(1)}, u32[]{:S(2)}, u32[]{:S(2)}) collective-permute-start(f32[1,2,128,128]{3,2,1,0:T(8,128)S(1)} %get-tuple-element.62), channel_id=1, source_target_pairs={{0,1},{1,0},{2,3},{3,2},{4,5},{5,4},{6,7},{7,6},{8,9},{9,8},{10,11... | collective-permute-start | bytes 393224 | tf_op jit(solution)/shard_map/ppermute | solution.py:539
  25.5 9.9 %collective-permute-start.6 = (f32[1,2,128,128]{3,2,1,0:T(8,128)S(1)}, f32[1,2,128,128]{3,2,1,0:T(8,128)S(1)}, u32[]{:S(2)}, u32[]{:S(2)}) collective-permute-start(f32[1,2,128,128]{3,2,1,0:T(8,128)S(1)} %get-tuple-element.59), channel_id=1, source_target_pairs={{0,15},{1,2},{2,1},{3,4},{4,3},{5,6},{6,5},{7,8},{8,7},{9,10},{10,... | collective-permute-start | bytes 393224 | tf_op jit(solution)/shard_map/ppermute | solution.py:539
  33.2 5.3 %collective-permute-start.9 = (f32[1,2,128,128]{3,2,1,0:T(8,128)S(1)}, f32[1,2,128,128]{3,2,1,0:T(8,128)S(1)}, u32[]{:S(2)}, u32[]{:S(2)}) collective-permute-start(f32[1,2,128,128]{3,2,1,0:T(8,128)S(1)} %get-tuple-element.65), channel_id=1, source_target_pairs={{0,1},{1,0},{2,3},{3,2},{4,5},{5,4},{6,7},{7,6},{8,9},{9,8},{10,11... | collective-permute-start | bytes 393224 | tf_op jit(solution)/shard_map/ppermute | solution.py:539
  36.6 1.9 %collective-permute-start.8 = (f32[1,2,128,128]{3,2,1,0:T(8,128)S(1)}, f32[1,2,128,128]{3,2,1,0:T(8,128)S(1)}, u32[]{:S(2)}, u32[]{:S(2)}) collective-permute-start(f32[1,2,128,128]{3,2,1,0:T(8,128)S(1)} %get-tuple-element.64), channel_id=1, source_target_pairs={{0,1},{1,0},{2,3},{3,2},{4,5},{5,4},{6,7},{7,6},{8,9},{9,8},{10,11... | collective-permute-start | bytes 393224 | tf_op jit(solution)/shard_map/ppermute | solution.py:539
  37.2 10.0 %collective-permute-start.10 = (f32[3,2,128,128]{3,2,1,0:T(8,128)S(1)}, f32[3,2,128,128]{3,2,1,0:T(8,128)S(1)}, u32[]{:S(2)}, u32[]{:S(2)}) collective-permute-start(f32[3,2,128,128]{3,2,1,0:T(8,128)S(1)} %get-tuple-element.69), channel_id=1, source_target_pairs={{0,15},{1,2},{2,1},{3,4},{4,3},{5,6},{6,5},{7,8},{8,7},{9,10},{10,... | collective-permute-start | bytes 1179656 | tf_op jit(solution)/shard_map/ppermute | solution.py:539
  39.7 1.4 %collective-permute-start.11 = (f32[1,2,128,128]{3,2,1,0:T(8,128)S(1)}, f32[1,2,128,128]{3,2,1,0:T(8,128)S(1)}, u32[]{:S(2)}, u32[]{:S(2)}) collective-permute-start(f32[1,2,128,128]{3,2,1,0:T(8,128)S(1)} %strip.1), channel_id=1, source_target_pairs={{0,1},{1,0},{2,3},{3,2},{4,5},{5,4},{6,7},{7,6},{8,9},{9,8},{10,11... | collective-permute-start | bytes 393224 | tf_op jit(solution)/shard_map/ppermute | solution.py:539
  44.0 1.4 %collective-permute-start.12 = (f32[1,2,128,128]{3,2,1,0:T(8,128)S(1)}, f32[1,2,128,128]{3,2,1,0:T(8,128)S(1)}, u32[]{:S(2)}, u32[]{:S(2)}) collective-permute-start(f32[1,2,128,128]{3,2,1,0:T(8,128)S(1)} %get-tuple-element.73), channel_id=1, source_target_pairs={{0,1},{1,0},{2,3},{3,2},{4,5},{5,4},{6,7},{7,6},{8,9},{9,8},{10,11... | collective-permute-start | bytes 393224 | tf_op jit(solution)/shard_map/ppermute | solution.py:539
  46.6 11.5 %collective-permute-start.14 = (f32[1,2,128,128]{3,2,1,0:T(8,128)S(1)}, f32[1,2,128,128]{3,2,1,0:T(8,128)S(1)}, u32[]{:S(2)}, u32[]{:S(2)}) collective-permute-start(f32[1,2,128,128]{3,2,1,0:T(8,128)S(1)} %get-tuple-element.84), channel_id=1, source_target_pairs={{0,1},{1,0},{2,3},{3,2},{4,5},{5,4},{6,7},{7,6},{8,9},{9,8},{10,11... | collective-permute-start | bytes 393224 | tf_op jit(solution)/shard_map/ppermute | solution.py:539
  51.1 8.1 %collective-permute-start.13 = (f32[1,2,128,128]{3,2,1,0:T(8,128)S(1)}, f32[1,2,128,128]{3,2,1,0:T(8,128)S(1)}, u32[]{:S(2)}, u32[]{:S(2)}) collective-permute-start(f32[1,2,128,128]{3,2,1,0:T(8,128)S(1)} %get-tuple-element.79), channel_id=1, source_target_pairs={{0,15},{1,2},{2,1},{3,4},{4,3},{5,6},{6,5},{7,8},{8,7},{9,10},{10,... | collective-permute-start | bytes 393224 | tf_op jit(solution)/shard_map/ppermute | solution.py:539

commit v6 on v5

--- a/solution.py
+++ b/solution.py
@@ -342,18 +342,28 @@
     return {OUTER + k: layer for k, layer in enumerate(found)}
 
 
-def inside_kernel(edge, middle, last, inner, beyond, moved, wall, out, flux_out, send, field, *more):
+def middle_kernel(edge, middle, last, moved, wall, flux_out, *slopes):
+    rows = moved.shape[2]
+
+    def work(i, h, r, donor):
+        speed = Layer(moved, i - 1, False).read(h, r)
+        Layer(flux_out, 0, False).write(h, r, face_flux(*donor(speed > 0.0), speed))
+
+    face_work(own_layers(edge, middle, last), wall, slopes, (OUTER + 1,), rows, work)
+
+
+def inside_kernel(edge, middle, last, inner, beyond, moved, wall, flux_low, out, send, field, *more):
     *slopes, flux = more
     rows = moved.shape[2]
     layers = own_layers(edge, middle, last)
     count = len(layers)
     layers.update(padded_halo(inner, field, [(0, OUTER + count)]))
     layers[OUTER + count + 1] = Layer(beyond, 0, False)
-    first_fluxes(layers, wall, moved, slopes, flux, range(OUTER + 1, OUTER + count))
-    copy_layer(Layer(flux, OUTER, False), Layer(flux_out, 0, False), rows)
-    for i in range(OUTER + 2, OUTER + count):
-        target = Layer(out, i - OUTER - 2)
-        update(target, layers[i], Layer(flux, i - 2, False), Layer(flux, i - 1, False), rows)
+    first_fluxes(layers, wall, moved, slopes, flux, range(OUTER + 2, OUTER + count))
+    fluxes = [Layer(flux_low, 0, False)] + [Layer(flux, i - 1, False) for i in range(OUTER + 2, OUTER + count)]
+    for k, i in enumerate(range(OUTER + 2, OUTER + count)):
+        target = Layer(out, k)
+        update(target, layers[i], fluxes[k], fluxes[k + 1], rows)
         target.wrap()
     copy_layer(Layer(out, count - 3), Layer(send, 0, False), rows)
 
@@ -642,17 +652,17 @@
         final = turn == STEPS - 1
         if turn > 0:
             flux = pltpu.VMEM(plain(count + 2), jnp.float32)
-            inside, flux_low, send_inner = call(
+            (flux_low,) = call(middle_kernel, "middle", [held(plain(1))], [], [*own, moved, wall], slopes[1:])
+            inside, send_inner = call(
                 inside_kernel,
                 "inside",
-                [held(padded(count - 2)), held(plain(1)), held(plain(1))],
+                [held(padded(count - 2)), held(plain(1))],
                 [],
-                [*own, inner, beyond, moved, wall],
+                [*own, inner, beyond, moved, wall, flux_low],
                 [*slopes, flux],
                 faces=0.1,
             )
             last, inner = last_second(inside, (OUTER + 2, True), send_inner)
-            outer, last = lax.optimization_barrier((outer, last))
             above, outside = call(
                 outside_kernel,
                 "outside",

time: 61.4 us -> 60.6 us (0.987)
    pallas_call x22 -> x23, Pallas kernels: 30.5 us -> 30.6 us  [call(): pl.pallas_call(kernel, out_shape=outs, in_specs=[IN_SMEM] * len(scalars)...]
  transfers between devices with their start and end apart: 15 -> 15, of which waited for: 7 -> 7; matrix products, arithmetic and copies ran while one was open for 0% -> 0% of each run, Pallas kernels for 44% -> 45%
where the time goes in v6:
time: 60.6 us; the launch traced here: 60.4 us
  Pallas kernels  32.5 us (54%)
  starting transfers between devices  17 us (28%)
  waiting for transfers between devices  10.6 us (17%)
    pallas_call x23, Pallas kernels, call(): pl.pallas_call(kernel, out_shape=outs, in_specs=[IN_SMEM] * len(scalars)...  30.6 us
    ppermute x11, starting transfers between devices, swap(): return lax.ppermute(array, 'gx', pairs)  15 us
    ppermute x4, waiting for transfers between devices, largest_round(): received = lax.ppermute(array, 'gx', pairs)  8.16 us
    ppermute x11, waiting for transfers between devices, swap(): return lax.ppermute(array, 'gx', pairs)  2.44 us
    ppermute x4, starting transfers between devices, largest_round(): received = lax.ppermute(array, 'gx', pairs)  2 us
    pallas_call x1, Pallas kernels, last_call(): pl.pallas_call(functools.partial(last_kernel, places=places), out_shape=j...  1.83 us
  transfers between devices with their start and end apart: 15, of which 7 were waited for; matrix products, arithmetic and copies ran while one was open for 0% of the time, Pallas kernels for 45%

profile of v6, /device:TPU:0, one launch (start us, length us, event | category | flops | bytes accessed | tf_op | source)
XLA Modules:
  0.0 60.4 jit_solution(13394544506465474902)
XLA Ops:
  0.0 1.8 %begin.1 = (f32[4,128,256]{2,1,0:T(8,128)S(1)}, f32[4,128,256]{2,1,0:T(8,128)S(1)}, f32[4,128,256]{2,1,0:T(8,128)S(1)}, f32[8,128]{1,0:T(8,128)S(1)}, f32[4,2,14...) custom-call(s32[1]{0:T(128)} %bitcast.odd_ref, f32[4,128,256]{2,1,0:T(8,128)} %fraction_in.1, s32[4,128,256]{2,1,0:T(8,128)} %mask_in.1, ...), custom_call_target="tpu_custom_call" | custom-call | flops 110000000 | bytes 1024 | tf_op jit(solution)/shard_map/begin/pallas_call | solution.py:531
  1.8 0.1 first_send.1
  1.9 5.5 %collective-permute-start.5 = (f32[5,2,128,128]{3,2,1,0:T(8,128)S(1)}, f32[5,2,128,128]{3,2,1,0:T(8,128)S(1)}, u32[]{:S(2)}, u32[]{:S(2)}) collective-permute-start(f32[5,2,128,128]{3,2,1,0:T(8,128)S(1)} %get-tuple-element.49), channel_id=1, source_target_pairs={{0,15},{1,2},{2,1},{3,4},{4,3},{5,6},{6,5},{7,8},{8,7},{9,10},{10,... | collective-permute-start | bytes 1966088 | tf_op jit(solution)/shard_map/ppermute | solution.py:549
  7.4 0.5 collective-permute-start
  7.9 1.2 %collective-permute-done = f32[8,128]{1,0:T(8,128)S(1)} collective-permute-done((f32[8,128]{1,0:T(8,128)S(1)}, f32[8,128]{1,0:T(8,128)S(1)}, u32[]{:S(2)}, u32[]{:S(2)}) %collective-permute-start) | collective-permute-done | bytes 4128 | tf_op jit(solution)/shard_map/ppermute | solution.py:558
  9.1 0.0 collective-permute-start.1
  9.1 0.4 wall.1.refs_0_
  9.5 0.0 collective-permute-done.2.refs_3_
  9.5 1.6 %prepare.3.refs_2_ = f32[18,2,128,128]{3,2,1,0:T(8,128)S(1)} custom-call(s32[1]{0:T(128)} %bitcast.odd_ref, f32[9,128,128]{2,1,0:T(8,128)S(1)} %wall.1.refs_0_, f32[4,128,256]{2,1,0:T(8,128)S(1)} %get-tuple-element.44.first.refs_1_, f32[4,2,144,128]{3,2,1,0:T(8,128)S(1)} %get-tuple-element.45.state.refs_2_.refs_3_, ...), custom_call_target="tpu_custom_call" | custom-call | flops 22000000 | bytes 1024 | tf_op jit(solution)/shard_map/prepare/pallas_call | solution.py:531
  11.1 4.5 %collective-permute-done.1 = f32[8,128]{1,0:T(8,128)S(1)} collective-permute-done((f32[8,128]{1,0:T(8,128)S(1)}, f32[8,128]{1,0:T(8,128)S(1)}, u32[]{:S(2)}, u32[]{:S(2)}) %collective-permute-start.1) | collective-permute-done | bytes 4128 | tf_op jit(solution)/shard_map/ppermute | solution.py:558
  15.7 1.5 %collective-permute-start.3 = (f32[8,128]{1,0:T(8,128)S(1)}, f32[8,128]{1,0:T(8,128)S(1)}, u32[]{:S(2)}, u32[]{:S(2)}) collective-permute-start(f32[8,128]{1,0:T(8,128)S(1)} %max.13), channel_id=1, source_target_pairs={{0,4},{1,5},{2,6},{3,7},{4,0},{5,1},{6,2},{7,3},{8,12},{9,13},{10,... | collective-permute-start | bytes 12296 | tf_op jit(solution)/shard_map/ppermute | solution.py:558
  17.1 0.9 %prepare.4.refs_1_ = f32[9,2,128,128]{3,2,1,0:T(8,128)S(1)} custom-call(s32[1]{0:T(128)} %bitcast.odd_ref, f32[9,128,128]{2,1,0:T(8,128)S(1)} %wall.1.refs_0_, f32[4,128,256]{2,1,0:T(8,128)S(1)} %get-tuple-element.44.first.refs_1_, f32[4,2,144,128]{3,2,1,0:T(8,128)S(1)} %get-tuple-element.45.state.refs_2_.refs_3_, ...), custom_call_target="tpu_custom_call" | custom-call | flops 22000000 | bytes 1024 | tf_op jit(solution)/shard_map/prepare/pallas_call | solution.py:531
  18.1 1.2 %collective-permute-done.3 = f32[8,128]{1,0:T(8,128)S(1)} collective-permute-done((f32[8,128]{1,0:T(8,128)S(1)}, f32[8,128]{1,0:T(8,128)S(1)}, u32[]{:S(2)}, u32[]{:S(2)}) %collective-permute-start.3) | collective-permute-done | bytes 4128 | tf_op jit(solution)/shard_map/ppermute | solution.py:558
  19.3 0.0 collective-permute-start.4
  19.3 0.0 collective-permute-done.5.refs_3_.refs_4_
  19.3 2.4 %prepare.5.refs_0_ = f32[27,2,128,128]{3,2,1,0:T(8,128)S(1)} custom-call(s32[1]{0:T(128)} %bitcast.odd_ref, f32[9,128,128]{2,1,0:T(8,128)S(1)} %wall.1.refs_0_, f32[4,128,256]{2,1,0:T(8,128)S(1)} %get-tuple-element.44.first.refs_1_, f32[4,2,144,128]{3,2,1,0:T(8,128)S(1)} %get-tuple-element.45.state.refs_2_.refs_3_, ...), custom_call_target="tpu_custom_call" | custom-call | flops 22000000 | bytes 1024 | tf_op jit(solution)/shard_map/prepare/pallas_call | solution.py:531
  21.6 1.2 %collective-permute-done.4 = f32[8,128]{1,0:T(8,128)S(1)} collective-permute-done((f32[8,128]{1,0:T(8,128)S(1)}, f32[8,128]{1,0:T(8,128)S(1)}, u32[]{:S(2)}, u32[]{:S(2)}) %collective-permute-start.4) | collective-permute-done | bytes 4128 | tf_op jit(solution)/shard_map/ppermute | solution.py:558
  22.9 1.5 %finish.1 = (f32[4,2,144,128]{3,2,1,0:T(8,128)S(1)}, f32[1,2,128,128]{3,2,1,0:T(8,128)S(1)}, f32[6,2,128,128]{3,2,1,0:T(8,128)S(1)}, f32[8,128]{1,0:T(8,128)S(1)}, f32[1,2,128,128]{3,2,1,0:T(8,128)S(1)}) custom-call(f32[8,128]{1,0:T(8,128)S(1)} %max.15.peak, f32[27,2,128,128]{3,2,1,0:T(8,128)S(1)} %prepare.5.refs_0_, f32[9,2,128,128]{3,2,1,0:T(8,128)S(1)} %prepare.4.refs_1_, ...), custom_call_target="tpu_custom_call" | custom-call | flops 1100000000 | bytes 1024 | tf_op jit(solution)/shard_map/finish/pallas_call | solution.py:531
  24.4 0.1 collective-permute-start.7
  24.5 1.1 %second.6 = (f32[1,2,144,128]{3,2,1,0:T(8,128)S(1)}, f32[1,2,128,128]{3,2,1,0:T(8,128)S(1)}) custom-call(s32[1]{0:T(128)} %bitcast.odd_ref, f32[8,128]{1,0:T(8,128)S(1)} %get-tuple-element.51.step, f32[4,128,256]{2,1,0:T(8,128)S(1)} %get-tuple-element.53.speed_ref, f32[9,128,128]{2,1,0:T(8,128)S(1)} %wall.1.refs_0_, ...), custom_call_target="tpu_custom_call" | custom-call | flops 1100000000 | bytes 1024 | tf_op jit(solution)/shard_map/second/pallas_call | solution.py:531
  25.5 4.6 %collective-permute-start.6 = (f32[1,2,128,128]{3,2,1,0:T(8,128)S(1)}, f32[1,2,128,128]{3,2,1,0:T(8,128)S(1)}, u32[]{:S(2)}, u32[]{:S(2)}) collective-permute-start(f32[1,2,128,128]{3,2,1,0:T(8,128)S(1)} %get-tuple-element.56), channel_id=1, source_target_pairs={{0,15},{1,2},{2,1},{3,4},{4,3},{5,6},{6,5},{7,8},{8,7},{9,10},{10,... | collective-permute-start | bytes 393224 | tf_op jit(solution)/shard_map/ppermute | solution.py:549
  30.2 2.0 %second.7.refs_2_.refs_1_.refs_0_ = f32[2,2,144,128]{3,2,1,0:T(8,128)S(1)} custom-call(s32[1]{0:T(128)} %bitcast.odd_ref, f32[8,128]{1,0:T(8,128)S(1)} %get-tuple-element.51.step, f32[4,128,256]{2,1,0:T(8,128)S(1)} %get-tuple-element.53.speed_ref, f32[9,128,128]{2,1,0:T(8,128)S(1)} %wall.1.refs_0_, f32[4,2,144,128]{3,2,1,0:T(8,128)S(1)} %get-tuple-element.58.refs_1_.refs_0_), custom_call_target="tpu_custom_call" | custom-call | flops 2200000000 | bytes 1024 | tf_op jit(solution)/shard_map/second/pallas_call | solution.py:531
  32.1 0.0 collective-permute-done.7.refs_1_
  32.2 1.1 %second.8 = (f32[1,2,144,128]{3,2,1,0:T(8,128)S(1)}, f32[1,2,128,128]{3,2,1,0:T(8,128)S(1)}) custom-call(s32[1]{0:T(128)} %bitcast.odd_ref, f32[8,128]{1,0:T(8,128)S(1)} %get-tuple-element.51.step, f32[4,128,256]{2,1,0:T(8,128)S(1)} %get-tuple-element.53.speed_ref, f32[9,128,128]{2,1,0:T(8,128)S(1)} %wall.1.refs_0_, ...), custom_call_target="tpu_custom_call" | custom-call | flops 110000000 | bytes 1024 | tf_op jit(solution)/shard_map/second/pallas_call | solution.py:531
  33.2 0.1 collective-permute-start.9
  33.3 2.2 %third.6.middle = f32[2,2,144,128]{3,2,1,0:T(8,128)S(1)} custom-call(s32[1]{0:T(128)} %bitcast.odd_ref, f32[8,128]{1,0:T(8,128)S(1)} %get-tuple-element.51.step, f32[4,128,256]{2,1,0:T(8,128)S(1)} %get-tuple-element.52.speed_ref, f32[9,128,128]{2,1,0:T(8,128)S(1)} %wall.1.refs_0_, f32[1,2,144,128]{3,2,1,0:T(8,128)S(1)} %get-tuple-element.57.refs_1_.refs_0_, ...), custom_call_target="tpu_custom_call" | custom-call | flops 2200000000 | bytes 1024 | tf_op jit(solution)/shard_map/third/pallas_call | solution.py:531
  35.4 0.0 collective-permute-done.6.refs_0_
  35.5 1.1 %third.5.edge = f32[1,2,144,128]{3,2,1,0:T(8,128)S(1)} custom-call(s32[1]{0:T(128)} %bitcast.odd_ref, f32[8,128]{1,0:T(8,128)S(1)} %get-tuple-element.51.step, f32[4,128,256]{2,1,0:T(8,128)S(1)} %get-tuple-element.52.speed_ref, f32[9,128,128]{2,1,0:T(8,128)S(1)} %wall.1.refs_0_, f32[1,2,128,128]{3,2,1,0:T(8,128)S(1)} %collective-permute-done.6.refs_0_, ...), custom_call_target="tpu_custom_call" | custom-call | flops 1100000000 | bytes 1024 | tf_op jit(solution)/shard_map/third/pallas_call | solution.py:531
  36.6 0.6 collective-permute-start.8
  37.2 1.4 %collective-permute-start.10 = (f32[3,2,128,128]{3,2,1,0:T(8,128)S(1)}, f32[3,2,128,128]{3,2,1,0:T(8,128)S(1)}, u32[]{:S(2)}, u32[]{:S(2)}) collective-permute-start(f32[3,2,128,128]{3,2,1,0:T(8,128)S(1)} %get-tuple-element.66), channel_id=1, source_target_pairs={{0,15},{1,2},{2,1},{3,4},{4,3},{5,6},{6,5},{7,8},{8,7},{9,10},{10,... | collective-permute-start | bytes 1179656 | tf_op jit(solution)/shard_map/ppermute | solution.py:549
  38.5 1.1 %third.7.last = f32[1,2,144,128]{3,2,1,0:T(8,128)S(1)} custom-call(s32[1]{0:T(128)} %bitcast.odd_ref, f32[8,128]{1,0:T(8,128)S(1)} %get-tuple-element.51.step, f32[4,128,256]{2,1,0:T(8,128)S(1)} %get-tuple-element.52.speed_ref, f32[9,128,128]{2,1,0:T(8,128)S(1)} %wall.1.refs_0_, f32[2,2,144,128]{3,2,1,0:T(8,128)S(1)} %second.7.refs_2_.refs_1_.refs_0_, ...), custom_call_target="tpu_custom_call" | custom-call | flops 1100000000 | bytes 1024 | tf_op jit(solution)/shard_map/third/pallas_call | solution.py:531
  39.7 0.1 collective-permute-start.12
  39.7 1.1 %middle.1.flux_above.flux_low = f32[1,2,128,128]{3,2,1,0:T(8,128)S(1)} custom-call(f32[1,2,144,128]{3,2,1,0:T(8,128)S(1)} %third.5.edge, f32[2,2,144,128]{3,2,1,0:T(8,128)S(1)} %third.6.middle, f32[1,2,144,128]{3,2,1,0:T(8,128)S(1)} %third.7.last, f32[6,2,128,128]{3,2,1,0:T(8,128)S(1)} %get-tuple-element.67.moved, f32[9,128,128]{2,1,0:T(8,128)S(1)} %wall.1.refs_0_), custom_call_target="tpu_custom_call" | custom-call | flops 110000000 | bytes 1024 | tf_op jit(solution)/shard_map/middle/pallas_call | solution.py:531
  40.8 0.2 collective-permute-done.12.inner
  41.1 2.0 %inside.1 = (f32[2,2,144,128]{3,2,1,0:T(8,128)S(1)}, f32[1,2,128,128]{3,2,1,0:T(8,128)S(1)}) custom-call(f32[1,2,144,128]{3,2,1,0:T(8,128)S(1)} %third.5.edge, f32[2,2,144,128]{3,2,1,0:T(8,128)S(1)} %third.6.middle, f32[1,2,144,128]{3,2,1,0:T(8,128)S(1)} %third.7.last, f32[1,2,128,128]{3,2,1,0:T(8,128)S(1)} %collective-permute-done.12.inner, ...), custom_call_target="tpu_custom_call" | custom-call | flops 110000000 | bytes 1024 | tf_op jit(solution)/shard_map/inside/pallas_call | solution.py:531
  43.1 0.3 collective-permute-start.13
  43.4 1.1 %collective-permute-done.13.refs_1_ = f32[1,2,128,128]{3,2,1,0:T(8,128)S(1)} collective-permute-done((f32[1,2,128,128]{3,2,1,0:T(8,128)S(1)}, f32[1,2,128,128]{3,2,1,0:T(8,128)S(1)}, u32[]{:S(2)}, u32[]{:S(2)}) %collective-permute-start.13) | collective-permute-done | bytes 131104 | tf_op jit(solution)/shard_map/ppermute | solution.py:549
  44.5 1.3 %second.11 = (f32[1,2,144,128]{3,2,1,0:T(8,128)S(1)}, f32[1,2,128,128]{3,2,1,0:T(8,128)S(1)}) custom-call(s32[1]{0:T(128)} %bitcast.odd_ref, f32[8,128]{1,0:T(8,128)S(1)} %get-tuple-element.51.step, f32[4,128,256]{2,1,0:T(8,128)S(1)} %get-tuple-element.53.speed_ref, f32[9,128,128]{2,1,0:T(8,128)S(1)} %wall.1.refs_0_, ...), custom_call_target="tpu_custom_call" | custom-call | flops 110000000 | bytes 1024 | tf_op jit(solution)/shard_map/second/pallas_call | solution.py:531
  45.8 0.3 collective-permute-start.14
  46.1 1.1 %collective-permute-done.10.outer = f32[3,2,128,128]{3,2,1,0:T(8,128)S(1)} collective-permute-done((f32[3,2,128,128]{3,2,1,0:T(8,128)S(1)}, f32[3,2,128,128]{3,2,1,0:T(8,128)S(1)}, u32[]{:S(2)}, u32[]{:S(2)}) %collective-permute-start.10) | collective-permute-done | bytes 393248 | tf_op jit(solution)/shard_map/ppermute | solution.py:549
  47.2 2.9 %outside.1 = (f32[1,2,128,128]{3,2,1,0:T(8,128)S(1)}, f32[2,2,144,128]{3,2,1,0:T(8,128)S(1)}) custom-call(f32[1,2,144,128]{3,2,1,0:T(8,128)S(1)} %third.5.edge, f32[2,2,144,128]{3,2,1,0:T(8,128)S(1)} %third.6.middle, f32[1,2,144,128]{3,2,1,0:T(8,128)S(1)} %third.7.last, f32[3,2,128,128]{3,2,1,0:T(8,128)S(1)} %collective-permute-done.10.outer, ...), custom_call_target="tpu_custom_call" | custom-call | flops 3300000000 | bytes 1024 | tf_op jit(solution)/shard_map/outside/pallas_call | solution.py:531
  50.1 1.0 %second.9 = (f32[1,2,144,128]{3,2,1,0:T(8,128)S(1)}, f32[1,2,128,128]{3,2,1,0:T(8,128)S(1)}) custom-call(s32[1]{0:T(128)} %bitcast.odd_ref, f32[8,128]{1,0:T(8,128)S(1)} %get-tuple-element.51.step, f32[4,128,256]{2,1,0:T(8,128)S(1)} %get-tuple-element.53.speed_ref, f32[9,128,128]{2,1,0:T(8,128)S(1)} %wall.1.refs_0_, ...), custom_call_target="tpu_custom_call" | custom-call | flops 1100000000 | bytes 1024 | tf_op jit(solution)/shard_map/second/pallas_call | solution.py:531
  51.1 2.1 %collective-permute-start.11 = (f32[1,2,128,128]{3,2,1,0:T(8,128)S(1)}, f32[1,2,128,128]{3,2,1,0:T(8,128)S(1)}, u32[]{:S(2)}, u32[]{:S(2)}) collective-permute-start(f32[1,2,128,128]{3,2,1,0:T(8,128)S(1)} %get-tuple-element.70), channel_id=1, source_target_pairs={{0,15},{1,2},{2,1},{3,4},{4,3},{5,6},{6,5},{7,8},{8,7},{9,10},{10,... | collective-permute-start | bytes 393224 | tf_op jit(solution)/shard_map/ppermute | solution.py:549
  53.2 2.0 %second.10.refs_1_.refs_0_.refs_2_ = f32[2,2,144,128]{3,2,1,0:T(8,128)S(1)} custom-call(s32[1]{0:T(128)} %bitcast.odd_ref, f32[8,128]{1,0:T(8,128)S(1)} %get-tuple-element.51.step, f32[4,128,256]{2,1,0:T(8,128)S(1)} %get-tuple-element.53.speed_ref, f32[9,128,128]{2,1,0:T(8,128)S(1)} %wall.1.refs_0_, ...), custom_call_target="tpu_custom_call" | custom-call | flops 2200000000 | bytes 1024 | tf_op jit(solution)/shard_map/second/pallas_call | solution.py:531
  55.2 2.2 %third.8.refs_3_ = f32[2,2,144,128]{3,2,1,0:T(8,128)S(1)} custom-call(s32[1]{0:T(128)} %bitcast.odd_ref, f32[8,128]{1,0:T(8,128)S(1)} %get-tuple-element.51.step, f32[4,128,256]{2,1,0:T(8,128)S(1)} %get-tuple-element.52.speed_ref, f32[9,128,128]{2,1,0:T(8,128)S(1)} %wall.1.refs_0_, f32[1,2,144,128]{3,2,1,0:T(8,128)S(1)} %get-tuple-element.71.refs_0_.refs_1_, ...), custom_call_target="tpu_custom_call" | custom-call | flops 2200000000 | bytes 1024 | tf_op jit(solution)/shard_map/third/pallas_call | solution.py:531
  57.3 0.0 collective-permute-done.14.refs_2_
  57.3 1.1 %third.9.refs_4_ = f32[1,2,144,128]{3,2,1,0:T(8,128)S(1)} custom-call(s32[1]{0:T(128)} %bitcast.odd_ref, f32[8,128]{1,0:T(8,128)S(1)} %get-tuple-element.51.step, f32[4,128,256]{2,1,0:T(8,128)S(1)} %get-tuple-element.52.speed_ref, f32[9,128,128]{2,1,0:T(8,128)S(1)} %wall.1.refs_0_, f32[2,2,144,128]{3,2,1,0:T(8,128)S(1)} %second.10.refs_1_.refs_0_.refs_2_, ...), custom_call_target="tpu_custom_call" | custom-call | flops 1100000000 | bytes 1024 | tf_op jit(solution)/shard_map/third/pallas_call | solution.py:531
  58.4 1.8 %last.1 = f32[4,128,256]{2,1,0:T(8,128)} custom-call(s32[1]{0:T(128)} %bitcast.odd_ref, f32[8,128]{1,0:T(8,128)S(1)} %get-tuple-element.51.step, f32[4,128,256]{2,1,0:T(8,128)S(1)} %get-tuple-element.52.speed_ref, f32[9,128,128]{2,1,0:T(8,128)S(1)} %wall.1.refs_0_, f32[1,2,128,128]{3,2,1,0:T(8,128)S(1)} %collective-permute-done.11.refs_0_, ...), custom_call_target="tpu_custom_call" | custom-call | flops 1100000000 | bytes 1024 | tf_op jit(solution)/shard_map/last/pallas_call | solution.py:717
  (10 shorter events, 0.1 us)
Async XLA Ops:
  1.9 17.4 %collective-permute-start.5 = (f32[5,2,128,128]{3,2,1,0:T(8,128)S(1)}, f32[5,2,128,128]{3,2,1,0:T(8,128)S(1)}, u32[]{:S(2)}, u32[]{:S(2)}) collective-permute-start(f32[5,2,128,128]{3,2,1,0:T(8,128)S(1)} %get-tuple-element.49), channel_id=1, source_target_pairs={{0,15},{1,2},{2,1},{3,4},{4,3},{5,6},{6,5},{7,8},{8,7},{9,10},{10,... | collective-permute-start | bytes 1966088 | tf_op jit(solution)/shard_map/ppermute | solution.py:549
  7.4 2.1 %collective-permute-start.2 = (f32[3,2,128,128]{3,2,1,0:T(8,128)S(1)}, f32[3,2,128,128]{3,2,1,0:T(8,128)S(1)}, u32[]{:S(2)}, u32[]{:S(2)}) collective-permute-start(f32[3,2,128,128]{3,2,1,0:T(8,128)S(1)} %get-tuple-element.46), channel_id=1, source_target_pairs={{0,1},{1,0},{2,3},{3,2},{4,5},{5,4},{6,7},{7,6},{8,9},{9,8},{10,11... | collective-permute-start | bytes 1179656 | tf_op jit(solution)/shard_map/ppermute | solution.py:549
  7.4 1.7 %collective-permute-start = (f32[8,128]{1,0:T(8,128)S(1)}, f32[8,128]{1,0:T(8,128)S(1)}, u32[]{:S(2)}, u32[]{:S(2)}) collective-permute-start(f32[8,128]{1,0:T(8,128)S(1)} %get-tuple-element.42), channel_id=1, source_target_pairs={{0,1},{1,0},{2,3},{3,2},{4,5},{5,4},{6,7},{7,6},{8,9},{9,8},{10,11... | collective-permute-start | bytes 12296 | tf_op jit(solution)/shard_map/ppermute | solution.py:558
  9.1 6.5 %collective-permute-start.1 = (f32[8,128]{1,0:T(8,128)S(1)}, f32[8,128]{1,0:T(8,128)S(1)}, u32[]{:S(2)}, u32[]{:S(2)}) collective-permute-start(f32[8,128]{1,0:T(8,128)S(1)} %max.12), channel_id=1, source_target_pairs={{0,8},{1,9},{2,10},{3,11},{4,12},{5,13},{6,14},{7,15},{8,0},{9,1},... | collective-permute-start | bytes 12296 | tf_op jit(solution)/shard_map/ppermute | solution.py:558
  15.7 3.6 %collective-permute-start.3 = (f32[8,128]{1,0:T(8,128)S(1)}, f32[8,128]{1,0:T(8,128)S(1)}, u32[]{:S(2)}, u32[]{:S(2)}) collective-permute-start(f32[8,128]{1,0:T(8,128)S(1)} %max.13), channel_id=1, source_target_pairs={{0,4},{1,5},{2,6},{3,7},{4,0},{5,1},{6,2},{7,3},{8,12},{9,13},{10,... | collective-permute-start | bytes 12296 | tf_op jit(solution)/shard_map/ppermute | solution.py:558
  19.3 3.6 %collective-permute-start.4 = (f32[8,128]{1,0:T(8,128)S(1)}, f32[8,128]{1,0:T(8,128)S(1)}, u32[]{:S(2)}, u32[]{:S(2)}) collective-permute-start(f32[8,128]{1,0:T(8,128)S(1)} %max.14), channel_id=1, source_target_pairs={{0,2},{1,3},{2,0},{3,1},{4,6},{5,7},{6,4},{7,5},{8,10},{9,11},{10,... | collective-permute-start | bytes 12296 | tf_op jit(solution)/shard_map/ppermute | solution.py:558
  24.4 7.8 %collective-permute-start.7 = (f32[1,2,128,128]{3,2,1,0:T(8,128)S(1)}, f32[1,2,128,128]{3,2,1,0:T(8,128)S(1)}, u32[]{:S(2)}, u32[]{:S(2)}) collective-permute-start(f32[1,2,128,128]{3,2,1,0:T(8,128)S(1)} %get-tuple-element.59), channel_id=1, source_target_pairs={{0,1},{1,0},{2,3},{3,2},{4,5},{5,4},{6,7},{7,6},{8,9},{9,8},{10,11... | collective-permute-start | bytes 393224 | tf_op jit(solution)/shard_map/ppermute | solution.py:549
  25.5 9.9 %collective-permute-start.6 = (f32[1,2,128,128]{3,2,1,0:T(8,128)S(1)}, f32[1,2,128,128]{3,2,1,0:T(8,128)S(1)}, u32[]{:S(2)}, u32[]{:S(2)}) collective-permute-start(f32[1,2,128,128]{3,2,1,0:T(8,128)S(1)} %get-tuple-element.56), channel_id=1, source_target_pairs={{0,15},{1,2},{2,1},{3,4},{4,3},{5,6},{6,5},{7,8},{8,7},{9,10},{10,... | collective-permute-start | bytes 393224 | tf_op jit(solution)/shard_map/ppermute | solution.py:549
  33.2 5.3 %collective-permute-start.9 = (f32[1,2,128,128]{3,2,1,0:T(8,128)S(1)}, f32[1,2,128,128]{3,2,1,0:T(8,128)S(1)}, u32[]{:S(2)}, u32[]{:S(2)}) collective-permute-start(f32[1,2,128,128]{3,2,1,0:T(8,128)S(1)} %get-tuple-element.62), channel_id=1, source_target_pairs={{0,1},{1,0},{2,3},{3,2},{4,5},{5,4},{6,7},{7,6},{8,9},{9,8},{10,11... | collective-permute-start | bytes 393224 | tf_op jit(solution)/shard_map/ppermute | solution.py:549
  36.6 1.9 %collective-permute-start.8 = (f32[1,2,128,128]{3,2,1,0:T(8,128)S(1)}, f32[1,2,128,128]{3,2,1,0:T(8,128)S(1)}, u32[]{:S(2)}, u32[]{:S(2)}) collective-permute-start(f32[1,2,128,128]{3,2,1,0:T(8,128)S(1)} %get-tuple-element.61), channel_id=1, source_target_pairs={{0,1},{1,0},{2,3},{3,2},{4,5},{5,4},{6,7},{7,6},{8,9},{9,8},{10,11... | collective-permute-start | bytes 393224 | tf_op jit(solution)/shard_map/ppermute | solution.py:549
  37.2 10.0 %collective-permute-start.10 = (f32[3,2,128,128]{3,2,1,0:T(8,128)S(1)}, f32[3,2,128,128]{3,2,1,0:T(8,128)S(1)}, u32[]{:S(2)}, u32[]{:S(2)}) collective-permute-start(f32[3,2,128,128]{3,2,1,0:T(8,128)S(1)} %get-tuple-element.66), channel_id=1, source_target_pairs={{0,15},{1,2},{2,1},{3,4},{4,3},{5,6},{6,5},{7,8},{8,7},{9,10},{10,... | collective-permute-start | bytes 1179656 | tf_op jit(solution)/shard_map/ppermute | solution.py:549
  39.7 1.4 %collective-permute-start.12 = (f32[1,2,128,128]{3,2,1,0:T(8,128)S(1)}, f32[1,2,128,128]{3,2,1,0:T(8,128)S(1)}, u32[]{:S(2)}, u32[]{:S(2)}) collective-permute-start(f32[1,2,128,128]{3,2,1,0:T(8,128)S(1)} %strip.1), channel_id=1, source_target_pairs={{0,1},{1,0},{2,3},{3,2},{4,5},{5,4},{6,7},{7,6},{8,9},{9,8},{10,11... | collective-permute-start | bytes 393224 | tf_op jit(solution)/shard_map/ppermute | solution.py:549
  43.1 1.4 %collective-permute-start.13 = (f32[1,2,128,128]{3,2,1,0:T(8,128)S(1)}, f32[1,2,128,128]{3,2,1,0:T(8,128)S(1)}, u32[]{:S(2)}, u32[]{:S(2)}) collective-permute-start(f32[1,2,128,128]{3,2,1,0:T(8,128)S(1)} %get-tuple-element.76), channel_id=1, source_target_pairs={{0,1},{1,0},{2,3},{3,2},{4,5},{5,4},{6,7},{7,6},{8,9},{9,8},{10,11... | collective-permute-start | bytes 393224 | tf_op jit(solution)/shard_map/ppermute | solution.py:549
  45.8 11.6 %collective-permute-start.14 = (f32[1,2,128,128]{3,2,1,0:T(8,128)S(1)}, f32[1,2,128,128]{3,2,1,0:T(8,128)S(1)}, u32[]{:S(2)}, u32[]{:S(2)}) collective-permute-start(f32[1,2,128,128]{3,2,1,0:T(8,128)S(1)} %get-tuple-element.78), channel_id=1, source_target_pairs={{0,1},{1,0},{2,3},{3,2},{4,5},{5,4},{6,7},{7,6},{8,9},{9,8},{10,11... | collective-permute-start | bytes 393224 | tf_op jit(solution)/shard_map/ppermute | solution.py:549
  51.1 7.3 %collective-permute-start.11 = (f32[1,2,128,128]{3,2,1,0:T(8,128)S(1)}, f32[1,2,128,128]{3,2,1,0:T(8,128)S(1)}, u32[]{:S(2)}, u32[]{:S(2)}) collective-permute-start(f32[1,2,128,128]{3,2,1,0:T(8,128)S(1)} %get-tuple-element.70), channel_id=1, source_target_pairs={{0,15},{1,2},{2,1},{3,4},{4,3},{5,6},{6,5},{7,8},{8,7},{9,10},{10,... | collective-permute-start | bytes 393224 | tf_op jit(solution)/shard_map/ppermute | solution.py:549

commit v7 on v6

--- a/solution.py
+++ b/solution.py
@@ -674,9 +674,10 @@
             )
             swept = [above, outside, inside]
             places = [(OUTER - 1, False), (OUTER, True), (OUTER + 2, True)]
-        else:
+        edge, send_outer = second_call((OUTER,), swept[:2], places[:2], True)
+        if turn == 0:
+            send_outer, send_inner = lax.optimization_barrier((send_outer, send_inner))
             last, inner = last_second(swept[-1], places[-1], send_inner)
-        edge, send_outer = second_call((OUTER,), swept[:2], places[:2], True)
         after = lax.optimization_barrier((edge, *swept[1:]))[1:]
         (middle,) = second_call(tuple(range(OUTER + 1, own_end - 1)), after, places[1:], False)
         outer = swap(send_outer, True)

time: 60.6 us -> 58.6 us (0.967)
  waiting for transfers between devices: 10.6 us -> 9.53 us
  starting transfers between devices: 17 us -> 16.1 us
    ppermute x11, waiting for transfers between devices: 2.44 us -> 1.36 us  [swap(): return lax.ppermute(array, 'gx', pairs)]
    ppermute x11, starting transfers between devices: 15 us -> 14.1 us  [swap(): return lax.ppermute(array, 'gx', pairs)]
  transfers between devices with their start and end apart: 15 -> 15, of which waited for: 7 -> 6; matrix products, arithmetic and copies ran while one was open for 0% -> 0% of each run, Pallas kernels for 45% -> 45%
where the time goes in v7:
time: 58.6 us; the launch traced here: 58.5 us
  Pallas kernels  32.5 us (55%)
  starting transfers between devices  16.1 us (27%)
  waiting for transfers between devices  9.53 us (16%)
    pallas_call x23, Pallas kernels, call(): pl.pallas_call(kernel, out_shape=outs, in_specs=[IN_SMEM] * len(scalars)...  30.6 us
    ppermute x11, starting transfers between devices, swap(): return lax.ppermute(array, 'gx', pairs)  14.1 us
    ppermute x4, waiting for transfers between devices, largest_round(): received = lax.ppermute(array, 'gx', pairs)  8.16 us
    ppermute x4, starting transfers between devices, largest_round(): received = lax.ppermute(array, 'gx', pairs)  2 us
    pallas_call x1, Pallas kernels, last_call(): pl.pallas_call(functools.partial(last_kernel, places=places), out_shape=j...  1.83 us
    ppermute x11, waiting for transfers between devices, swap(): return lax.ppermute(array, 'gx', pairs)  1.36 us
  transfers between devices with their start and end apart: 15, of which 6 were waited for; matrix products, arithmetic and copies ran while one was open for 0% of the time, Pallas kernels for 45%

profile of v7, /device:TPU:0, one launch (start us, length us, event | category | flops | bytes accessed | tf_op | source)
XLA Modules:
  0.0 58.5 jit_solution(1073510515233865700)
XLA Ops:
  0.0 1.8 %begin.1 = (f32[4,128,256]{2,1,0:T(8,128)S(1)}, f32[4,128,256]{2,1,0:T(8,128)S(1)}, f32[4,128,256]{2,1,0:T(8,128)S(1)}, f32[8,128]{1,0:T(8,128)S(1)}, f32[4,2,14...) custom-call(s32[1]{0:T(128)} %bitcast.odd_ref, f32[4,128,256]{2,1,0:T(8,128)} %fraction_in.1, s32[4,128,256]{2,1,0:T(8,128)} %mask_in.1, ...), custom_call_target="tpu_custom_call" | custom-call | flops 110000000 | bytes 1024 | tf_op jit(solution)/shard_map/begin/pallas_call | solution.py:531
  1.8 0.1 first_send.1
  1.9 5.5 %collective-permute-start.5 = (f32[5,2,128,128]{3,2,1,0:T(8,128)S(1)}, f32[5,2,128,128]{3,2,1,0:T(8,128)S(1)}, u32[]{:S(2)}, u32[]{:S(2)}) collective-permute-start(f32[5,2,128,128]{3,2,1,0:T(8,128)S(1)} %get-tuple-element.51), channel_id=1, source_target_pairs={{0,15},{1,2},{2,1},{3,4},{4,3},{5,6},{6,5},{7,8},{8,7},{9,10},{10,... | collective-permute-start | bytes 1966088 | tf_op jit(solution)/shard_map/ppermute | solution.py:549
  7.4 0.0 collective-permute-start.2
  7.4 0.5 collective-permute-start
  7.9 1.2 %collective-permute-done = f32[8,128]{1,0:T(8,128)S(1)} collective-permute-done((f32[8,128]{1,0:T(8,128)S(1)}, f32[8,128]{1,0:T(8,128)S(1)}, u32[]{:S(2)}, u32[]{:S(2)}) %collective-permute-start) | collective-permute-done | bytes 4128 | tf_op jit(solution)/shard_map/ppermute | solution.py:558
  9.1 0.0 collective-permute-start.1
  9.1 0.4 wall.1.refs_0_
  9.5 0.0 collective-permute-done.2.refs_3_
  9.5 1.6 %prepare.3.refs_2_ = f32[18,2,128,128]{3,2,1,0:T(8,128)S(1)} custom-call(s32[1]{0:T(128)} %bitcast.odd_ref, f32[9,128,128]{2,1,0:T(8,128)S(1)} %wall.1.refs_0_, f32[4,128,256]{2,1,0:T(8,128)S(1)} %get-tuple-element.46.first.refs_1_, f32[4,2,144,128]{3,2,1,0:T(8,128)S(1)} %get-tuple-element.47.state.refs_2_.refs_3_, ...), custom_call_target="tpu_custom_call" | custom-call | flops 22000000 | bytes 1024 | tf_op jit(solution)/shard_map/prepare/pallas_call | solution.py:531
  11.1 4.5 %collective-permute-done.1 = f32[8,128]{1,0:T(8,128)S(1)} collective-permute-done((f32[8,128]{1,0:T(8,128)S(1)}, f32[8,128]{1,0:T(8,128)S(1)}, u32[]{:S(2)}, u32[]{:S(2)}) %collective-permute-start.1) | collective-permute-done | bytes 4128 | tf_op jit(solution)/shard_map/ppermute | solution.py:558
  15.7 1.5 %collective-permute-start.3 = (f32[8,128]{1,0:T(8,128)S(1)}, f32[8,128]{1,0:T(8,128)S(1)}, u32[]{:S(2)}, u32[]{:S(2)}) collective-permute-start(f32[8,128]{1,0:T(8,128)S(1)} %max.13), channel_id=1, source_target_pairs={{0,4},{1,5},{2,6},{3,7},{4,0},{5,1},{6,2},{7,3},{8,12},{9,13},{10,... | collective-permute-start | bytes 12296 | tf_op jit(solution)/shard_map/ppermute | solution.py:558
  17.1 0.9 %prepare.4.refs_1_ = f32[9,2,128,128]{3,2,1,0:T(8,128)S(1)} custom-call(s32[1]{0:T(128)} %bitcast.odd_ref, f32[9,128,128]{2,1,0:T(8,128)S(1)} %wall.1.refs_0_, f32[4,128,256]{2,1,0:T(8,128)S(1)} %get-tuple-element.46.first.refs_1_, f32[4,2,144,128]{3,2,1,0:T(8,128)S(1)} %get-tuple-element.47.state.refs_2_.refs_3_, ...), custom_call_target="tpu_custom_call" | custom-call | flops 22000000 | bytes 1024 | tf_op jit(solution)/shard_map/prepare/pallas_call | solution.py:531
  18.1 1.2 %collective-permute-done.3 = f32[8,128]{1,0:T(8,128)S(1)} collective-permute-done((f32[8,128]{1,0:T(8,128)S(1)}, f32[8,128]{1,0:T(8,128)S(1)}, u32[]{:S(2)}, u32[]{:S(2)}) %collective-permute-start.3) | collective-permute-done | bytes 4128 | tf_op jit(solution)/shard_map/ppermute | solution.py:558
  19.3 0.0 collective-permute-start.4
  19.3 0.0 collective-permute-done.5.refs_3_.refs_4_
  19.3 2.4 %prepare.5.refs_0_ = f32[27,2,128,128]{3,2,1,0:T(8,128)S(1)} custom-call(s32[1]{0:T(128)} %bitcast.odd_ref, f32[9,128,128]{2,1,0:T(8,128)S(1)} %wall.1.refs_0_, f32[4,128,256]{2,1,0:T(8,128)S(1)} %get-tuple-element.46.first.refs_1_, f32[4,2,144,128]{3,2,1,0:T(8,128)S(1)} %get-tuple-element.47.state.refs_2_.refs_3_, ...), custom_call_target="tpu_custom_call" | custom-call | flops 22000000 | bytes 1024 | tf_op jit(solution)/shard_map/prepare/pallas_call | solution.py:531
  21.6 1.2 %collective-permute-done.4 = f32[8,128]{1,0:T(8,128)S(1)} collective-permute-done((f32[8,128]{1,0:T(8,128)S(1)}, f32[8,128]{1,0:T(8,128)S(1)}, u32[]{:S(2)}, u32[]{:S(2)}) %collective-permute-start.4) | collective-permute-done | bytes 4128 | tf_op jit(solution)/shard_map/ppermute | solution.py:558
  22.9 1.5 %finish.1 = (f32[4,2,144,128]{3,2,1,0:T(8,128)S(1)}, f32[1,2,128,128]{3,2,1,0:T(8,128)S(1)}, f32[6,2,128,128]{3,2,1,0:T(8,128)S(1)}, f32[8,128]{1,0:T(8,128)S(1)}, f32[1,2,128,128]{3,2,1,0:T(8,128)S(1)}) custom-call(f32[8,128]{1,0:T(8,128)S(1)} %max.15.peak, f32[27,2,128,128]{3,2,1,0:T(8,128)S(1)} %prepare.5.refs_0_, f32[9,2,128,128]{3,2,1,0:T(8,128)S(1)} %prepare.4.refs_1_, ...), custom_call_target="tpu_custom_call" | custom-call | flops 1100000000 | bytes 1024 | tf_op jit(solution)/shard_map/finish/pallas_call | solution.py:531
  24.4 1.1 %second.6 = (f32[1,2,144,128]{3,2,1,0:T(8,128)S(1)}, f32[1,2,128,128]{3,2,1,0:T(8,128)S(1)}) custom-call(s32[1]{0:T(128)} %bitcast.odd_ref, f32[8,128]{1,0:T(8,128)S(1)} %get-tuple-element.53.step, f32[4,128,256]{2,1,0:T(8,128)S(1)} %get-tuple-element.55.speed_ref, f32[9,128,128]{2,1,0:T(8,128)S(1)} %wall.1.refs_0_, ...), custom_call_target="tpu_custom_call" | custom-call | flops 1100000000 | bytes 1024 | tf_op jit(solution)/shard_map/second/pallas_call | solution.py:531
  25.4 1.9 %collective-permute-start.6 = (f32[1,2,128,128]{3,2,1,0:T(8,128)S(1)}, f32[1,2,128,128]{3,2,1,0:T(8,128)S(1)}, u32[]{:S(2)}, u32[]{:S(2)}) collective-permute-start(f32[1,2,128,128]{3,2,1,0:T(8,128)S(1)} %get-tuple-element.60), channel_id=1, source_target_pairs={{0,15},{1,2},{2,1},{3,4},{4,3},{5,6},{6,5},{7,8},{8,7},{9,10},{10,... | collective-permute-start | bytes 393224 | tf_op jit(solution)/shard_map/ppermute | solution.py:549
  27.3 0.0 collective-permute-start.7
  27.3 2.0 %second.7.refs_2_.refs_1_.refs_0_ = f32[2,2,144,128]{3,2,1,0:T(8,128)S(1)} custom-call(s32[1]{0:T(128)} %bitcast.odd_ref, f32[8,128]{1,0:T(8,128)S(1)} %get-tuple-element.53.step, f32[4,128,256]{2,1,0:T(8,128)S(1)} %get-tuple-element.55.speed_ref, f32[9,128,128]{2,1,0:T(8,128)S(1)} %wall.1.refs_0_, f32[4,2,144,128]{3,2,1,0:T(8,128)S(1)} %get-tuple-element.62.refs_1_.refs_0_), custom_call_target="tpu_custom_call" | custom-call | flops 2200000000 | bytes 1024 | tf_op jit(solution)/shard_map/second/pallas_call | solution.py:531
  29.3 1.1 %second.8 = (f32[1,2,144,128]{3,2,1,0:T(8,128)S(1)}, f32[1,2,128,128]{3,2,1,0:T(8,128)S(1)}) custom-call(s32[1]{0:T(128)} %bitcast.odd_ref, f32[8,128]{1,0:T(8,128)S(1)} %get-tuple-element.53.step, f32[4,128,256]{2,1,0:T(8,128)S(1)} %get-tuple-element.55.speed_ref, f32[9,128,128]{2,1,0:T(8,128)S(1)} %wall.1.refs_0_, ...), custom_call_target="tpu_custom_call" | custom-call | flops 110000000 | bytes 1024 | tf_op jit(solution)/shard_map/second/pallas_call | solution.py:531
  30.4 0.6 collective-permute-start.9
  30.9 2.2 %third.6.middle = f32[2,2,144,128]{3,2,1,0:T(8,128)S(1)} custom-call(s32[1]{0:T(128)} %bitcast.odd_ref, f32[8,128]{1,0:T(8,128)S(1)} %get-tuple-element.53.step, f32[4,128,256]{2,1,0:T(8,128)S(1)} %get-tuple-element.54.speed_ref, f32[9,128,128]{2,1,0:T(8,128)S(1)} %wall.1.refs_0_, f32[1,2,144,128]{3,2,1,0:T(8,128)S(1)} %get-tuple-element.61.refs_1_.refs_0_, ...), custom_call_target="tpu_custom_call" | custom-call | flops 2200000000 | bytes 1024 | tf_op jit(solution)/shard_map/third/pallas_call | solution.py:531
  33.1 0.0 collective-permute-done.6.refs_0_
  33.1 1.1 %third.5.edge = f32[1,2,144,128]{3,2,1,0:T(8,128)S(1)} custom-call(s32[1]{0:T(128)} %bitcast.odd_ref, f32[8,128]{1,0:T(8,128)S(1)} %get-tuple-element.53.step, f32[4,128,256]{2,1,0:T(8,128)S(1)} %get-tuple-element.54.speed_ref, f32[9,128,128]{2,1,0:T(8,128)S(1)} %wall.1.refs_0_, f32[1,2,128,128]{3,2,1,0:T(8,128)S(1)} %collective-permute-done.6.refs_0_, ...), custom_call_target="tpu_custom_call" | custom-call | flops 1100000000 | bytes 1024 | tf_op jit(solution)/shard_map/third/pallas_call | solution.py:531
  34.3 0.1 collective-permute-start.8
  34.4 2.8 %collective-permute-start.10 = (f32[3,2,128,128]{3,2,1,0:T(8,128)S(1)}, f32[3,2,128,128]{3,2,1,0:T(8,128)S(1)}, u32[]{:S(2)}, u32[]{:S(2)}) collective-permute-start(f32[3,2,128,128]{3,2,1,0:T(8,128)S(1)} %get-tuple-element.70), channel_id=1, source_target_pairs={{0,15},{1,2},{2,1},{3,4},{4,3},{5,6},{6,5},{7,8},{8,7},{9,10},{10,... | collective-permute-start | bytes 1179656 | tf_op jit(solution)/shard_map/ppermute | solution.py:549
  37.2 1.1 %third.7.last = f32[1,2,144,128]{3,2,1,0:T(8,128)S(1)} custom-call(s32[1]{0:T(128)} %bitcast.odd_ref, f32[8,128]{1,0:T(8,128)S(1)} %get-tuple-element.53.step, f32[4,128,256]{2,1,0:T(8,128)S(1)} %get-tuple-element.54.speed_ref, f32[9,128,128]{2,1,0:T(8,128)S(1)} %wall.1.refs_0_, f32[2,2,144,128]{3,2,1,0:T(8,128)S(1)} %second.7.refs_2_.refs_1_.refs_0_, ...), custom_call_target="tpu_custom_call" | custom-call | flops 1100000000 | bytes 1024 | tf_op jit(solution)/shard_map/third/pallas_call | solution.py:531
  38.3 0.1 collective-permute-start.12
  38.4 1.1 %middle.1.flux_above.flux_low = f32[1,2,128,128]{3,2,1,0:T(8,128)S(1)} custom-call(f32[1,2,144,128]{3,2,1,0:T(8,128)S(1)} %third.5.edge, f32[2,2,144,128]{3,2,1,0:T(8,128)S(1)} %third.6.middle, f32[1,2,144,128]{3,2,1,0:T(8,128)S(1)} %third.7.last, f32[6,2,128,128]{3,2,1,0:T(8,128)S(1)} %get-tuple-element.71.moved, f32[9,128,128]{2,1,0:T(8,128)S(1)} %wall.1.refs_0_), custom_call_target="tpu_custom_call" | custom-call | flops 110000000 | bytes 1024 | tf_op jit(solution)/shard_map/middle/pallas_call | solution.py:531
  39.5 0.2 collective-permute-done.12.inner
  39.7 2.0 %inside.1 = (f32[2,2,144,128]{3,2,1,0:T(8,128)S(1)}, f32[1,2,128,128]{3,2,1,0:T(8,128)S(1)}) custom-call(f32[1,2,144,128]{3,2,1,0:T(8,128)S(1)} %third.5.edge, f32[2,2,144,128]{3,2,1,0:T(8,128)S(1)} %third.6.middle, f32[1,2,144,128]{3,2,1,0:T(8,128)S(1)} %third.7.last, f32[1,2,128,128]{3,2,1,0:T(8,128)S(1)} %collective-permute-done.12.inner, ...), custom_call_target="tpu_custom_call" | custom-call | flops 110000000 | bytes 1024 | tf_op jit(solution)/shard_map/inside/pallas_call | solution.py:531
  41.7 0.3 collective-permute-start.13
  42.1 1.1 %collective-permute-done.13.refs_1_ = f32[1,2,128,128]{3,2,1,0:T(8,128)S(1)} collective-permute-done((f32[1,2,128,128]{3,2,1,0:T(8,128)S(1)}, f32[1,2,128,128]{3,2,1,0:T(8,128)S(1)}, u32[]{:S(2)}, u32[]{:S(2)}) %collective-permute-start.13) | collective-permute-done | bytes 131104 | tf_op jit(solution)/shard_map/ppermute | solution.py:549
  43.1 1.3 %second.11 = (f32[1,2,144,128]{3,2,1,0:T(8,128)S(1)}, f32[1,2,128,128]{3,2,1,0:T(8,128)S(1)}) custom-call(s32[1]{0:T(128)} %bitcast.odd_ref, f32[8,128]{1,0:T(8,128)S(1)} %get-tuple-element.53.step, f32[4,128,256]{2,1,0:T(8,128)S(1)} %get-tuple-element.55.speed_ref, f32[9,128,128]{2,1,0:T(8,128)S(1)} %wall.1.refs_0_, ...), custom_call_target="tpu_custom_call" | custom-call | flops 110000000 | bytes 1024 | tf_op jit(solution)/shard_map/second/pallas_call | solution.py:531
  44.4 0.3 collective-permute-start.14
  44.7 2.9 %outside.1 = (f32[1,2,128,128]{3,2,1,0:T(8,128)S(1)}, f32[2,2,144,128]{3,2,1,0:T(8,128)S(1)}) custom-call(f32[1,2,144,128]{3,2,1,0:T(8,128)S(1)} %third.5.edge, f32[2,2,144,128]{3,2,1,0:T(8,128)S(1)} %third.6.middle, f32[1,2,144,128]{3,2,1,0:T(8,128)S(1)} %third.7.last, f32[3,2,128,128]{3,2,1,0:T(8,128)S(1)} %collective-permute-done.10.outer, ...), custom_call_target="tpu_custom_call" | custom-call | flops 3300000000 | bytes 1024 | tf_op jit(solution)/shard_map/outside/pallas_call | solution.py:531
  47.6 1.0 %second.9 = (f32[1,2,144,128]{3,2,1,0:T(8,128)S(1)}, f32[1,2,128,128]{3,2,1,0:T(8,128)S(1)}) custom-call(s32[1]{0:T(128)} %bitcast.odd_ref, f32[8,128]{1,0:T(8,128)S(1)} %get-tuple-element.53.step, f32[4,128,256]{2,1,0:T(8,128)S(1)} %get-tuple-element.55.speed_ref, f32[9,128,128]{2,1,0:T(8,128)S(1)} %wall.1.refs_0_, ...), custom_call_target="tpu_custom_call" | custom-call | flops 1100000000 | bytes 1024 | tf_op jit(solution)/shard_map/second/pallas_call | solution.py:531
  48.7 2.5 %collective-permute-start.11 = (f32[1,2,128,128]{3,2,1,0:T(8,128)S(1)}, f32[1,2,128,128]{3,2,1,0:T(8,128)S(1)}, u32[]{:S(2)}, u32[]{:S(2)}) collective-permute-start(f32[1,2,128,128]{3,2,1,0:T(8,128)S(1)} %get-tuple-element.74), channel_id=1, source_target_pairs={{0,15},{1,2},{2,1},{3,4},{4,3},{5,6},{6,5},{7,8},{8,7},{9,10},{10,... | collective-permute-start | bytes 393224 | tf_op jit(solution)/shard_map/ppermute | solution.py:549
  51.2 2.0 %second.10.refs_1_.refs_0_.refs_2_ = f32[2,2,144,128]{3,2,1,0:T(8,128)S(1)} custom-call(s32[1]{0:T(128)} %bitcast.odd_ref, f32[8,128]{1,0:T(8,128)S(1)} %get-tuple-element.53.step, f32[4,128,256]{2,1,0:T(8,128)S(1)} %get-tuple-element.55.speed_ref, f32[9,128,128]{2,1,0:T(8,128)S(1)} %wall.1.refs_0_, ...), custom_call_target="tpu_custom_call" | custom-call | flops 2200000000 | bytes 1024 | tf_op jit(solution)/shard_map/second/pallas_call | solution.py:531
  53.2 2.2 %third.8.refs_3_ = f32[2,2,144,128]{3,2,1,0:T(8,128)S(1)} custom-call(s32[1]{0:T(128)} %bitcast.odd_ref, f32[8,128]{1,0:T(8,128)S(1)} %get-tuple-element.53.step, f32[4,128,256]{2,1,0:T(8,128)S(1)} %get-tuple-element.54.speed_ref, f32[9,128,128]{2,1,0:T(8,128)S(1)} %wall.1.refs_0_, f32[1,2,144,128]{3,2,1,0:T(8,128)S(1)} %get-tuple-element.75.refs_0_.refs_1_, ...), custom_call_target="tpu_custom_call" | custom-call | flops 2200000000 | bytes 1024 | tf_op jit(solution)/shard_map/third/pallas_call | solution.py:531
  55.3 0.0 collective-permute-done.14.refs_2_
  55.4 1.1 %third.9.refs_4_ = f32[1,2,144,128]{3,2,1,0:T(8,128)S(1)} custom-call(s32[1]{0:T(128)} %bitcast.odd_ref, f32[8,128]{1,0:T(8,128)S(1)} %get-tuple-element.53.step, f32[4,128,256]{2,1,0:T(8,128)S(1)} %get-tuple-element.54.speed_ref, f32[9,128,128]{2,1,0:T(8,128)S(1)} %wall.1.refs_0_, f32[2,2,144,128]{3,2,1,0:T(8,128)S(1)} %second.10.refs_1_.refs_0_.refs_2_, ...), custom_call_target="tpu_custom_call" | custom-call | flops 1100000000 | bytes 1024 | tf_op jit(solution)/shard_map/third/pallas_call | solution.py:531
  56.4 0.0 collective-permute-done.11.refs_0_
  56.5 1.8 %last.1 = f32[4,128,256]{2,1,0:T(8,128)} custom-call(s32[1]{0:T(128)} %bitcast.odd_ref, f32[8,128]{1,0:T(8,128)S(1)} %get-tuple-element.53.step, f32[4,128,256]{2,1,0:T(8,128)S(1)} %get-tuple-element.54.speed_ref, f32[9,128,128]{2,1,0:T(8,128)S(1)} %wall.1.refs_0_, f32[1,2,128,128]{3,2,1,0:T(8,128)S(1)} %collective-permute-done.11.refs_0_, ...), custom_call_target="tpu_custom_call" | custom-call | flops 1100000000 | bytes 1024 | tf_op jit(solution)/shard_map/last/pallas_call | solution.py:718
  (10 shorter events, 0.1 us)
Async XLA Ops:
  1.9 17.4 %collective-permute-start.5 = (f32[5,2,128,128]{3,2,1,0:T(8,128)S(1)}, f32[5,2,128,128]{3,2,1,0:T(8,128)S(1)}, u32[]{:S(2)}, u32[]{:S(2)}) collective-permute-start(f32[5,2,128,128]{3,2,1,0:T(8,128)S(1)} %get-tuple-element.51), channel_id=1, source_target_pairs={{0,15},{1,2},{2,1},{3,4},{4,3},{5,6},{6,5},{7,8},{8,7},{9,10},{10,... | collective-permute-start | bytes 1966088 | tf_op jit(solution)/shard_map/ppermute | solution.py:549
  7.4 2.1 %collective-permute-start.2 = (f32[3,2,128,128]{3,2,1,0:T(8,128)S(1)}, f32[3,2,128,128]{3,2,1,0:T(8,128)S(1)}, u32[]{:S(2)}, u32[]{:S(2)}) collective-permute-start(f32[3,2,128,128]{3,2,1,0:T(8,128)S(1)} %get-tuple-element.48), channel_id=1, source_target_pairs={{0,1},{1,0},{2,3},{3,2},{4,5},{5,4},{6,7},{7,6},{8,9},{9,8},{10,11... | collective-permute-start | bytes 1179656 | tf_op jit(solution)/shard_map/ppermute | solution.py:549
  7.4 1.7 %collective-permute-start = (f32[8,128]{1,0:T(8,128)S(1)}, f32[8,128]{1,0:T(8,128)S(1)}, u32[]{:S(2)}, u32[]{:S(2)}) collective-permute-start(f32[8,128]{1,0:T(8,128)S(1)} %get-tuple-element.44), channel_id=1, source_target_pairs={{0,1},{1,0},{2,3},{3,2},{4,5},{5,4},{6,7},{7,6},{8,9},{9,8},{10,11... | collective-permute-start | bytes 12296 | tf_op jit(solution)/shard_map/ppermute | solution.py:558
  9.1 6.5 %collective-permute-start.1 = (f32[8,128]{1,0:T(8,128)S(1)}, f32[8,128]{1,0:T(8,128)S(1)}, u32[]{:S(2)}, u32[]{:S(2)}) collective-permute-start(f32[8,128]{1,0:T(8,128)S(1)} %max.12), channel_id=1, source_target_pairs={{0,8},{1,9},{2,10},{3,11},{4,12},{5,13},{6,14},{7,15},{8,0},{9,1},... | collective-permute-start | bytes 12296 | tf_op jit(solution)/shard_map/ppermute | solution.py:558
  15.7 3.6 %collective-permute-start.3 = (f32[8,128]{1,0:T(8,128)S(1)}, f32[8,128]{1,0:T(8,128)S(1)}, u32[]{:S(2)}, u32[]{:S(2)}) collective-permute-start(f32[8,128]{1,0:T(8,128)S(1)} %max.13), channel_id=1, source_target_pairs={{0,4},{1,5},{2,6},{3,7},{4,0},{5,1},{6,2},{7,3},{8,12},{9,13},{10,... | collective-permute-start | bytes 12296 | tf_op jit(solution)/shard_map/ppermute | solution.py:558
  19.3 3.6 %collective-permute-start.4 = (f32[8,128]{1,0:T(8,128)S(1)}, f32[8,128]{1,0:T(8,128)S(1)}, u32[]{:S(2)}, u32[]{:S(2)}) collective-permute-start(f32[8,128]{1,0:T(8,128)S(1)} %max.14), channel_id=1, source_target_pairs={{0,2},{1,3},{2,0},{3,1},{4,6},{5,7},{6,4},{7,5},{8,10},{9,11},{10,... | collective-permute-start | bytes 12296 | tf_op jit(solution)/shard_map/ppermute | solution.py:558
  25.4 7.7 %collective-permute-start.6 = (f32[1,2,128,128]{3,2,1,0:T(8,128)S(1)}, f32[1,2,128,128]{3,2,1,0:T(8,128)S(1)}, u32[]{:S(2)}, u32[]{:S(2)}) collective-permute-start(f32[1,2,128,128]{3,2,1,0:T(8,128)S(1)} %get-tuple-element.60), channel_id=1, source_target_pairs={{0,15},{1,2},{2,1},{3,4},{4,3},{5,6},{6,5},{7,8},{8,7},{9,10},{10,... | collective-permute-start | bytes 393224 | tf_op jit(solution)/shard_map/ppermute | solution.py:549
  27.3 2.0 %collective-permute-start.7 = (f32[1,2,128,128]{3,2,1,0:T(8,128)S(1)}, f32[1,2,128,128]{3,2,1,0:T(8,128)S(1)}, u32[]{:S(2)}, u32[]{:S(2)}) collective-permute-start(f32[1,2,128,128]{3,2,1,0:T(8,128)S(1)} %get-tuple-element.63), channel_id=1, source_target_pairs={{0,1},{1,0},{2,3},{3,2},{4,5},{5,4},{6,7},{7,6},{8,9},{9,8},{10,11... | collective-permute-start | bytes 393224 | tf_op jit(solution)/shard_map/ppermute | solution.py:549
  30.4 6.8 %collective-permute-start.9 = (f32[1,2,128,128]{3,2,1,0:T(8,128)S(1)}, f32[1,2,128,128]{3,2,1,0:T(8,128)S(1)}, u32[]{:S(2)}, u32[]{:S(2)}) collective-permute-start(f32[1,2,128,128]{3,2,1,0:T(8,128)S(1)} %get-tuple-element.66), channel_id=1, source_target_pairs={{0,1},{1,0},{2,3},{3,2},{4,5},{5,4},{6,7},{7,6},{8,9},{9,8},{10,11... | collective-permute-start | bytes 393224 | tf_op jit(solution)/shard_map/ppermute | solution.py:549
  34.3 2.9 %collective-permute-start.8 = (f32[1,2,128,128]{3,2,1,0:T(8,128)S(1)}, f32[1,2,128,128]{3,2,1,0:T(8,128)S(1)}, u32[]{:S(2)}, u32[]{:S(2)}) collective-permute-start(f32[1,2,128,128]{3,2,1,0:T(8,128)S(1)} %get-tuple-element.65), channel_id=1, source_target_pairs={{0,1},{1,0},{2,3},{3,2},{4,5},{5,4},{6,7},{7,6},{8,9},{9,8},{10,11... | collective-permute-start | bytes 393224 | tf_op jit(solution)/shard_map/ppermute | solution.py:549
  34.4 10.4 %collective-permute-start.10 = (f32[3,2,128,128]{3,2,1,0:T(8,128)S(1)}, f32[3,2,128,128]{3,2,1,0:T(8,128)S(1)}, u32[]{:S(2)}, u32[]{:S(2)}) collective-permute-start(f32[3,2,128,128]{3,2,1,0:T(8,128)S(1)} %get-tuple-element.70), channel_id=1, source_target_pairs={{0,15},{1,2},{2,1},{3,4},{4,3},{5,6},{6,5},{7,8},{8,7},{9,10},{10,... | collective-permute-start | bytes 1179656 | tf_op jit(solution)/shard_map/ppermute | solution.py:549
  38.3 1.4 %collective-permute-start.12 = (f32[1,2,128,128]{3,2,1,0:T(8,128)S(1)}, f32[1,2,128,128]{3,2,1,0:T(8,128)S(1)}, u32[]{:S(2)}, u32[]{:S(2)}) collective-permute-start(f32[1,2,128,128]{3,2,1,0:T(8,128)S(1)} %strip.1), channel_id=1, source_target_pairs={{0,1},{1,0},{2,3},{3,2},{4,5},{5,4},{6,7},{7,6},{8,9},{9,8},{10,11... | collective-permute-start | bytes 393224 | tf_op jit(solution)/shard_map/ppermute | solution.py:549
  41.7 1.4 %collective-permute-start.13 = (f32[1,2,128,128]{3,2,1,0:T(8,128)S(1)}, f32[1,2,128,128]{3,2,1,0:T(8,128)S(1)}, u32[]{:S(2)}, u32[]{:S(2)}) collective-permute-start(f32[1,2,128,128]{3,2,1,0:T(8,128)S(1)} %get-tuple-element.80), channel_id=1, source_target_pairs={{0,1},{1,0},{2,3},{3,2},{4,5},{5,4},{6,7},{7,6},{8,9},{9,8},{10,11... | collective-permute-start | bytes 393224 | tf_op jit(solution)/shard_map/ppermute | solution.py:549
  44.4 10.9 %collective-permute-start.14 = (f32[1,2,128,128]{3,2,1,0:T(8,128)S(1)}, f32[1,2,128,128]{3,2,1,0:T(8,128)S(1)}, u32[]{:S(2)}, u32[]{:S(2)}) collective-permute-start(f32[1,2,128,128]{3,2,1,0:T(8,128)S(1)} %get-tuple-element.82), channel_id=1, source_target_pairs={{0,1},{1,0},{2,3},{3,2},{4,5},{5,4},{6,7},{7,6},{8,9},{9,8},{10,11... | collective-permute-start | bytes 393224 | tf_op jit(solution)/shard_map/ppermute | solution.py:549
  48.7 7.8 %collective-permute-start.11 = (f32[1,2,128,128]{3,2,1,0:T(8,128)S(1)}, f32[1,2,128,128]{3,2,1,0:T(8,128)S(1)}, u32[]{:S(2)}, u32[]{:S(2)}) collective-permute-start(f32[1,2,128,128]{3,2,1,0:T(8,128)S(1)} %get-tuple-element.74), channel_id=1, source_target_pairs={{0,15},{1,2},{2,1},{3,4},{4,3},{5,6},{6,5},{7,8},{8,7},{9,10},{10,... | collective-permute-start | bytes 393224 | tf_op jit(solution)/shard_map/ppermute | solution.py:549

commit v8 on v7

--- a/solution.py
+++ b/solution.py
@@ -662,7 +662,9 @@
                 [*slopes, flux],
                 faces=0.1,
             )
-            last, inner = last_second(inside, (OUTER + 2, True), send_inner)
+            inner = swap(send_inner, False)
+            last, send_inner = second_call((own_end - 1,), [inside, inner], [(OUTER + 2, True), (own_end, False)], True)
+            outer, last = lax.optimization_barrier((outer, last))
             above, outside = call(
                 outside_kernel,
                 "outside",
@@ -675,9 +677,11 @@
             swept = [above, outside, inside]
             places = [(OUTER - 1, False), (OUTER, True), (OUTER + 2, True)]
         edge, send_outer = second_call((OUTER,), swept[:2], places[:2], True)
+        send_outer, send_inner = lax.optimization_barrier((send_outer, send_inner))
         if turn == 0:
-            send_outer, send_inner = lax.optimization_barrier((send_outer, send_inner))
             last, inner = last_second(swept[-1], places[-1], send_inner)
+        else:
+            inner = swap(send_inner, False)
         after = lax.optimization_barrier((edge, *swept[1:]))[1:]
         (middle,) = second_call(tuple(range(OUTER + 1, own_end - 1)), after, places[1:], False)
         outer = swap(send_outer, True)

time: 58.6 us -> 58.7 us (level)
  transfers between devices with their start and end apart: 15 -> 15, of which waited for: 6 -> 6; matrix products, arithmetic and copies ran while one was open for 0% -> 0% of each run, Pallas kernels for 45% -> 38%
where the time goes in v8:
time: 58.7 us; the launch traced here: 58.5 us
  Pallas kernels  32.5 us (55%)
  starting transfers between devices  16.1 us (27%)
  waiting for transfers between devices  9.53 us (16%)
    pallas_call x23, Pallas kernels, call(): pl.pallas_call(kernel, out_shape=outs, in_specs=[IN_SMEM] * len(scalars)...  30.6 us
    ppermute x11, starting transfers between devices, swap(): return lax.ppermute(array, 'gx', pairs)  14.1 us
    ppermute x4, waiting for transfers between devices, largest_round(): received = lax.ppermute(array, 'gx', pairs)  8.16 us
    ppermute x4, starting transfers between devices, largest_round(): received = lax.ppermute(array, 'gx', pairs)  2 us
    pallas_call x1, Pallas kernels, last_call(): pl.pallas_call(functools.partial(last_kernel, places=places), out_shape=j...  1.83 us
    ppermute x11, waiting for transfers between devices, swap(): return lax.ppermute(array, 'gx', pairs)  1.36 us
  transfers between devices with their start and end apart: 15, of which 6 were waited for; matrix products, arithmetic and copies ran while one was open for 0% of the time, Pallas kernels for 38%

profile of v8, /device:TPU:0, one launch (start us, length us, event | category | flops | bytes accessed | tf_op | source)
XLA Modules:
  0.0 58.5 jit_solution(16596901176652561453)
XLA Ops:
  0.0 1.8 %begin.1 = (f32[4,128,256]{2,1,0:T(8,128)S(1)}, f32[4,128,256]{2,1,0:T(8,128)S(1)}, f32[4,128,256]{2,1,0:T(8,128)S(1)}, f32[8,128]{1,0:T(8,128)S(1)}, f32[4,2,14...) custom-call(s32[1]{0:T(128)} %bitcast.odd_ref, f32[4,128,256]{2,1,0:T(8,128)} %fraction_in.1, s32[4,128,256]{2,1,0:T(8,128)} %mask_in.1, ...), custom_call_target="tpu_custom_call" | custom-call | flops 110000000 | bytes 1024 | tf_op jit(solution)/shard_map/begin/pallas_call | solution.py:531
  1.8 0.1 first_send.1
  1.9 5.5 %collective-permute-start.5 = (f32[5,2,128,128]{3,2,1,0:T(8,128)S(1)}, f32[5,2,128,128]{3,2,1,0:T(8,128)S(1)}, u32[]{:S(2)}, u32[]{:S(2)}) collective-permute-start(f32[5,2,128,128]{3,2,1,0:T(8,128)S(1)} %get-tuple-element.55), channel_id=1, source_target_pairs={{0,15},{1,2},{2,1},{3,4},{4,3},{5,6},{6,5},{7,8},{8,7},{9,10},{10,... | collective-permute-start | bytes 1966088 | tf_op jit(solution)/shard_map/ppermute | solution.py:549
  7.4 0.0 collective-permute-start.2
  7.4 0.5 collective-permute-start
  7.9 1.2 %collective-permute-done = f32[8,128]{1,0:T(8,128)S(1)} collective-permute-done((f32[8,128]{1,0:T(8,128)S(1)}, f32[8,128]{1,0:T(8,128)S(1)}, u32[]{:S(2)}, u32[]{:S(2)}) %collective-permute-start) | collective-permute-done | bytes 4128 | tf_op jit(solution)/shard_map/ppermute | solution.py:558
  9.1 0.0 collective-permute-start.1
  9.1 0.4 wall.1.refs_0_
  9.5 0.0 collective-permute-done.2.refs_3_
  9.5 1.6 %prepare.3.refs_2_ = f32[18,2,128,128]{3,2,1,0:T(8,128)S(1)} custom-call(s32[1]{0:T(128)} %bitcast.odd_ref, f32[9,128,128]{2,1,0:T(8,128)S(1)} %wall.1.refs_0_, f32[4,128,256]{2,1,0:T(8,128)S(1)} %get-tuple-element.50.first.refs_1_, f32[4,2,144,128]{3,2,1,0:T(8,128)S(1)} %get-tuple-element.51.state.refs_2_.refs_3_, ...), custom_call_target="tpu_custom_call" | custom-call | flops 22000000 | bytes 1024 | tf_op jit(solution)/shard_map/prepare/pallas_call | solution.py:531
  11.1 4.5 %collective-permute-done.1 = f32[8,128]{1,0:T(8,128)S(1)} collective-permute-done((f32[8,128]{1,0:T(8,128)S(1)}, f32[8,128]{1,0:T(8,128)S(1)}, u32[]{:S(2)}, u32[]{:S(2)}) %collective-permute-start.1) | collective-permute-done | bytes 4128 | tf_op jit(solution)/shard_map/ppermute | solution.py:558
  15.7 1.5 %collective-permute-start.3 = (f32[8,128]{1,0:T(8,128)S(1)}, f32[8,128]{1,0:T(8,128)S(1)}, u32[]{:S(2)}, u32[]{:S(2)}) collective-permute-start(f32[8,128]{1,0:T(8,128)S(1)} %max.13), channel_id=1, source_target_pairs={{0,4},{1,5},{2,6},{3,7},{4,0},{5,1},{6,2},{7,3},{8,12},{9,13},{10,... | collective-permute-start | bytes 12296 | tf_op jit(solution)/shard_map/ppermute | solution.py:558
  17.1 0.9 %prepare.4.refs_1_ = f32[9,2,128,128]{3,2,1,0:T(8,128)S(1)} custom-call(s32[1]{0:T(128)} %bitcast.odd_ref, f32[9,128,128]{2,1,0:T(8,128)S(1)} %wall.1.refs_0_, f32[4,128,256]{2,1,0:T(8,128)S(1)} %get-tuple-element.50.first.refs_1_, f32[4,2,144,128]{3,2,1,0:T(8,128)S(1)} %get-tuple-element.51.state.refs_2_.refs_3_, ...), custom_call_target="tpu_custom_call" | custom-call | flops 22000000 | bytes 1024 | tf_op jit(solution)/shard_map/prepare/pallas_call | solution.py:531
  18.1 1.2 %collective-permute-done.3 = f32[8,128]{1,0:T(8,128)S(1)} collective-permute-done((f32[8,128]{1,0:T(8,128)S(1)}, f32[8,128]{1,0:T(8,128)S(1)}, u32[]{:S(2)}, u32[]{:S(2)}) %collective-permute-start.3) | collective-permute-done | bytes 4128 | tf_op jit(solution)/shard_map/ppermute | solution.py:558
  19.3 0.0 collective-permute-done.5.refs_3_.refs_4_
  19.3 2.4 %prepare.5.refs_0_ = f32[27,2,128,128]{3,2,1,0:T(8,128)S(1)} custom-call(s32[1]{0:T(128)} %bitcast.odd_ref, f32[9,128,128]{2,1,0:T(8,128)S(1)} %wall.1.refs_0_, f32[4,128,256]{2,1,0:T(8,128)S(1)} %get-tuple-element.50.first.refs_1_, f32[4,2,144,128]{3,2,1,0:T(8,128)S(1)} %get-tuple-element.51.state.refs_2_.refs_3_, ...), custom_call_target="tpu_custom_call" | custom-call | flops 22000000 | bytes 1024 | tf_op jit(solution)/shard_map/prepare/pallas_call | solution.py:531
  21.6 1.2 %collective-permute-done.4 = f32[8,128]{1,0:T(8,128)S(1)} collective-permute-done((f32[8,128]{1,0:T(8,128)S(1)}, f32[8,128]{1,0:T(8,128)S(1)}, u32[]{:S(2)}, u32[]{:S(2)}) %collective-permute-start.4) | collective-permute-done | bytes 4128 | tf_op jit(solution)/shard_map/ppermute | solution.py:558
  22.9 1.5 %finish.1 = (f32[4,2,144,128]{3,2,1,0:T(8,128)S(1)}, f32[1,2,128,128]{3,2,1,0:T(8,128)S(1)}, f32[6,2,128,128]{3,2,1,0:T(8,128)S(1)}, f32[8,128]{1,0:T(8,128)S(1)}, f32[1,2,128,128]{3,2,1,0:T(8,128)S(1)}) custom-call(f32[8,128]{1,0:T(8,128)S(1)} %max.15.peak, f32[27,2,128,128]{3,2,1,0:T(8,128)S(1)} %prepare.5.refs_0_, f32[9,2,128,128]{3,2,1,0:T(8,128)S(1)} %prepare.4.refs_1_, ...), custom_call_target="tpu_custom_call" | custom-call | flops 1100000000 | bytes 1024 | tf_op jit(solution)/shard_map/finish/pallas_call | solution.py:531
  24.4 1.1 %second.6 = (f32[1,2,144,128]{3,2,1,0:T(8,128)S(1)}, f32[1,2,128,128]{3,2,1,0:T(8,128)S(1)}) custom-call(s32[1]{0:T(128)} %bitcast.odd_ref, f32[8,128]{1,0:T(8,128)S(1)} %get-tuple-element.57.step, f32[4,128,256]{2,1,0:T(8,128)S(1)} %get-tuple-element.59.speed_ref, f32[9,128,128]{2,1,0:T(8,128)S(1)} %wall.1.refs_0_, ...), custom_call_target="tpu_custom_call" | custom-call | flops 1100000000 | bytes 1024 | tf_op jit(solution)/shard_map/second/pallas_call | solution.py:531
  25.4 1.9 %collective-permute-start.6 = (f32[1,2,128,128]{3,2,1,0:T(8,128)S(1)}, f32[1,2,128,128]{3,2,1,0:T(8,128)S(1)}, u32[]{:S(2)}, u32[]{:S(2)}) collective-permute-start(f32[1,2,128,128]{3,2,1,0:T(8,128)S(1)} %get-tuple-element.64), channel_id=1, source_target_pairs={{0,15},{1,2},{2,1},{3,4},{4,3},{5,6},{6,5},{7,8},{8,7},{9,10},{10,... | collective-permute-start | bytes 393224 | tf_op jit(solution)/shard_map/ppermute | solution.py:549
  27.3 0.0 collective-permute-start.7
  27.3 2.0 %second.7.refs_2_.refs_1_.refs_0_ = f32[2,2,144,128]{3,2,1,0:T(8,128)S(1)} custom-call(s32[1]{0:T(128)} %bitcast.odd_ref, f32[8,128]{1,0:T(8,128)S(1)} %get-tuple-element.57.step, f32[4,128,256]{2,1,0:T(8,128)S(1)} %get-tuple-element.59.speed_ref, f32[9,128,128]{2,1,0:T(8,128)S(1)} %wall.1.refs_0_, f32[4,2,144,128]{3,2,1,0:T(8,128)S(1)} %get-tuple-element.66.refs_1_.refs_0_), custom_call_target="tpu_custom_call" | custom-call | flops 2200000000 | bytes 1024 | tf_op jit(solution)/shard_map/second/pallas_call | solution.py:531
  29.3 0.0 collective-permute-done.7.refs_1_
  29.3 1.1 %second.8 = (f32[1,2,144,128]{3,2,1,0:T(8,128)S(1)}, f32[1,2,128,128]{3,2,1,0:T(8,128)S(1)}) custom-call(s32[1]{0:T(128)} %bitcast.odd_ref, f32[8,128]{1,0:T(8,128)S(1)} %get-tuple-element.57.step, f32[4,128,256]{2,1,0:T(8,128)S(1)} %get-tuple-element.59.speed_ref, f32[9,128,128]{2,1,0:T(8,128)S(1)} %wall.1.refs_0_, ...), custom_call_target="tpu_custom_call" | custom-call | flops 110000000 | bytes 1024 | tf_op jit(solution)/shard_map/second/pallas_call | solution.py:531
  30.4 0.6 collective-permute-start.9
  30.9 2.2 %third.6.middle = f32[2,2,144,128]{3,2,1,0:T(8,128)S(1)} custom-call(s32[1]{0:T(128)} %bitcast.odd_ref, f32[8,128]{1,0:T(8,128)S(1)} %get-tuple-element.57.step, f32[4,128,256]{2,1,0:T(8,128)S(1)} %get-tuple-element.58.speed_ref, f32[9,128,128]{2,1,0:T(8,128)S(1)} %wall.1.refs_0_, f32[1,2,144,128]{3,2,1,0:T(8,128)S(1)} %get-tuple-element.65.refs_1_.refs_0_, ...), custom_call_target="tpu_custom_call" | custom-call | flops 2200000000 | bytes 1024 | tf_op jit(solution)/shard_map/third/pallas_call | solution.py:531
  33.1 0.0 collective-permute-done.6.refs_0_
  33.1 1.1 %third.5.edge = f32[1,2,144,128]{3,2,1,0:T(8,128)S(1)} custom-call(s32[1]{0:T(128)} %bitcast.odd_ref, f32[8,128]{1,0:T(8,128)S(1)} %get-tuple-element.57.step, f32[4,128,256]{2,1,0:T(8,128)S(1)} %get-tuple-element.58.speed_ref, f32[9,128,128]{2,1,0:T(8,128)S(1)} %wall.1.refs_0_, f32[1,2,128,128]{3,2,1,0:T(8,128)S(1)} %collective-permute-done.6.refs_0_, ...), custom_call_target="tpu_custom_call" | custom-call | flops 1100000000 | bytes 1024 | tf_op jit(solution)/shard_map/third/pallas_call | solution.py:531
  34.3 0.1 collective-permute-start.8
  34.4 2.8 %collective-permute-start.10 = (f32[3,2,128,128]{3,2,1,0:T(8,128)S(1)}, f32[3,2,128,128]{3,2,1,0:T(8,128)S(1)}, u32[]{:S(2)}, u32[]{:S(2)}) collective-permute-start(f32[3,2,128,128]{3,2,1,0:T(8,128)S(1)} %get-tuple-element.74), channel_id=1, source_target_pairs={{0,15},{1,2},{2,1},{3,4},{4,3},{5,6},{6,5},{7,8},{8,7},{9,10},{10,... | collective-permute-start | bytes 1179656 | tf_op jit(solution)/shard_map/ppermute | solution.py:549
  37.2 0.0 collective-permute-done.9.refs_2_
  37.2 0.0 collective-permute-done.8.beyond
  37.2 1.1 %third.7.last = f32[1,2,144,128]{3,2,1,0:T(8,128)S(1)} custom-call(s32[1]{0:T(128)} %bitcast.odd_ref, f32[8,128]{1,0:T(8,128)S(1)} %get-tuple-element.57.step, f32[4,128,256]{2,1,0:T(8,128)S(1)} %get-tuple-element.58.speed_ref, f32[9,128,128]{2,1,0:T(8,128)S(1)} %wall.1.refs_0_, f32[2,2,144,128]{3,2,1,0:T(8,128)S(1)} %second.7.refs_2_.refs_1_.refs_0_, ...), custom_call_target="tpu_custom_call" | custom-call | flops 1100000000 | bytes 1024 | tf_op jit(solution)/shard_map/third/pallas_call | solution.py:531
  38.3 0.1 collective-permute-start.11
  38.4 1.1 %middle.1.flux_low.flux_above = f32[1,2,128,128]{3,2,1,0:T(8,128)S(1)} custom-call(f32[1,2,144,128]{3,2,1,0:T(8,128)S(1)} %third.5.edge, f32[2,2,144,128]{3,2,1,0:T(8,128)S(1)} %third.6.middle, f32[1,2,144,128]{3,2,1,0:T(8,128)S(1)} %third.7.last, f32[6,2,128,128]{3,2,1,0:T(8,128)S(1)} %get-tuple-element.76.moved, f32[9,128,128]{2,1,0:T(8,128)S(1)} %wall.1.refs_0_), custom_call_target="tpu_custom_call" | custom-call | flops 110000000 | bytes 1024 | tf_op jit(solution)/shard_map/middle/pallas_call | solution.py:531
  39.5 0.2 collective-permute-done.11.inner
  39.7 2.0 %inside.1 = (f32[2,2,144,128]{3,2,1,0:T(8,128)S(1)}, f32[1,2,128,128]{3,2,1,0:T(8,128)S(1)}) custom-call(f32[1,2,144,128]{3,2,1,0:T(8,128)S(1)} %third.5.edge, f32[2,2,144,128]{3,2,1,0:T(8,128)S(1)} %third.6.middle, f32[1,2,144,128]{3,2,1,0:T(8,128)S(1)} %third.7.last, f32[1,2,128,128]{3,2,1,0:T(8,128)S(1)} %collective-permute-done.11.inner, ...), custom_call_target="tpu_custom_call" | custom-call | flops 110000000 | bytes 1024 | tf_op jit(solution)/shard_map/inside/pallas_call | solution.py:531
  41.7 0.3 collective-permute-start.12
  42.1 1.1 %collective-permute-done.12.refs_1_ = f32[1,2,128,128]{3,2,1,0:T(8,128)S(1)} collective-permute-done((f32[1,2,128,128]{3,2,1,0:T(8,128)S(1)}, f32[1,2,128,128]{3,2,1,0:T(8,128)S(1)}, u32[]{:S(2)}, u32[]{:S(2)}) %collective-permute-start.12) | collective-permute-done | bytes 131104 | tf_op jit(solution)/shard_map/ppermute | solution.py:549
  43.1 1.3 %second.9 = (f32[1,2,144,128]{3,2,1,0:T(8,128)S(1)}, f32[1,2,128,128]{3,2,1,0:T(8,128)S(1)}) custom-call(s32[1]{0:T(128)} %bitcast.odd_ref, f32[8,128]{1,0:T(8,128)S(1)} %get-tuple-element.57.step, f32[4,128,256]{2,1,0:T(8,128)S(1)} %get-tuple-element.59.speed_ref, f32[9,128,128]{2,1,0:T(8,128)S(1)} %wall.1.refs_0_, ...), custom_call_target="tpu_custom_call" | custom-call | flops 110000000 | bytes 1024 | tf_op jit(solution)/shard_map/second/pallas_call | solution.py:531
  44.4 2.9 %outside.1 = (f32[1,2,128,128]{3,2,1,0:T(8,128)S(1)}, f32[2,2,144,128]{3,2,1,0:T(8,128)S(1)}) custom-call(f32[1,2,144,128]{3,2,1,0:T(8,128)S(1)} %third.5.edge, f32[2,2,144,128]{3,2,1,0:T(8,128)S(1)} %third.6.middle, f32[1,2,144,128]{3,2,1,0:T(8,128)S(1)} %third.7.last, f32[3,2,128,128]{3,2,1,0:T(8,128)S(1)} %collective-permute-done.10.outer, ...), custom_call_target="tpu_custom_call" | custom-call | flops 3300000000 | bytes 1024 | tf_op jit(solution)/shard_map/outside/pallas_call | solution.py:531
  47.3 1.1 %second.10 = (f32[1,2,144,128]{3,2,1,0:T(8,128)S(1)}, f32[1,2,128,128]{3,2,1,0:T(8,128)S(1)}) custom-call(s32[1]{0:T(128)} %bitcast.odd_ref, f32[8,128]{1,0:T(8,128)S(1)} %get-tuple-element.57.step, f32[4,128,256]{2,1,0:T(8,128)S(1)} %get-tuple-element.59.speed_ref, f32[9,128,128]{2,1,0:T(8,128)S(1)} %wall.1.refs_0_, ...), custom_call_target="tpu_custom_call" | custom-call | flops 1100000000 | bytes 1024 | tf_op jit(solution)/shard_map/second/pallas_call | solution.py:531
  48.4 2.8 %collective-permute-start.13 = (f32[1,2,128,128]{3,2,1,0:T(8,128)S(1)}, f32[1,2,128,128]{3,2,1,0:T(8,128)S(1)}, u32[]{:S(2)}, u32[]{:S(2)}) collective-permute-start(f32[1,2,128,128]{3,2,1,0:T(8,128)S(1)} %get-tuple-element.85), channel_id=1, source_target_pairs={{0,15},{1,2},{2,1},{3,4},{4,3},{5,6},{6,5},{7,8},{8,7},{9,10},{10,... | collective-permute-start | bytes 393224 | tf_op jit(solution)/shard_map/ppermute | solution.py:549
  51.2 2.0 %second.11.refs_1_.refs_0_.refs_2_ = f32[2,2,144,128]{3,2,1,0:T(8,128)S(1)} custom-call(s32[1]{0:T(128)} %bitcast.odd_ref, f32[8,128]{1,0:T(8,128)S(1)} %get-tuple-element.57.step, f32[4,128,256]{2,1,0:T(8,128)S(1)} %get-tuple-element.59.speed_ref, f32[9,128,128]{2,1,0:T(8,128)S(1)} %wall.1.refs_0_, ...), custom_call_target="tpu_custom_call" | custom-call | flops 2200000000 | bytes 1024 | tf_op jit(solution)/shard_map/second/pallas_call | solution.py:531
  53.2 2.2 %third.8.refs_3_ = f32[2,2,144,128]{3,2,1,0:T(8,128)S(1)} custom-call(s32[1]{0:T(128)} %bitcast.odd_ref, f32[8,128]{1,0:T(8,128)S(1)} %get-tuple-element.57.step, f32[4,128,256]{2,1,0:T(8,128)S(1)} %get-tuple-element.58.speed_ref, f32[9,128,128]{2,1,0:T(8,128)S(1)} %wall.1.refs_0_, f32[1,2,144,128]{3,2,1,0:T(8,128)S(1)} %get-tuple-element.86.refs_0_.refs_1_, ...), custom_call_target="tpu_custom_call" | custom-call | flops 2200000000 | bytes 1024 | tf_op jit(solution)/shard_map/third/pallas_call | solution.py:531
  55.3 0.0 collective-permute-done.14.refs_2_
  55.4 1.1 %third.9.refs_4_ = f32[1,2,144,128]{3,2,1,0:T(8,128)S(1)} custom-call(s32[1]{0:T(128)} %bitcast.odd_ref, f32[8,128]{1,0:T(8,128)S(1)} %get-tuple-element.57.step, f32[4,128,256]{2,1,0:T(8,128)S(1)} %get-tuple-element.58.speed_ref, f32[9,128,128]{2,1,0:T(8,128)S(1)} %wall.1.refs_0_, f32[2,2,144,128]{3,2,1,0:T(8,128)S(1)} %second.11.refs_1_.refs_0_.refs_2_, ...), custom_call_target="tpu_custom_call" | custom-call | flops 1100000000 | bytes 1024 | tf_op jit(solution)/shard_map/third/pallas_call | solution.py:531
  56.5 1.8 %last.1 = f32[4,128,256]{2,1,0:T(8,128)} custom-call(s32[1]{0:T(128)} %bitcast.odd_ref, f32[8,128]{1,0:T(8,128)S(1)} %get-tuple-element.57.step, f32[4,128,256]{2,1,0:T(8,128)S(1)} %get-tuple-element.58.speed_ref, f32[9,128,128]{2,1,0:T(8,128)S(1)} %wall.1.refs_0_, f32[1,2,128,128]{3,2,1,0:T(8,128)S(1)} %collective-permute-done.13.refs_0_, ...), custom_call_target="tpu_custom_call" | custom-call | flops 1100000000 | bytes 1024 | tf_op jit(solution)/shard_map/last/pallas_call | solution.py:722
  (10 shorter events, 0.1 us)
Async XLA Ops:
  1.9 17.4 %collective-permute-start.5 = (f32[5,2,128,128]{3,2,1,0:T(8,128)S(1)}, f32[5,2,128,128]{3,2,1,0:T(8,128)S(1)}, u32[]{:S(2)}, u32[]{:S(2)}) collective-permute-start(f32[5,2,128,128]{3,2,1,0:T(8,128)S(1)} %get-tuple-element.55), channel_id=1, source_target_pairs={{0,15},{1,2},{2,1},{3,4},{4,3},{5,6},{6,5},{7,8},{8,7},{9,10},{10,... | collective-permute-start | bytes 1966088 | tf_op jit(solution)/shard_map/ppermute | solution.py:549
  7.4 2.1 %collective-permute-start.2 = (f32[3,2,128,128]{3,2,1,0:T(8,128)S(1)}, f32[3,2,128,128]{3,2,1,0:T(8,128)S(1)}, u32[]{:S(2)}, u32[]{:S(2)}) collective-permute-start(f32[3,2,128,128]{3,2,1,0:T(8,128)S(1)} %get-tuple-element.52), channel_id=1, source_target_pairs={{0,1},{1,0},{2,3},{3,2},{4,5},{5,4},{6,7},{7,6},{8,9},{9,8},{10,11... | collective-permute-start | bytes 1179656 | tf_op jit(solution)/shard_map/ppermute | solution.py:549
  7.4 1.7 %collective-permute-start = (f32[8,128]{1,0:T(8,128)S(1)}, f32[8,128]{1,0:T(8,128)S(1)}, u32[]{:S(2)}, u32[]{:S(2)}) collective-permute-start(f32[8,128]{1,0:T(8,128)S(1)} %get-tuple-element.48), channel_id=1, source_target_pairs={{0,1},{1,0},{2,3},{3,2},{4,5},{5,4},{6,7},{7,6},{8,9},{9,8},{10,11... | collective-permute-start | bytes 12296 | tf_op jit(solution)/shard_map/ppermute | solution.py:558
  9.1 6.5 %collective-permute-start.1 = (f32[8,128]{1,0:T(8,128)S(1)}, f32[8,128]{1,0:T(8,128)S(1)}, u32[]{:S(2)}, u32[]{:S(2)}) collective-permute-start(f32[8,128]{1,0:T(8,128)S(1)} %max.12), channel_id=1, source_target_pairs={{0,8},{1,9},{2,10},{3,11},{4,12},{5,13},{6,14},{7,15},{8,0},{9,1},... | collective-permute-start | bytes 12296 | tf_op jit(solution)/shard_map/ppermute | solution.py:558
  15.7 3.6 %collective-permute-start.3 = (f32[8,128]{1,0:T(8,128)S(1)}, f32[8,128]{1,0:T(8,128)S(1)}, u32[]{:S(2)}, u32[]{:S(2)}) collective-permute-start(f32[8,128]{1,0:T(8,128)S(1)} %max.13), channel_id=1, source_target_pairs={{0,4},{1,5},{2,6},{3,7},{4,0},{5,1},{6,2},{7,3},{8,12},{9,13},{10,... | collective-permute-start | bytes 12296 | tf_op jit(solution)/shard_map/ppermute | solution.py:558
  19.3 3.6 %collective-permute-start.4 = (f32[8,128]{1,0:T(8,128)S(1)}, f32[8,128]{1,0:T(8,128)S(1)}, u32[]{:S(2)}, u32[]{:S(2)}) collective-permute-start(f32[8,128]{1,0:T(8,128)S(1)} %max.14), channel_id=1, source_target_pairs={{0,2},{1,3},{2,0},{3,1},{4,6},{5,7},{6,4},{7,5},{8,10},{9,11},{10,... | collective-permute-start | bytes 12296 | tf_op jit(solution)/shard_map/ppermute | solution.py:558
  25.4 7.7 %collective-permute-start.6 = (f32[1,2,128,128]{3,2,1,0:T(8,128)S(1)}, f32[1,2,128,128]{3,2,1,0:T(8,128)S(1)}, u32[]{:S(2)}, u32[]{:S(2)}) collective-permute-start(f32[1,2,128,128]{3,2,1,0:T(8,128)S(1)} %get-tuple-element.64), channel_id=1, source_target_pairs={{0,15},{1,2},{2,1},{3,4},{4,3},{5,6},{6,5},{7,8},{8,7},{9,10},{10,... | collective-permute-start | bytes 393224 | tf_op jit(solution)/shard_map/ppermute | solution.py:549
  27.3 2.0 %collective-permute-start.7 = (f32[1,2,128,128]{3,2,1,0:T(8,128)S(1)}, f32[1,2,128,128]{3,2,1,0:T(8,128)S(1)}, u32[]{:S(2)}, u32[]{:S(2)}) collective-permute-start(f32[1,2,128,128]{3,2,1,0:T(8,128)S(1)} %get-tuple-element.67), channel_id=1, source_target_pairs={{0,1},{1,0},{2,3},{3,2},{4,5},{5,4},{6,7},{7,6},{8,9},{9,8},{10,11... | collective-permute-start | bytes 393224 | tf_op jit(solution)/shard_map/ppermute | solution.py:549
  30.4 6.8 %collective-permute-start.9 = (f32[1,2,128,128]{3,2,1,0:T(8,128)S(1)}, f32[1,2,128,128]{3,2,1,0:T(8,128)S(1)}, u32[]{:S(2)}, u32[]{:S(2)}) collective-permute-start(f32[1,2,128,128]{3,2,1,0:T(8,128)S(1)} %get-tuple-element.70), channel_id=1, source_target_pairs={{0,1},{1,0},{2,3},{3,2},{4,5},{5,4},{6,7},{7,6},{8,9},{9,8},{10,11... | collective-permute-start | bytes 393224 | tf_op jit(solution)/shard_map/ppermute | solution.py:549
  34.3 2.9 %collective-permute-start.8 = (f32[1,2,128,128]{3,2,1,0:T(8,128)S(1)}, f32[1,2,128,128]{3,2,1,0:T(8,128)S(1)}, u32[]{:S(2)}, u32[]{:S(2)}) collective-permute-start(f32[1,2,128,128]{3,2,1,0:T(8,128)S(1)} %get-tuple-element.69), channel_id=1, source_target_pairs={{0,1},{1,0},{2,3},{3,2},{4,5},{5,4},{6,7},{7,6},{8,9},{9,8},{10,11... | collective-permute-start | bytes 393224 | tf_op jit(solution)/shard_map/ppermute | solution.py:549
  34.4 10.1 %collective-permute-start.10 = (f32[3,2,128,128]{3,2,1,0:T(8,128)S(1)}, f32[3,2,128,128]{3,2,1,0:T(8,128)S(1)}, u32[]{:S(2)}, u32[]{:S(2)}) collective-permute-start(f32[3,2,128,128]{3,2,1,0:T(8,128)S(1)} %get-tuple-element.74), channel_id=1, source_target_pairs={{0,15},{1,2},{2,1},{3,4},{4,3},{5,6},{6,5},{7,8},{8,7},{9,10},{10,... | collective-permute-start | bytes 1179656 | tf_op jit(solution)/shard_map/ppermute | solution.py:549
  38.3 1.4 %collective-permute-start.11 = (f32[1,2,128,128]{3,2,1,0:T(8,128)S(1)}, f32[1,2,128,128]{3,2,1,0:T(8,128)S(1)}, u32[]{:S(2)}, u32[]{:S(2)}) collective-permute-start(f32[1,2,128,128]{3,2,1,0:T(8,128)S(1)} %strip.1), channel_id=1, source_target_pairs={{0,1},{1,0},{2,3},{3,2},{4,5},{5,4},{6,7},{7,6},{8,9},{9,8},{10,11... | collective-permute-start | bytes 393224 | tf_op jit(solution)/shard_map/ppermute | solution.py:549
  41.7 1.4 %collective-permute-start.12 = (f32[1,2,128,128]{3,2,1,0:T(8,128)S(1)}, f32[1,2,128,128]{3,2,1,0:T(8,128)S(1)}, u32[]{:S(2)}, u32[]{:S(2)}) collective-permute-start(f32[1,2,128,128]{3,2,1,0:T(8,128)S(1)} %get-tuple-element.78), channel_id=1, source_target_pairs={{0,1},{1,0},{2,3},{3,2},{4,5},{5,4},{6,7},{7,6},{8,9},{9,8},{10,11... | collective-permute-start | bytes 393224 | tf_op jit(solution)/shard_map/ppermute | solution.py:549
  48.4 8.1 %collective-permute-start.13 = (f32[1,2,128,128]{3,2,1,0:T(8,128)S(1)}, f32[1,2,128,128]{3,2,1,0:T(8,128)S(1)}, u32[]{:S(2)}, u32[]{:S(2)}) collective-permute-start(f32[1,2,128,128]{3,2,1,0:T(8,128)S(1)} %get-tuple-element.85), channel_id=1, source_target_pairs={{0,15},{1,2},{2,1},{3,4},{4,3},{5,6},{6,5},{7,8},{8,7},{9,10},{10,... | collective-permute-start | bytes 393224 | tf_op jit(solution)/shard_map/ppermute | solution.py:549
  51.2 4.2 %collective-permute-start.14 = (f32[1,2,128,128]{3,2,1,0:T(8,128)S(1)}, f32[1,2,128,128]{3,2,1,0:T(8,128)S(1)}, u32[]{:S(2)}, u32[]{:S(2)}) collective-permute-start(f32[1,2,128,128]{3,2,1,0:T(8,128)S(1)} %get-tuple-element.90), channel_id=1, source_target_pairs={{0,1},{1,0},{2,3},{3,2},{4,5},{5,4},{6,7},{7,6},{8,9},{9,8},{10,11... | collective-permute-start | bytes 393224 | tf_op jit(solution)/shard_map/ppermute | solution.py:549
